TPU v7x, 32 devices: a whole 2x2x4 slice. The times are simulated.
32 devices in a mesh: groups: 2 (over x), sector: 16 (over z, y, core).
Axes of the slice: x: 2, y: 2, z: 4, core: 2. Of those that a mesh axis runs over, the one named last changes fastest.
Arguments:
- wavefunction: bfloat16 [64, 256, 256], P(('groups', 'sector')), parts along dimension 0, may hold values from -8 to 8
- lower_states: bfloat16 [3, 64, 256, 256], P(None, ('groups', 'sector')), parts along dimension 1, may hold values from -8 to 8
- left_env: bfloat16 [2944, 256, 256], P(('groups', 'sector')), parts along dimension 0, may hold values from -0.375 to 0.375
- right_env: bfloat16 [2944, 256, 256], P(('groups', 'sector')), parts along dimension 0, may hold values from -0.0546875 to 0.0546875
- term_list: int32 [2944, 2], P(('groups', 'sector')), parts along dimension 0, may hold values from 0 to 31, all different within a row
Outputs:
- residual: float32 [64, 256, 256], P(('groups', 'sector')), parts along dimension 0
- ritz_value: float32 [2], P('groups'), parts along dimension 0
There are 2 independent parts, one for each index of `groups`. A program takes and returns all parts, laid end to end along the dimension named above; each array names one. Nothing has to cross between parts.
Inputs may be any that keep to these rules, and one draw needn't show every extreme that they name: Each row of term_list names a source sector and a different destination sector; every sector appears in some row.
All inputs are finite; a program needn't handle non-finite values.
Results may differ from a plain program's by a relative error of at most 0.0015.
The roundings to bfloat16 on the way count: a program that leaves them out, or rounds other values in their place, can miss the bound.
Values may be sent and summed in bfloat16 or wider, within the bound.
No kernel may reach another device: no remote copies, remote signals or barrier semaphores. Data moves between devices by JAX's collectives and lax.ppermute only.
A program may use at most 192 MiB of HBM per device.

v0:
```python
import jax
import jax.numpy as jnp
from jax import lax
from jax.sharding import PartitionSpec as P

shift_energy = 2.0


def per_device(wavefunction, lower_states, left_env, right_env, term_list):
    sectors = wavefunction.shape[0] * lax.axis_size("sector")
    psi_local = wavefunction.astype(jnp.float32)
    lower_local = lower_states.astype(jnp.float32)
    correlation_part = jnp.sum(lower_local * psi_local[None], axis=(1, 2, 3))
    own_part = jnp.sum(lower_local * lower_local, axis=(1, 2, 3))
    norm_part = jnp.sum(psi_local * psi_local)
    correlation, own_norm, psi_norm = lax.psum((correlation_part, own_part, norm_part), "sector")
    gathered = lax.all_gather(wavefunction, "sector", axis=0, tiled=True)
    blocks = gathered[term_list[:, 0]]
    half_block = jnp.einsum(
        "kab,kbc->kac", left_env, blocks, preferred_element_type=jnp.float32
    ).astype(jnp.bfloat16)
    contrib = jnp.einsum("kab,kbc->kac", half_block, right_env, preferred_element_type=jnp.float32)
    targets = term_list[:, 1]
    partial_sigma = jax.ops.segment_sum(contrib, targets, num_segments=sectors)
    sigma_local = lax.psum_scatter(partial_sigma, "sector", scatter_dimension=0, tiled=True)
    cross_part = jnp.sum(psi_local * sigma_local)
    cross_term = lax.psum(cross_part, "sector")
    coeffs = correlation / own_norm
    deflated = sigma_local + shift_energy * jnp.sum(
        coeffs[:, None, None, None] * lower_local, axis=0
    )
    ritz_value = (cross_term + shift_energy * jnp.sum(coeffs * correlation)) / psi_norm
    residual = deflated - ritz_value * psi_local
    return (residual, ritz_value.reshape(1))


def solution(mesh):
    return jax.shard_map(
        per_device,
        mesh=mesh,
        in_specs=(
            P(("groups", "sector"), None, None),
            P(None, ("groups", "sector"), None, None),
            P(("groups", "sector"), None, None),
            P(("groups", "sector"), None, None),
            P(("groups", "sector"), None),
        ),
        out_specs=(P(("groups", "sector"), None, None), P("groups")),
        check_vma=False,
    )
```

profile of v0, /device:TPU:0, one launch (start us, length us, event | category | flops | bytes accessed | tf_op | source)
XLA Modules:
  0.0 302.4 jit_solution(12918636434816405141)
XLA Ops:
  7.2 0.0 all-gather.2.cloned.1.call-start
  7.2 0.7 all-gather.2.cloned.1.call-update
  7.9 0.0 reduce-scatter.2.cloned.1.call-start
  7.9 0.8 fusion.7
  8.7 54.7 %all-gather.2.cloned.1.call-done = bf16[32,256,256]{2,1,0:T(8,128)(2,1)} async-done(((bf16[2,256,256]{2,1,0:T(8,128)(2,1)}), bf16[32,256,256]{2,1,0:T(8,128)(2,1)}) %all-gather.2.cloned.1.call-update) | async-done | bytes 4194320 | tf_op jit(solution)/shard_map/all_gather | solution.py:17
  63.5 8.9 %gather_fusion = bf16[92,256,256]{2,1,0:T(8,128)(2,1)} fusion(bf16[32,256,256]{2,1,0:T(8,128)(2,1)} %all-gather.2.cloned.1.call-done, s32[1024]{0:T(1024)S(1)} %pad_clamp_fusion), kind=kCustom, calls=%fused_computation | custom fusion | bytes 24117616 | tf_op jit(solution)/shard_map/gather | solution.py:18
  72.3 20.5 %fusion = f32[92,256,256]{2,1,0:T(8,128)} fusion(bf16[92,256,256]{2,1,0:T(8,128)(2,1)} %param.8, bf16[92,256,256]{2,1,0:T(8,128)(2,1)} %gather_fusion, bf16[92,256,256]{2,1,0:T(8,128)(2,1)} %param.7), kind=kOutput, calls=%fused_computation.2 | convolution fusion | flops 6180044800 | bytes 60293120 | tf_op jit(solution)/shard_map/kab,kbc->kac/dot_general | solution.py:22
  92.8 4.3 %broadcast_in_dim.2 = f32[32,256,256]{2,1,0:T(8,128)} broadcast(f32[]{:T(128)} %constant.4.clone.1), dimensions={} | broadcast | bytes 8388612 | tf_op jit(solution)/shard_map/broadcast_in_dim | solution.py:24
  97.1 0.0 copy-start
  97.1 0.0 copy-start.1
  97.1 54.1 %scatter_fusion = f32[32,256,256]{2,1,0:T(8,128)} fusion(f32[32,256,256]{2,1,0:T(8,128)} %broadcast_in_dim.2, s32[92]{0:T(128)S(1)} %get-tuple-element.13, f32[92,256,256]{2,1,0:T(8,128)} %fusion), kind=kCustom, calls=%fused_computation.1 | custom fusion | flops 6029312 | bytes 72352112 | tf_op jit(solution)/shard_map/scatter-add | solution.py:24
  151.2 0.0 reduce-scatter.2.cloned.1.call-update
  151.3 0.0 copy-done
  151.3 0.0 copy-done.1
  151.3 0.5 fusion.5
  151.8 103.2 %reduce-scatter.2.cloned.1.call-done = f32[2,256,256]{2,1,0:T(8,128)} async-done(((f32[32,256,256]{2,1,0:T(8,128)}), f32[2,256,256]{2,1,0:T(8,128)}) %reduce-scatter.2.cloned.1.call-update) | async-done | bytes 524304 | tf_op jit(solution)/shard_map/reduce_scatter | solution.py:25
  255.0 1.8 multiply_reduce_fusion
  256.7 32.8 %all-reduce = (f32[3]{0:T(128)S(1)}, f32[3]{0:T(128)S(1)}, f32[]{:T(128)}, f32[]{:T(128)}) all-reduce(f32[3]{0:T(128)S(1)} %get-tuple-element.3, f32[3]{0:T(128)S(1)} %get-tuple-element.2, f32[]{:T(128)} %get-tuple-element.5, f32[]{:T(128)} %get-tuple-element.4), channel_id=1, replica_groups=mesh['groups'=2,'sector'=16] {'sector'}, use_global_device_ids=true, to_apply=%region_3.0 | all-reduce | flops 8 | bytes 64 | tf_op jit(solution)/shard_map/psum | solution.py:16
  289.6 0.7 multiply_reduce_fusion.2
  290.3 0.2 fusion.6
  292.5 1.9 multiply_subtract_fusion
  (2 shorter events, 0.0 us)
Async XLA Ops:
  7.2 56.3 %all-gather.2.cloned.1.call-start = ((), (), s32[]{:S(2)}) async-start(), calls=%async_computation.1 | async-start | bytes 4456448 | tf_op jit(solution)/shard_map/all_gather | solution.py:17
  7.9 247.1 %reduce-scatter.2.cloned.1.call-start = ((), (), s32[]{:S(2)}) async-start(), calls=%async_computation.2 | async-start | bytes 8912896 | tf_op jit(solution)/shard_map/reduce_scatter | solution.py:25
  97.1 54.1 %copy-start = (bf16[2,256,256]{2,1,0:T(8,128)(2,1)S(1)}, bf16[2,256,256]{2,1,0:T(8,128)(2,1)}, u32[]{:S(2)}) copy-start(bf16[2,256,256]{2,1,0:T(8,128)(2,1)} %param.5) | copy-start | bytes 786436
  97.1 54.2 %copy-start.1 = (bf16[3,2,256,256]{3,2,1,0:T(8,128)(2,1)S(1)}, bf16[3,2,256,256]{3,2,1,0:T(8,128)(2,1)}, u32[]{:S(2)}) copy-start(bf16[3,2,256,256]{3,2,1,0:T(8,128)(2,1)} %param.6) | copy-start | bytes 2359300
Sparse Core Ops, SparseCore 0:
  10.2 53.2 all-gather.1
  151.4 103.5 reduce-scatter.1
where the time goes:
time: 303 us; the launch traced here: 302 us
  waiting for transfers between devices  159 us (52%)
  other arithmetic  60 us (20%)
  blocking collectives  32.8 us (11%)
  matrix products  20.5 us (7%)
  between operations  17.2 us (6%)
  local copies, waits for them, and re-layouts  13.2 us (4%)
    reduce_scatter x1, waiting for transfers between devices, per_device(): lax.psum_scatter(partial_sigma, 'sector', scatter_dimension=0, tiled=True)  103 us
    all_gather x1, waiting for transfers between devices, per_device(): gathered = lax.all_gather(wavefunction, 'sector', axis=0, tiled=True)  54.7 us
    scatter-add x1, other arithmetic, per_device(): partial_sigma = jax.ops.segment_sum(contrib, targets, num_segments=sectors)  54.1 us
    psum x1, blocking collectives, per_device(): lax.psum((correlation_part, own_part, norm_part), 'sector')  32.8 us
    dot_general x1, matrix products, per_device(): jnp.einsum('kab,kbc->kac', half_block, right_env, preferred_element_type=...  20.5 us
    gather x1, local copies, waits for them, and re-layouts, per_device(): blocks = gathered[term_list[:, 0]]  8.87 us
  transfers between devices with their start and end apart: 2, of which 2 were waited for; matrix products, arithmetic and copies ran while one was open for 0% of the time, Pallas kernels for 0%

commit v1 on v0

v1 whole, which is shorter than its diff:
```python
import functools

import jax
import jax.numpy as jnp
from jax import lax
from jax.experimental import pallas as pl
from jax.experimental.pallas import tpu as pltpu
from jax.sharding import PartitionSpec as P

shift_energy = 2.0
CORES = 2


def ring_of(mesh):
    chips = mesh.shape["sector"] // CORES
    rows = 2 if mesh.shape["groups"] == 2 else 1
    cols = chips // rows
    order = [z * rows for z in range(cols)]
    for y in range(1, rows):
        order += [z * rows + y for z in reversed(range(cols))]
    return order


def term_kernel(block, sectors, src_ref, dst_ref, left_ref, right_ref, *rest):
    pieces, rest = rest[: -8], rest[-8:]
    psi_hbm = [p for p in pieces]
    mine_ref, other_ref, cross_ref, psi, acc, psi_sem, out_sem, offs = rest
    step = pl.program_id(0)
    last = pl.num_programs(0) - 1

    @pl.when(step == 0)
    def _():
        at = 0
        copies = []
        for n, piece in enumerate(psi_hbm):
            size = piece.shape[0]
            copies.append(pltpu.make_async_copy(piece, psi.at[pl.ds(at, size)], psi_sem.at[n]))
            at += size
        for copy in copies:
            copy.start()
        acc[...] = jnp.zeros_like(acc)
        for copy in copies:
            copy.wait()

    for t in range(block):
        k = step * block + t
        source, target = src_ref[k], dst_ref[k]
        half = jnp.dot(left_ref[t], psi[source], preferred_element_type=jnp.float32).astype(jnp.bfloat16)
        acc[target] += jnp.dot(half, right_ref[t], preferred_element_type=jnp.float32)

    @pl.when(step == last)
    def _():
        half = sectors // 2
        one = pltpu.make_async_copy(acc.at[pl.ds(0, half)], mine_ref, out_sem.at[0])
        two = pltpu.make_async_copy(acc.at[pl.ds(half, half)], other_ref, out_sem.at[1])
        two.start()
        one.start()

        def add(s, total):
            return total + jnp.sum((acc[s] * psi[s].astype(jnp.float32)).reshape(-1, 8, 256), axis=0)

        total = lax.fori_loop(0, sectors, add, jnp.zeros((8, 256), jnp.float32))
        cross_ref[...] = total[:, :128] + total[:, 128:]
        two.wait()
        one.wait()


def all_terms(src, dst, left, right, pieces, sectors):
    terms, side, _ = left.shape
    block = next(b for b in (4, 2, 1) if terms % b == 0)
    half = sectors // 2
    env = pl.BlockSpec((block, side, side), lambda i, *_: (i, 0, 0))
    return pl.pallas_call(
        functools.partial(term_kernel, block, sectors),
        grid_spec=pltpu.PrefetchScalarGridSpec(
            num_scalar_prefetch=2,
            grid=(terms // block,),
            in_specs=[env, env] + [pl.BlockSpec(memory_space=pl.ANY)] * len(pieces),
            out_specs=[
                pl.BlockSpec(memory_space=pl.ANY),
                pl.BlockSpec(memory_space=pl.ANY),
                pl.BlockSpec((8, 128), lambda i, *_: (0, 0)),
            ],
            scratch_shapes=[
                pltpu.VMEM((sectors, side, side), jnp.bfloat16),
                pltpu.VMEM((sectors, side, side), jnp.float32),
                pltpu.SemaphoreType.DMA((len(pieces),)),
                pltpu.SemaphoreType.DMA((2,)),
                pltpu.SMEM((1,), jnp.int32),
            ],
        ),
        out_shape=[
            jax.ShapeDtypeStruct((half, side, side), jnp.float32),
            jax.ShapeDtypeStruct((half, side, side), jnp.float32),
            jax.ShapeDtypeStruct((8, 128), jnp.float32),
        ],
        compiler_params=pltpu.CompilerParams(
            dimension_semantics=("arbitrary",), vmem_limit_bytes=40 * 1024 * 1024
        ),
        cost_estimate=pl.CostEstimate(
            flops=4 * terms * side**3, bytes_accessed=4 * terms * side * side, transcendentals=0
        ),
    )(src, dst, left, right, *pieces)


def make_per_device(mesh):
    devices = mesh.shape["sector"]
    ring = ring_of(mesh)
    chips = len(ring)
    place = [ring.index(c) for c in range(chips)]

    def shift(by):
        return [
            (ring[p] * CORES + c, ring[(p + by) % chips] * CORES + c) for p in range(chips) for c in range(CORES)
        ]

    to_right, to_left = shift(1), shift(-1)
    swap = [(i, i ^ 1) for i in range(devices)]

    def right(x):
        return lax.ppermute(x, "sector", to_right)

    def left(x):
        return lax.ppermute(x, "sector", to_left)

    def across(x):
        return lax.ppermute(x, "sector", swap)

    def everywhere(sums, tops):
        hop = 1
        while hop < devices:
            pairs = [(i, i ^ hop) for i in range(devices)]
            both = lax.ppermute(jnp.concatenate([sums, tops]), "sector", pairs)
            sums, tops = sums + both[: sums.shape[0]], jnp.maximum(tops, both[sums.shape[0] :])
            hop *= 2
        return sums, tops

    def per_device(wavefunction, lower_states, left_env, right_env, term_list):
        per, side, _ = wavefunction.shape
        sectors = per * devices
        part = per // 2
        me = lax.axis_index("sector")
        my_place, my_core = jnp.asarray(place, jnp.int32)[me // CORES], me % CORES

        def slot(sector):
            chip, core, j = sector // (per * CORES), (sector // per) % CORES, sector % per
            rel = (jnp.asarray(place, jnp.int32)[chip] - my_place) % chips
            return jnp.where(core == my_core, 0, chips * per) + rel * per + j

        src, dst = slot(term_list[:, 0]), slot(term_list[:, 1])

        got = {0: [wavefunction]}
        r = l = wavefunction
        for s in range(1, chips // 2):
            r, l = right(r), left(l)
            got[chips - s], got[s] = [r], [l]
        got[chips // 2] = [right(r[:part]), left(l[part:])]
        own = [piece for rel in range(chips) for piece in got[rel]]
        pieces = own + [across(p) for p in own]

        psi_local = wavefunction.astype(jnp.float32)
        lower_local = lower_states.astype(jnp.float32)
        correlation_part = jnp.sum(lower_local * psi_local[None], axis=(1, 2, 3))
        own_part = jnp.sum(lower_local * lower_local, axis=(1, 2, 3))
        norm_part = jnp.sum(psi_local * psi_local)
        tops = jnp.stack([jnp.max(jnp.abs(a)).astype(jnp.float32) for a in (wavefunction, left_env, right_env)])
        sums, tops = everywhere(jnp.concatenate([correlation_part, own_part, norm_part[None]]), tops)
        lower_count = lower_states.shape[0]
        correlation, own_norm, psi_norm = sums[:lower_count], sums[lower_count : 2 * lower_count], sums[-1]
        bound = 1.02 * left_env.shape[0] * devices * side * side * (tops[0] * tops[1] * tops[2])
        power = jnp.clip(15.0 - jnp.ceil(jnp.log2(jnp.maximum(bound, 1e-30))), -60.0, 90.0)
        scale, unscale = jnp.exp2(power), 1.0 / jnp.exp2(power)

        mine, other, cross = all_terms(src, dst, left_env, right_env, pieces, sectors)
        cross_sum, _ = everywhere(jnp.sum(cross)[None], tops[:1])

        got_other = across(other)
        partial = mine + got_other

        def pack(x):
            return (x * scale).astype(jnp.float16)

        def unpack(x):
            return x.astype(jnp.float32) * unscale

        def chunk(rel):
            return partial[rel % chips * per : (rel % chips + 1) * per]

        far = chunk(chips // 2)
        r, l = right(pack(far[:part])), left(pack(far[part:]))
        zero = jnp.zeros((part, side, side), jnp.float32)
        r, l = jnp.concatenate([unpack(r), zero]), jnp.concatenate([zero, unpack(l)])
        for s in range(chips // 2 - 1, 0, -1):
            r, l = unpack(right(pack(chunk(s) + r))), unpack(left(pack(chunk(-s) + l)))
        sigma_local = chunk(0) + r + l

        coeffs = correlation / own_norm
        deflated = sigma_local + shift_energy * jnp.sum(coeffs[:, None, None, None] * lower_local, axis=0)
        ritz_value = (cross_sum[0] + shift_energy * jnp.sum(coeffs * correlation)) / psi_norm
        residual = deflated - ritz_value * psi_local
        return (residual, ritz_value.reshape(1))

    return per_device


def solution(mesh):
    return jax.shard_map(
        make_per_device(mesh),
        mesh=mesh,
        in_specs=(
            P(("groups", "sector"), None, None),
            P(None, ("groups", "sector"), None, None),
            P(("groups", "sector"), None, None),
            P(("groups", "sector"), None, None),
            P(("groups", "sector"), None),
        ),
        out_specs=(P(("groups", "sector"), None, None), P("groups")),
        check_vma=False,
    )
```

time: 303 us -> 167 us (0.55)
  waiting for transfers between devices: 159 us -> 51.4 us
  blocking collectives: 32.8 us -> 0 us
  starting transfers between devices: 0.08 us -> 29 us
  other arithmetic: 60 us -> 34 us
  Pallas kernels: 0 us -> 25.7 us
  matrix products: 20.5 us -> 0 us
  between operations: 17.2 us -> 12.3 us
    reduce_scatter x1 -> x0, waiting for transfers between devices: 103 us -> none  [per_device(): lax.psum_scatter(partial_sigma, 'sector', scatter_dimension=0, tiled=True)]
    all_gather x1 -> x0, waiting for transfers between devices: 54.7 us -> none  [per_device(): gathered = lax.all_gather(wavefunction, 'sector', axis=0, tiled=True)]
    scatter-add x1 -> x0, other arithmetic: 54.1 us -> none  [per_device(): partial_sigma = jax.ops.segment_sum(contrib, targets, num_segments=sectors)]
    ppermute x0 -> x34, waiting for transfers between devices: none -> 51.4 us  [the longest x8 29.2 us: right(): return lax.ppermute(x, 'sector', to_right)]
    psum x1 -> x0, blocking collectives: 32.8 us -> none  [per_device(): lax.psum((correlation_part, own_part, norm_part), 'sector')]
    ppermute x0 -> x34, starting transfers between devices: none -> 29 us  [the longest x8 14.4 us: right(): return lax.ppermute(x, 'sector', to_right)]
    pallas_call x0 -> x1, Pallas kernels: none -> 25.7 us  [all_terms(): pl.pallas_call(functools.partial(term_kernel, block, sectors), grid_spec=...]
    dot_general x1 -> x0, matrix products: 20.5 us -> none  [per_device(): jnp.einsum('kab,kbc->kac', half_block, right_env, preferred_element_type=...]
  transfers between devices with their start and end apart: 2 -> 34, of which waited for: 2 -> 17; matrix products, arithmetic and copies ran while one was open for 0% -> 20% of each run, Pallas kernels for 0% -> 0%
where the time goes in v1:
time: 167 us; the launch traced here: 165 us
  waiting for transfers between devices  51.4 us (31%)
  other arithmetic  34 us (20%)
  starting transfers between devices  29 us (17%)
  Pallas kernels  25.7 us (15%)
  local copies, waits for them, and re-layouts  13 us (8%)
  between operations  12.3 us (7%)
    ppermute x8, waiting for transfers between devices, right(): return lax.ppermute(x, 'sector', to_right)  29.2 us
    pallas_call x1, Pallas kernels, all_terms(): pl.pallas_call(functools.partial(term_kernel, block, sectors), grid_spec=...  25.7 us
    ppermute x8, waiting for transfers between devices, everywhere(): both = lax.ppermute(jnp.concatenate([sums, tops]), 'sector', pairs)  15.8 us
    reduce_max x3, other arithmetic, per_device(): jnp.max(jnp.abs(a)).astype(jnp.float32)  14.9 us
    ppermute x8, starting transfers between devices, right(): return lax.ppermute(x, 'sector', to_right)  14.4 us
    ppermute x8, starting transfers between devices, everywhere(): both = lax.ppermute(jnp.concatenate([sums, tops]), 'sector', pairs)  9.72 us
    ppermute x8, waiting for transfers between devices, left(): return lax.ppermute(x, 'sector', to_left)  6.3 us
    convert_element_type x6, other arithmetic, pack(): return (x * scale).astype(jnp.float16)  6.01 us
  transfers between devices with their start and end apart: 34, of which 17 were waited for; matrix products, arithmetic and copies ran while one was open for 20% of the time, Pallas kernels for 0%

profile of v1, /device:TPU:0, one launch (start us, length us, event | category | flops | bytes accessed | tf_op | source)
XLA Modules:
  0.0 165.5 jit_solution(12860666611849498193)
XLA Ops:
  0.6 3.1 %collective-permute-start.3 = (bf16[2,256,256]{2,1,0:T(8,128)(2,1)}, bf16[2,256,256]{2,1,0:T(8,128)(2,1)S(1)}, u32[]{:S(2)}, u32[]{:S(2)}) collective-permute-start(bf16[2,256,256]{2,1,0:T(8,128)(2,1)} %rest_0_.1), channel_id=1, source_target_pairs={{0,4},{1,5},{4,8},{5,9},{8,12},{9,13},{12,14},{13,15},{14,10},{15,... | collective-permute-start | bytes 786440 | tf_op jit(solution)/shard_map/ppermute | solution.py:121
  3.7 6.5 %collective-permute-done.3.rest_8_ = bf16[2,256,256]{2,1,0:T(8,128)(2,1)S(1)} collective-permute-done((bf16[2,256,256]{2,1,0:T(8,128)(2,1)}, bf16[2,256,256]{2,1,0:T(8,128)(2,1)S(1)}, u32[]{:S(2)}, u32[]{:S(2)}) %collective-permute-start.3) | collective-permute-done | bytes 262176 | tf_op jit(solution)/shard_map/ppermute | solution.py:121
  10.2 1.8 %collective-permute-start.4 = (bf16[2,256,256]{2,1,0:T(8,128)(2,1)S(1)}, bf16[2,256,256]{2,1,0:T(8,128)(2,1)S(1)}, u32[]{:S(2)}, u32[]{:S(2)}) collective-permute-start(bf16[2,256,256]{2,1,0:T(8,128)(2,1)S(1)} %collective-permute-done.3.rest_8_), channel_id=1, source_target_pairs={{0,4},{1,5},{4,8},{5,9},{8,12},{9,13},{12,14},{13,15},{14,10},{15,... | collective-permute-start | bytes 786440 | tf_op jit(solution)/shard_map/ppermute | solution.py:121
  12.2 5.5 %collective-permute-done.4.rest_7_ = bf16[2,256,256]{2,1,0:T(8,128)(2,1)S(1)} collective-permute-done((bf16[2,256,256]{2,1,0:T(8,128)(2,1)S(1)}, bf16[2,256,256]{2,1,0:T(8,128)(2,1)S(1)}, u32[]{:S(2)}, u32[]{:S(2)}) %collective-permute-start.4) | collective-permute-done | bytes 262176 | tf_op jit(solution)/shard_map/ppermute | solution.py:121
  17.7 1.5 collective-permute-start.5
  19.1 0.6 collective-permute-start.2
  19.7 0.5 collective-permute-start.16
  20.2 4.0 %collective-permute-done.5.rest_6_ = bf16[2,256,256]{2,1,0:T(8,128)(2,1)S(1)} collective-permute-done((bf16[2,256,256]{2,1,0:T(8,128)(2,1)S(1)}, bf16[2,256,256]{2,1,0:T(8,128)(2,1)S(1)}, u32[]{:S(2)}, u32[]{:S(2)}) %collective-permute-start.5) | collective-permute-done | bytes 262176 | tf_op jit(solution)/shard_map/ppermute | solution.py:121
  24.2 0.7 slice.158
  24.9 0.6 collective-permute-done.2.rest_3_
  25.5 1.6 collective-permute-start.6
  27.1 0.6 slice.159
  28.8 1.2 dynamic_slice.3
  30.0 1.0 collective-permute-done.6.rest_4_
  31.0 2.0 %collective-permute-done.7.rest_5_ = bf16[1,256,256]{2,1,0:T(8,128)(2,1)} collective-permute-done((bf16[1,256,256]{2,1,0:T(8,128)(2,1)}, bf16[1,256,256]{2,1,0:T(8,128)(2,1)}, u32[]{:S(2)}, u32[]{:S(2)}) %collective-permute-start.7) | collective-permute-done | bytes 131104 | tf_op jit(solution)/shard_map/ppermute | solution.py:124
  33.0 1.4 fusion.21
  34.6 0.9 copy-done
  35.5 25.7 %shard_map.95 = (f32[16,256,256]{2,1,0:T(8,128)S(1)}, f32[16,256,256]{2,1,0:T(8,128)}, f32[8,128]{1,0:T(8,128)S(1)}) custom-call(s32[92]{0:T(128)S(1)} %get-tuple-element.19.src_ref, s32[92]{0:T(128)S(1)} %get-tuple-element.18.dst_ref, bf16[92,256,256]{2,1,0:T(8,128)(2,1)} %left_ref.1, bf16[92,256,256]{2,1,0:T(8,128)(2,1)} %right_ref.1, ...), custom_call_target="tpu_custom_call" | custom-call | flops 6174015488 | bytes 24117248 | tf_op jit(solution)/shard_map/pallas_call | solution.py:73
  61.3 2.0 %copy-done.2 = f32[16,256,256]{2,1,0:T(8,128)} copy-done((f32[16,256,256]{2,1,0:T(8,128)}, f32[16,256,256]{2,1,0:T(8,128)S(1)}, u32[]{:S(2)}) %copy-start.2) | copy-done | bytes 4194328
  63.7 0.7 multiply_reduce_fusion
  64.5 0.6 abs_reduce_fusion.2
  65.6 7.1 %abs_reduce_fusion.1 = bf16[]{:T(256)} fusion(bf16[92,256,256]{2,1,0:T(8,128)(2,1)} %left_ref.1), kind=kLoop, calls=%fused_computation.1 | loop fusion | flops 12058623 | bytes 12058626 | tf_op jit(solution)/shard_map/reduce_max | solution.py:166
  72.7 7.1 %abs_reduce_fusion = bf16[]{:T(256)} fusion(bf16[92,256,256]{2,1,0:T(8,128)(2,1)} %right_ref.1), kind=kLoop, calls=%fused_computation | loop fusion | flops 12058623 | bytes 12058626 | tf_op jit(solution)/shard_map/reduce_max | solution.py:166
  79.8 2.5 %concatenate.34 = f32[10]{0:T(128)S(1)} concatenate(f32[3]{0:T(128)S(1)} %get-tuple-element.8, f32[3]{0:T(128)S(1)} %get-tuple-element.9, f32[1]{0:T(128)} %bitcast.10, bf16[1]{0:T(256)(128)(2,1)} %bitcast.11, bf16[1]{0:T(256)(128)(2,1)} %bitcast.12, bf16[1]{0:T(256)(128)(2,1)} %bitcast.13), dimensions={0} | concatenate | bytes 74 | tf_op jit(solution)/shard_map/concatenate | solution.py:133
  84.3 0.7 maximum_add_fusion
  85.2 0.5 collective-permute-start.19
  85.7 3.0 %collective-permute-done.19 = f32[10]{0:T(128)S(1)} collective-permute-done((f32[10]{0:T(128)S(1)}, f32[10]{0:T(128)S(1)}, u32[]{:S(2)}, u32[]{:S(2)}) %collective-permute-start.19) | collective-permute-done | bytes 72 | tf_op jit(solution)/shard_map/ppermute | solution.py:133
  88.9 1.6 collective-permute-start.20
  90.5 2.0 %collective-permute-done.20 = f32[10]{0:T(128)S(1)} collective-permute-done((f32[10]{0:T(128)S(1)}, f32[10]{0:T(128)S(1)}, u32[]{:S(2)}, u32[]{:S(2)}) %collective-permute-start.20) | collective-permute-done | bytes 72 | tf_op jit(solution)/shard_map/ppermute | solution.py:133
  92.6 2.5 %collective-permute-start.21 = (f32[10]{0:T(128)S(1)}, f32[10]{0:T(128)S(1)}, u32[]{:S(2)}, u32[]{:S(2)}) collective-permute-start(f32[10]{0:T(128)S(1)} %pad_maximum_fusion.2), channel_id=1, source_target_pairs={{0,8},{1,9},{2,10},{3,11},{4,12},{5,13},{6,14},{7,15},{8,0},{9,1},... | collective-permute-start | bytes 128 | tf_op jit(solution)/shard_map/ppermute | solution.py:133
  95.1 1.9 %collective-permute-done.21 = f32[10]{0:T(128)S(1)} collective-permute-done((f32[10]{0:T(128)S(1)}, f32[10]{0:T(128)S(1)}, u32[]{:S(2)}, u32[]{:S(2)}) %collective-permute-start.21) | collective-permute-done | bytes 72 | tf_op jit(solution)/shard_map/ppermute | solution.py:133
  97.1 0.6 fusion.37
  99.7 4.0 %add.135 = f32[16,256,256]{2,1,0:T(8,128)S(1)} add(f32[16,256,256]{2,1,0:T(8,128)} %copy-done.2, f32[16,256,256]{2,1,0:T(8,128)} %collective-permute-done.17) | non-fusion elementwise | flops 1048576 | bytes 12582912 | tf_op jit(solution)/shard_map/add | solution.py:178
  103.8 1.9 %copy-done.3 = f32[16,256,256]{2,1,0:T(8,128)} copy-done((f32[16,256,256]{2,1,0:T(8,128)}, f32[16,256,256]{2,1,0:T(8,128)S(1)}, u32[]{:S(2)}) %copy-start.3) | copy-done | bytes 4194328
  105.8 1.6 collective-permute-start.22
  107.5 3.7 %collective-permute-done.22 = f16[1,256,256]{2,1,0:T(8,128)(2,1)S(1)} collective-permute-done((f16[1,256,256]{2,1,0:T(8,128)(2,1)S(1)}, f16[1,256,256]{2,1,0:T(8,128)(2,1)S(1)}, u32[]{:S(2)}, u32[]{:S(2)}) %collective-permute-start.22) | collective-permute-done | bytes 131104 | tf_op jit(solution)/shard_map/ppermute | solution.py:121
  111.2 1.1 fusion.10
  112.3 1.6 collective-permute-start.23
  114.4 5.8 %collective-permute-done.23 = f16[2,256,256]{2,1,0:T(8,128)(2,1)S(1)} collective-permute-done((f16[2,256,256]{2,1,0:T(8,128)(2,1)S(1)}, f16[2,256,256]{2,1,0:T(8,128)(2,1)S(1)}, u32[]{:S(2)}, u32[]{:S(2)}) %collective-permute-start.23) | collective-permute-done | bytes 262176 | tf_op jit(solution)/shard_map/ppermute | solution.py:121
  120.2 1.2 fusion.12
  121.3 1.6 collective-permute-start.24
  123.0 0.7 multiply_reduce_fusion.1
  123.6 0.6 slice.139
  125.0 2.8 %collective-permute-done.24 = f16[2,256,256]{2,1,0:T(8,128)(2,1)S(1)} collective-permute-done((f16[2,256,256]{2,1,0:T(8,128)(2,1)S(1)}, f16[2,256,256]{2,1,0:T(8,128)(2,1)S(1)}, u32[]{:S(2)}, u32[]{:S(2)}) %collective-permute-start.24) | collective-permute-done | bytes 262176 | tf_op jit(solution)/shard_map/ppermute | solution.py:121
  127.7 1.4 fusion.14
  129.1 0.6 collective-permute-start.27
  129.9 0.6 reduce_sum.58
  130.5 1.3 pad_maximum_fusion.3
  131.9 3.7 %collective-permute-done.27 = f16[2,256,256]{2,1,0:T(8,128)(2,1)S(1)} collective-permute-done((f16[2,256,256]{2,1,0:T(8,128)(2,1)S(1)}, f16[2,256,256]{2,1,0:T(8,128)(2,1)S(1)}, u32[]{:S(2)}, u32[]{:S(2)}) %collective-permute-start.27) | collective-permute-done | bytes 262176 | tf_op jit(solution)/shard_map/ppermute | solution.py:124
  135.6 1.2 fusion.6
  136.7 0.6 collective-permute-start.28
  137.3 0.6 fusion.36
  140.4 0.9 collective-permute-start.31
  141.4 2.6 %collective-permute-done.31 = f32[2]{0:T(128)S(1)} collective-permute-done((f32[2]{0:T(128)S(1)}, f32[2]{0:T(128)S(1)}, u32[]{:S(2)}, u32[]{:S(2)}) %collective-permute-start.31) | collective-permute-done | bytes 40 | tf_op jit(solution)/shard_map/ppermute | solution.py:133
  144.0 0.6 fusion.35
  145.9 1.6 collective-permute-start.25
  147.4 1.2 fusion.8
  148.6 0.6 collective-permute-start.29
  149.2 1.5 collective-permute-start.32
  150.7 4.3 %collective-permute-done.32 = f32[2]{0:T(128)S(1)} collective-permute-done((f32[2]{0:T(128)S(1)}, f32[2]{0:T(128)S(1)}, u32[]{:S(2)}, u32[]{:S(2)}) %collective-permute-start.32) | collective-permute-done | bytes 40 | tf_op jit(solution)/shard_map/ppermute | solution.py:133
  155.1 0.6 fusion.34
  157.0 2.5 %collective-permute-start.33 = (f32[2]{0:T(128)S(1)}, f32[2]{0:T(128)S(1)}, u32[]{:S(2)}, u32[]{:S(2)}) collective-permute-start(f32[2]{0:T(128)S(1)} %pad_maximum_fusion.6), channel_id=1, source_target_pairs={{0,8},{1,9},{2,10},{3,11},{4,12},{5,13},{6,14},{7,15},{8,0},{9,1},... | collective-permute-start | bytes 32 | tf_op jit(solution)/shard_map/ppermute | solution.py:133
  159.6 1.9 %collective-permute-done.33 = f32[2]{0:T(128)S(1)} collective-permute-done((f32[2]{0:T(128)S(1)}, f32[2]{0:T(128)S(1)}, u32[]{:S(2)}, u32[]{:S(2)}) %collective-permute-start.33) | collective-permute-done | bytes 40 | tf_op jit(solution)/shard_map/ppermute | solution.py:133
  162.3 2.0 %fusion.17 = f32[2,256,256]{2,1,0:T(8,128)} fusion(f32[16,256,256]{2,1,0:T(8,128)} %copy-done.3, f32[2,256,256]{2,1,0:T(8,128)S(1)} %fusion.2, f16[2,256,256]{2,1,0:T(8,128)(2,1)S(1)} %collective-permute-done.29, f16[2,256,256]{2,1,0:T(8,128)(2,1)S(1)} %collective-permute-done.25, f32[]{:T(128)} %div.71, f32[]{:T(128)S(6)} %div.69, ...), kind=kLoop, calls=%fused_computation.29 | loop fusion | flops 1441792 | bytes 2359304 | tf_op jit(solution)/shard_map/sub | solution.py:200
  (60 shorter events, 4.0 us)
Async XLA Ops:
  0.6 9.5 %collective-permute-start.3 = (bf16[2,256,256]{2,1,0:T(8,128)(2,1)}, bf16[2,256,256]{2,1,0:T(8,128)(2,1)S(1)}, u32[]{:S(2)}, u32[]{:S(2)}) collective-permute-start(bf16[2,256,256]{2,1,0:T(8,128)(2,1)} %rest_0_.1), channel_id=1, source_target_pairs={{0,4},{1,5},{4,8},{5,9},{8,12},{9,13},{12,14},{13,15},{14,10},{15,... | collective-permute-start | bytes 786440 | tf_op jit(solution)/shard_map/ppermute | solution.py:121
  3.7 8.3 %collective-permute-start = (bf16[2,256,256]{2,1,0:T(8,128)(2,1)}, bf16[2,256,256]{2,1,0:T(8,128)(2,1)S(1)}, u32[]{:S(2)}, u32[]{:S(2)}) collective-permute-start(bf16[2,256,256]{2,1,0:T(8,128)(2,1)} %rest_0_.1), channel_id=1, source_target_pairs={{0,2},{1,3},{4,0},{5,1},{8,4},{9,5},{12,8},{13,9},{14,12},{15,13},... | collective-permute-start | bytes 786440 | tf_op jit(solution)/shard_map/ppermute | solution.py:124
  10.2 7.5 %collective-permute-start.4 = (bf16[2,256,256]{2,1,0:T(8,128)(2,1)S(1)}, bf16[2,256,256]{2,1,0:T(8,128)(2,1)S(1)}, u32[]{:S(2)}, u32[]{:S(2)}) collective-permute-start(bf16[2,256,256]{2,1,0:T(8,128)(2,1)S(1)} %collective-permute-done.3.rest_8_), channel_id=1, source_target_pairs={{0,4},{1,5},{4,8},{5,9},{8,12},{9,13},{12,14},{13,15},{14,10},{15,... | collective-permute-start | bytes 786440 | tf_op jit(solution)/shard_map/ppermute | solution.py:121
  12.0 7.2 %collective-permute-start.1 = (bf16[2,256,256]{2,1,0:T(8,128)(2,1)S(1)}, bf16[2,256,256]{2,1,0:T(8,128)(2,1)S(1)}, u32[]{:S(2)}, u32[]{:S(2)}) collective-permute-start(bf16[2,256,256]{2,1,0:T(8,128)(2,1)S(1)} %collective-permute-done.rest_1_), channel_id=1, source_target_pairs={{0,2},{1,3},{4,0},{5,1},{8,4},{9,5},{12,8},{13,9},{14,12},{15,13},... | collective-permute-start | bytes 786440 | tf_op jit(solution)/shard_map/ppermute | solution.py:124
  17.7 6.6 %collective-permute-start.5 = (bf16[2,256,256]{2,1,0:T(8,128)(2,1)S(1)}, bf16[2,256,256]{2,1,0:T(8,128)(2,1)S(1)}, u32[]{:S(2)}, u32[]{:S(2)}) collective-permute-start(bf16[2,256,256]{2,1,0:T(8,128)(2,1)S(1)} %collective-permute-done.4.rest_7_), channel_id=1, source_target_pairs={{0,4},{1,5},{4,8},{5,9},{8,12},{9,13},{12,14},{13,15},{14,10},{15,... | collective-permute-start | bytes 786440 | tf_op jit(solution)/shard_map/ppermute | solution.py:121
  19.1 6.4 %collective-permute-start.2 = (bf16[2,256,256]{2,1,0:T(8,128)(2,1)S(1)}, bf16[2,256,256]{2,1,0:T(8,128)(2,1)S(1)}, u32[]{:S(2)}, u32[]{:S(2)}) collective-permute-start(bf16[2,256,256]{2,1,0:T(8,128)(2,1)S(1)} %collective-permute-done.1.rest_2_), channel_id=1, source_target_pairs={{0,2},{1,3},{4,0},{5,1},{8,4},{9,5},{12,8},{13,9},{14,12},{15,13},... | collective-permute-start | bytes 786440 | tf_op jit(solution)/shard_map/ppermute | solution.py:124
  19.7 8.1 %collective-permute-start.8 = (bf16[2,256,256]{2,1,0:T(8,128)(2,1)}, bf16[2,256,256]{2,1,0:T(8,128)(2,1)S(1)}, u32[]{:S(2)}, u32[]{:S(2)}) collective-permute-start(bf16[2,256,256]{2,1,0:T(8,128)(2,1)} %rest_0_.1), channel_id=1, source_target_pairs={{0,1},{1,0},{2,3},{3,2},{4,5},{5,4},{6,7},{7,6},{8,9},{9,8},{10,11... | collective-permute-start | bytes 786440 | tf_op jit(solution)/shard_map/ppermute | solution.py:127
  19.7 8.5 %collective-permute-start.16 = (bf16[2,256,256]{2,1,0:T(8,128)(2,1)S(1)}, bf16[2,256,256]{2,1,0:T(8,128)(2,1)S(1)}, u32[]{:S(2)}, u32[]{:S(2)}) collective-permute-start(bf16[2,256,256]{2,1,0:T(8,128)(2,1)S(1)} %collective-permute-done.3.rest_8_), channel_id=1, source_target_pairs={{0,1},{1,0},{2,3},{3,2},{4,5},{5,4},{6,7},{7,6},{8,9},{9,8},{10,11... | collective-permute-start | bytes 786440 | tf_op jit(solution)/shard_map/ppermute | solution.py:127
  20.2 8.0 %collective-permute-start.9 = (bf16[2,256,256]{2,1,0:T(8,128)(2,1)S(1)}, bf16[2,256,256]{2,1,0:T(8,128)(2,1)S(1)}, u32[]{:S(2)}, u32[]{:S(2)}) collective-permute-start(bf16[2,256,256]{2,1,0:T(8,128)(2,1)S(1)} %collective-permute-done.rest_1_), channel_id=1, source_target_pairs={{0,1},{1,0},{2,3},{3,2},{4,5},{5,4},{6,7},{7,6},{8,9},{9,8},{10,11... | collective-permute-start | bytes 786440 | tf_op jit(solution)/shard_map/ppermute | solution.py:127
  24.2 4.5 %collective-permute-start.10 = (bf16[2,256,256]{2,1,0:T(8,128)(2,1)S(1)}, bf16[2,256,256]{2,1,0:T(8,128)(2,1)S(1)}, u32[]{:S(2)}, u32[]{:S(2)}) collective-permute-start(bf16[2,256,256]{2,1,0:T(8,128)(2,1)S(1)} %collective-permute-done.1.rest_2_), channel_id=1, source_target_pairs={{0,1},{1,0},{2,3},{3,2},{4,5},{5,4},{6,7},{7,6},{8,9},{9,8},{10,11... | collective-permute-start | bytes 786440 | tf_op jit(solution)/shard_map/ppermute | solution.py:127
  25.5 5.5 %collective-permute-start.6 = (bf16[1,256,256]{2,1,0:T(8,128)(2,1)}, bf16[1,256,256]{2,1,0:T(8,128)(2,1)S(1)}, u32[]{:S(2)}, u32[]{:S(2)}) collective-permute-start(bf16[1,256,256]{2,1,0:T(8,128)(2,1)} %slice.158), channel_id=1, source_target_pairs={{0,4},{1,5},{4,8},{5,9},{8,12},{9,13},{12,14},{13,15},{14,10},{15,... | collective-permute-start | bytes 393224 | tf_op jit(solution)/shard_map/ppermute | solution.py:121
  27.7 5.3 %collective-permute-start.7 = (bf16[1,256,256]{2,1,0:T(8,128)(2,1)}, bf16[1,256,256]{2,1,0:T(8,128)(2,1)}, u32[]{:S(2)}, u32[]{:S(2)}) collective-permute-start(bf16[1,256,256]{2,1,0:T(8,128)(2,1)} %slice.159), channel_id=1, source_target_pairs={{0,2},{1,3},{4,0},{5,1},{8,4},{9,5},{12,8},{13,9},{14,12},{15,13},... | collective-permute-start | bytes 393224 | tf_op jit(solution)/shard_map/ppermute | solution.py:124
  28.2 6.3 %collective-permute-start.15 = (bf16[2,256,256]{2,1,0:T(8,128)(2,1)S(1)}, bf16[2,256,256]{2,1,0:T(8,128)(2,1)S(1)}, u32[]{:S(2)}, u32[]{:S(2)}) collective-permute-start(bf16[2,256,256]{2,1,0:T(8,128)(2,1)S(1)} %collective-permute-done.4.rest_7_), channel_id=1, source_target_pairs={{0,1},{1,0},{2,3},{3,2},{4,5},{5,4},{6,7},{7,6},{8,9},{9,8},{10,11... | collective-permute-start | bytes 786440 | tf_op jit(solution)/shard_map/ppermute | solution.py:127
  28.2 6.4 %collective-permute-start.11 = (bf16[2,256,256]{2,1,0:T(8,128)(2,1)S(1)}, bf16[2,256,256]{2,1,0:T(8,128)(2,1)S(1)}, u32[]{:S(2)}, u32[]{:S(2)}) collective-permute-start(bf16[2,256,256]{2,1,0:T(8,128)(2,1)S(1)} %collective-permute-done.2.rest_3_), channel_id=1, source_target_pairs={{0,1},{1,0},{2,3},{3,2},{4,5},{5,4},{6,7},{7,6},{8,9},{9,8},{10,11... | collective-permute-start | bytes 786440 | tf_op jit(solution)/shard_map/ppermute | solution.py:127
  28.7 5.9 %collective-permute-start.14 = (bf16[2,256,256]{2,1,0:T(8,128)(2,1)S(1)}, bf16[2,256,256]{2,1,0:T(8,128)(2,1)S(1)}, u32[]{:S(2)}, u32[]{:S(2)}) collective-permute-start(bf16[2,256,256]{2,1,0:T(8,128)(2,1)S(1)} %collective-permute-done.5.rest_6_), channel_id=1, source_target_pairs={{0,1},{1,0},{2,3},{3,2},{4,5},{5,4},{6,7},{7,6},{8,9},{9,8},{10,11... | collective-permute-start | bytes 786440 | tf_op jit(solution)/shard_map/ppermute | solution.py:127
  31.0 3.5 %collective-permute-start.12 = (bf16[1,256,256]{2,1,0:T(8,128)(2,1)S(1)}, bf16[1,256,256]{2,1,0:T(8,128)(2,1)S(1)}, u32[]{:S(2)}, u32[]{:S(2)}) collective-permute-start(bf16[1,256,256]{2,1,0:T(8,128)(2,1)S(1)} %collective-permute-done.6.rest_4_), channel_id=1, source_target_pairs={{0,1},{1,0},{2,3},{3,2},{4,5},{5,4},{6,7},{7,6},{8,9},{9,8},{10,11... | collective-permute-start | bytes 393224 | tf_op jit(solution)/shard_map/ppermute | solution.py:127
  33.0 1.6 collective-permute-start.13
  34.6 1.0 copy-start
  35.5 29.5 %copy-start.4 = (bf16[3,2,256,256]{3,2,1,0:T(8,128)(2,1)S(1)}, bf16[3,2,256,256]{3,2,1,0:T(8,128)(2,1)}, u32[]{:S(2)}) copy-start(bf16[3,2,256,256]{3,2,1,0:T(8,128)(2,1)} %param.9) | copy-start | bytes 2359300
  61.3 2.0 %copy-start.2 = (f32[16,256,256]{2,1,0:T(8,128)}, f32[16,256,256]{2,1,0:T(8,128)S(1)}, u32[]{:S(2)}) copy-start(f32[16,256,256]{2,1,0:T(8,128)S(1)} %get-tuple-element.5) | copy-start | bytes 12582916
  63.3 36.4 %collective-permute-start.17 = (f32[16,256,256]{2,1,0:T(8,128)}, f32[16,256,256]{2,1,0:T(8,128)}, u32[]{:S(2)}, u32[]{:S(2)}) collective-permute-start(f32[16,256,256]{2,1,0:T(8,128)} %get-tuple-element.6), channel_id=1, source_target_pairs={{0,1},{1,0},{2,3},{3,2},{4,5},{5,4},{6,7},{7,6},{8,9},{9,8},{10,11... | collective-permute-start | bytes 12582920 | tf_op jit(solution)/shard_map/ppermute | solution.py:127
  82.4 1.9 %collective-permute-start.18 = (f32[10]{0:T(128)S(1)}, f32[10]{0:T(128)S(1)}, u32[]{:S(2)}, u32[]{:S(2)}) collective-permute-start(f32[10]{0:T(128)S(1)} %concatenate.34), channel_id=1, source_target_pairs={{0,1},{1,0},{2,3},{3,2},{4,5},{5,4},{6,7},{7,6},{8,9},{9,8},{10,11... | collective-permute-start | bytes 128 | tf_op jit(solution)/shard_map/ppermute | solution.py:133
  85.2 3.5 %collective-permute-start.19 = (f32[10]{0:T(128)S(1)}, f32[10]{0:T(128)S(1)}, u32[]{:S(2)}, u32[]{:S(2)}) collective-permute-start(f32[10]{0:T(128)S(1)} %pad_maximum_fusion), channel_id=1, source_target_pairs={{0,2},{1,3},{2,0},{3,1},{4,6},{5,7},{6,4},{7,5},{8,10},{9,11},{10,... | collective-permute-start | bytes 128 | tf_op jit(solution)/shard_map/ppermute | solution.py:133
  88.9 3.5 %collective-permute-start.20 = (f32[10]{0:T(128)S(1)}, f32[10]{0:T(128)S(1)}, u32[]{:S(2)}, u32[]{:S(2)}) collective-permute-start(f32[10]{0:T(128)S(1)} %pad_maximum_fusion.1), channel_id=1, source_target_pairs={{0,4},{1,5},{2,6},{3,7},{4,0},{5,1},{6,2},{7,3},{8,12},{9,13},{10,... | collective-permute-start | bytes 128 | tf_op jit(solution)/shard_map/ppermute | solution.py:133
  92.6 4.4 %collective-permute-start.21 = (f32[10]{0:T(128)S(1)}, f32[10]{0:T(128)S(1)}, u32[]{:S(2)}, u32[]{:S(2)}) collective-permute-start(f32[10]{0:T(128)S(1)} %pad_maximum_fusion.2), channel_id=1, source_target_pairs={{0,8},{1,9},{2,10},{3,11},{4,12},{5,13},{6,14},{7,15},{8,0},{9,1},... | collective-permute-start | bytes 128 | tf_op jit(solution)/shard_map/ppermute | solution.py:133
  103.8 1.9 %copy-start.3 = (f32[16,256,256]{2,1,0:T(8,128)}, f32[16,256,256]{2,1,0:T(8,128)S(1)}, u32[]{:S(2)}) copy-start(f32[16,256,256]{2,1,0:T(8,128)S(1)} %add.135) | copy-start | bytes 12582916
  103.8 25.9 %copy-start.5 = (bf16[3,2,256,256]{3,2,1,0:T(8,128)(2,1)S(1)}, bf16[3,2,256,256]{3,2,1,0:T(8,128)(2,1)}, u32[]{:S(2)}) copy-start(bf16[3,2,256,256]{3,2,1,0:T(8,128)(2,1)} %param.9) | copy-start | bytes 2359300
  105.8 5.4 %collective-permute-start.22 = (f16[1,256,256]{2,1,0:T(8,128)(2,1)S(1)}, f16[1,256,256]{2,1,0:T(8,128)(2,1)S(1)}, u32[]{:S(2)}, u32[]{:S(2)}) collective-permute-start(f16[1,256,256]{2,1,0:T(8,128)(2,1)S(1)} %get-tuple-element.14), channel_id=1, source_target_pairs={{0,4},{1,5},{4,8},{5,9},{8,12},{9,13},{12,14},{13,15},{14,10},{15,... | collective-permute-start | bytes 393224 | tf_op jit(solution)/shard_map/ppermute | solution.py:121
  107.4 54.8 %copy-start.1 = (bf16[2,256,256]{2,1,0:T(8,128)(2,1)S(1)}, bf16[2,256,256]{2,1,0:T(8,128)(2,1)}, u32[]{:S(2)}) copy-start(bf16[2,256,256]{2,1,0:T(8,128)(2,1)} %rest_0_.1) | copy-start | bytes 786436
  112.3 7.9 %collective-permute-start.23 = (f16[2,256,256]{2,1,0:T(8,128)(2,1)S(1)}, f16[2,256,256]{2,1,0:T(8,128)(2,1)S(1)}, u32[]{:S(2)}, u32[]{:S(2)}) collective-permute-start(f16[2,256,256]{2,1,0:T(8,128)(2,1)S(1)} %fusion.10), channel_id=1, source_target_pairs={{0,4},{1,5},{4,8},{5,9},{8,12},{9,13},{12,14},{13,15},{14,10},{15,... | collective-permute-start | bytes 786440 | tf_op jit(solution)/shard_map/ppermute | solution.py:121
  113.9 11.0 %collective-permute-start.26 = (f16[1,256,256]{2,1,0:T(8,128)(2,1)S(1)}, f16[1,256,256]{2,1,0:T(8,128)(2,1)S(1)}, u32[]{:S(2)}, u32[]{:S(2)}) collective-permute-start(f16[1,256,256]{2,1,0:T(8,128)(2,1)S(1)} %get-tuple-element.15), channel_id=1, source_target_pairs={{0,2},{1,3},{4,0},{5,1},{8,4},{9,5},{12,8},{13,9},{14,12},{15,13},... | collective-permute-start | bytes 393224 | tf_op jit(solution)/shard_map/ppermute | solution.py:124
  121.3 6.4 %collective-permute-start.24 = (f16[2,256,256]{2,1,0:T(8,128)(2,1)S(1)}, f16[2,256,256]{2,1,0:T(8,128)(2,1)S(1)}, u32[]{:S(2)}, u32[]{:S(2)}) collective-permute-start(f16[2,256,256]{2,1,0:T(8,128)(2,1)S(1)} %fusion.12), channel_id=1, source_target_pairs={{0,4},{1,5},{4,8},{5,9},{8,12},{9,13},{12,14},{13,15},{14,10},{15,... | collective-permute-start | bytes 786440 | tf_op jit(solution)/shard_map/ppermute | solution.py:121
  129.1 6.4 %collective-permute-start.27 = (f16[2,256,256]{2,1,0:T(8,128)(2,1)S(1)}, f16[2,256,256]{2,1,0:T(8,128)(2,1)S(1)}, u32[]{:S(2)}, u32[]{:S(2)}) collective-permute-start(f16[2,256,256]{2,1,0:T(8,128)(2,1)S(1)} %get-tuple-element.13), channel_id=1, source_target_pairs={{0,2},{1,3},{4,0},{5,1},{8,4},{9,5},{12,8},{13,9},{14,12},{15,13},... | collective-permute-start | bytes 786440 | tf_op jit(solution)/shard_map/ppermute | solution.py:124
  131.9 5.4 %collective-permute-start.30 = (f32[2]{0:T(128)S(1)}, f32[2]{0:T(128)S(1)}, u32[]{:S(2)}, u32[]{:S(2)}) collective-permute-start(f32[2]{0:T(128)S(1)} %pad_maximum_fusion.3), channel_id=1, source_target_pairs={{0,1},{1,0},{2,3},{3,2},{4,5},{5,4},{6,7},{7,6},{8,9},{9,8},{10,11... | collective-permute-start | bytes 32 | tf_op jit(solution)/shard_map/ppermute | solution.py:133
  136.7 10.7 %collective-permute-start.28 = (f16[2,256,256]{2,1,0:T(8,128)(2,1)S(1)}, f16[2,256,256]{2,1,0:T(8,128)(2,1)S(1)}, u32[]{:S(2)}, u32[]{:S(2)}) collective-permute-start(f16[2,256,256]{2,1,0:T(8,128)(2,1)S(1)} %fusion.6), channel_id=1, source_target_pairs={{0,2},{1,3},{4,0},{5,1},{8,4},{9,5},{12,8},{13,9},{14,12},{15,13},... | collective-permute-start | bytes 786440 | tf_op jit(solution)/shard_map/ppermute | solution.py:124
  140.4 3.5 %collective-permute-start.31 = (f32[2]{0:T(128)S(1)}, f32[2]{0:T(128)S(1)}, u32[]{:S(2)}, u32[]{:S(2)}) collective-permute-start(f32[2]{0:T(128)S(1)} %pad_maximum_fusion.4), channel_id=1, source_target_pairs={{0,2},{1,3},{2,0},{3,1},{4,6},{5,7},{6,4},{7,5},{8,10},{9,11},{10,... | collective-permute-start | bytes 32 | tf_op jit(solution)/shard_map/ppermute | solution.py:133
  145.9 16.4 %collective-permute-start.25 = (f16[2,256,256]{2,1,0:T(8,128)(2,1)S(1)}, f16[2,256,256]{2,1,0:T(8,128)(2,1)S(1)}, u32[]{:S(2)}, u32[]{:S(2)}) collective-permute-start(f16[2,256,256]{2,1,0:T(8,128)(2,1)S(1)} %get-tuple-element.12), channel_id=1, source_target_pairs={{0,4},{1,5},{4,8},{5,9},{8,12},{9,13},{12,14},{13,15},{14,10},{15,... | collective-permute-start | bytes 786440 | tf_op jit(solution)/shard_map/ppermute | solution.py:121
  148.6 13.7 %collective-permute-start.29 = (f16[2,256,256]{2,1,0:T(8,128)(2,1)S(1)}, f16[2,256,256]{2,1,0:T(8,128)(2,1)S(1)}, u32[]{:S(2)}, u32[]{:S(2)}) collective-permute-start(f16[2,256,256]{2,1,0:T(8,128)(2,1)S(1)} %fusion.8), channel_id=1, source_target_pairs={{0,2},{1,3},{4,0},{5,1},{8,4},{9,5},{12,8},{13,9},{14,12},{15,13},... | collective-permute-start | bytes 786440 | tf_op jit(solution)/shard_map/ppermute | solution.py:124
  149.2 5.9 %collective-permute-start.32 = (f32[2]{0:T(128)S(1)}, f32[2]{0:T(128)S(1)}, u32[]{:S(2)}, u32[]{:S(2)}) collective-permute-start(f32[2]{0:T(128)S(1)} %pad_maximum_fusion.5), channel_id=1, source_target_pairs={{0,4},{1,5},{2,6},{3,7},{4,0},{5,1},{6,2},{7,3},{8,12},{9,13},{10,... | collective-permute-start | bytes 32 | tf_op jit(solution)/shard_map/ppermute | solution.py:133
  157.0 4.4 %collective-permute-start.33 = (f32[2]{0:T(128)S(1)}, f32[2]{0:T(128)S(1)}, u32[]{:S(2)}, u32[]{:S(2)}) collective-permute-start(f32[2]{0:T(128)S(1)} %pad_maximum_fusion.6), channel_id=1, source_target_pairs={{0,8},{1,9},{2,10},{3,11},{4,12},{5,13},{6,14},{7,15},{8,0},{9,1},... | collective-permute-start | bytes 32 | tf_op jit(solution)/shard_map/ppermute | solution.py:133

commit v2 on v0

v2 whole, which is shorter than its diff:
```python
import functools

import jax
import jax.numpy as jnp
from jax import lax
from jax.experimental import pallas as pl
from jax.experimental.pallas import tpu as pltpu
from jax.sharding import PartitionSpec as P

shift_energy = 2.0
CORES = 2
BATCH = 8
KEEP = pl.BlockSpec(memory_space=pltpu.VMEM)
SCALAR = pl.BlockSpec(memory_space=pltpu.SMEM)
INHBM = pl.BlockSpec(memory_space=pltpu.HBM)
ANYWHERE = pl.BlockSpec(memory_space=pl.ANY)


def ring_of(mesh):
    chips = mesh.shape["sector"] // CORES
    rows = 2 if mesh.shape["groups"] == 2 else 1
    cols = chips // rows
    order = [z * rows for z in range(cols)]
    for y in range(1, rows):
        order += [z * rows + y for z in reversed(range(cols))]
    return order


def over(x, n):
    return lax.shift_right_logical(x, n.bit_length() - 1) if n & (n - 1) == 0 else lax.div(x, n)


def left_over(x, n):
    return x & (n - 1) if n & (n - 1) == 0 else lax.rem(x, n)


def starts_of(pieces, psi, starts, sems):
    copies = [
        pltpu.make_async_copy(piece, psi.at[pl.ds(start, piece.shape[0])], sems.at[n])
        for n, (piece, start) in enumerate(zip(pieces, starts))
    ]
    for copy in copies:
        copy.start()
    return copies


def top(ref, start, count, m):
    def body(k, m):
        for row in range(0, ref.shape[1], m.shape[0]):
            m = jnp.maximum(m, jnp.abs(ref[start + k, row : row + m.shape[0], :]))
        return m

    return lax.fori_loop(0, count, body, m)


def batch_of_terms(i, plan_ref, left, right, psi, acc, room=()):
    codes = [plan_ref[i * BATCH + u] for u in range(BATCH)]
    ks = [over(c, 65536) for c in codes]
    if room:
        held, sems = room
        copies = [pltpu.make_async_copy(right.at[k], held.at[u], sems.at[u]) for u, k in enumerate(ks)]
        for copy in copies:
            copy.start()
        for copy in copies:
            copy.wait()
        ks, right = list(zip(ks, range(BATCH))), held
    else:
        ks = list(zip(ks, ks))
    halves = [
        jnp.dot(left[k], psi[left_over(over(c, 256), 256)], preferred_element_type=jnp.float32).astype(jnp.bfloat16)
        for (k, _), c in zip(ks, codes)
    ]
    whole = [jnp.dot(h, right[k], preferred_element_type=jnp.float32) for (_, k), h in zip(ks, halves)]
    for c, w in zip(codes, whole):
        acc[left_over(c, 256)] += w


def plan_kernel(
    shape, tl_hbm, me_ref, left_hbm, psi_hbm, lower_hbm,
    left, vec, acc, psi, plan, bounds, tl_ref, psi_ref, lower_ref, codes, kinds, fill, sems, small_sems,
):
    chips, rows_y, per, cap, empty = shape
    terms, side, _ = left.shape
    lower = lower_ref.shape[0]
    reach = chips // 2
    group = terms // sems.shape[0]
    small = [
        pltpu.make_async_copy(a, b, small_sems.at[n])
        for n, (a, b) in enumerate(((tl_hbm, tl_ref), (psi_hbm, psi_ref), (lower_hbm, lower_ref)))
    ]
    copies = [
        pltpu.make_async_copy(left_hbm.at[pl.ds(g * group, group)], left.at[pl.ds(g * group, group)], sems.at[g])
        for g in range(sems.shape[0])
    ]
    for copy in small + copies:
        copy.start()
    small[0].wait()

    def place(chip):
        if rows_y == 1:
            return chip
        z, y = over(chip, rows_y), left_over(chip, rows_y)
        return jnp.where(y == 0, z, chips - 1 - z)

    me = me_ref[0]
    my_place, my_core = place(over(me, CORES)), left_over(me, CORES)

    def slot(sector):
        chip, core, j = over(sector, per * CORES), left_over(over(sector, per), CORES), left_over(sector, per)
        rel = left_over(place(chip) - my_place + chips, chips)
        return rel, jnp.where(core == my_core, 0, chips * per) + rel * per + j

    for stage in range(reach + 1):
        fill[stage] = 0

    def classify(k, carry):
        rel, src = slot(tl_ref[0, k])
        _, dst = slot(tl_ref[1, k])
        stage = jnp.minimum(rel, chips - rel)
        stage = jnp.where(stage == 1, 2, stage)
        codes[k] = k * 65536 + src * 256 + dst
        kinds[k] = stage
        fill[stage] += 1
        return carry

    lax.fori_loop(0, terms, classify, 0, unroll=4)
    at = jnp.int32(0)
    for stage in range(reach + 1):
        bounds[stage] = at
        count = fill[stage]
        fill[stage] = at * BATCH
        at = at + over(count + (BATCH - 1), BATCH)
    bounds[reach + 1] = at

    def put(k, carry):
        stage = kinds[k]
        plan[fill[stage]] = codes[k]
        fill[stage] += 1
        return carry

    lax.fori_loop(0, terms, put, 0, unroll=4)

    for stage in range(reach + 1):

        def pad(i, carry):
            before = plan[i - 1]
            plan[i] = before - left_over(before, 256) + empty
            return carry

        lax.fori_loop(fill[stage], bounds[stage + 1] * BATCH, pad, 0)

    def zero(i, carry):
        acc[i] = jnp.zeros((side, side), jnp.float32)
        return carry

    lax.fori_loop(0, acc.shape[0], zero, 0)

    def fold(x):
        x = jnp.sum(x.reshape(-1, 8, side), axis=0)
        return jnp.sum(x, axis=0, keepdims=True)

    def rows(j):
        psi = psi_ref[j].astype(jnp.float32)
        low = [lower_ref[i, j].astype(jnp.float32) for i in range(lower)]
        return [fold(x * psi) for x in low] + [fold(x * x) for x in low] + [fold(psi * psi)]

    small[1].wait()
    small[2].wait()
    parts = rows(0)
    for j in range(1, psi_ref.shape[0]):
        parts = [a + b for a, b in zip(parts, rows(j))]
    psi[0, 0:16] = jnp.zeros((16, side), psi.dtype)
    vec[...] = jnp.zeros_like(vec)
    for i, x in enumerate(parts):
        vec[pl.ds(i, 1), :] = sum(x[:, c : c + 128] for c in range(0, side, 128))

    for copy in copies:
        copy.wait()


def first_kernel(starts, empty, plan_ref, bounds_ref, left_ref, right_hbm, *rest):
    count = len(starts)
    pieces, rest = rest[:count], rest[count:]
    _, _, acc, psi, right, sems, right_sems = rest

    def brought(i):
        code = plan_ref[i]
        k = over(code, 65536)
        return left_over(code, 256) != empty, pltpu.make_async_copy(right_hbm.at[k], right.at[k], right_sems.at[k])

    def start(i, carry):
        real, copy = brought(i)

        @pl.when(real)
        def _():
            copy.start()

        return carry

    def wait(i, carry):
        real, copy = brought(i)

        @pl.when(real)
        def _():
            copy.wait()

        return carry

    copies = starts_of(pieces, psi, starts, sems)
    end = bounds_ref[bounds_ref.shape[0] - 1]
    lax.fori_loop(0, end * BATCH, start, 0)
    for copy in copies:
        copy.wait()

    def batch(i, carry):
        lax.fori_loop(i * BATCH, (i + 1) * BATCH, wait, 0)
        batch_of_terms(i, plan_ref, left_ref, right, psi, acc)
        return carry

    lax.fori_loop(0, bounds_ref[1], batch, 0)
    lax.fori_loop(bounds_ref[1] * BATCH, end * BATCH, wait, 0)


def stage_kernel(stage, starts, finish, limit, plan_ref, bounds_ref, left_ref, right_ref, *rest):
    count = len(starts)
    pieces, rest = rest[:count], rest[count:]
    if finish:
        vec_ref, _, _, acc, psi = rest[:5]
        outs, rest = rest[5 : 7 + len(finish)], rest[7 + len(finish) :]
        out_sems, rest = rest[0], rest[1:]
    else:
        _, _, acc, psi, *rest = rest
    sems, *room = rest
    copies = starts_of(pieces, psi, starts, sems)
    for copy in copies:
        copy.wait()

    def batch(i, carry):
        batch_of_terms(i, plan_ref, left_ref, right_ref, psi, acc, room)
        return carry

    lax.fori_loop(bounds_ref[stage], bounds_ref[stage + 1], batch, 0)
    if finish:
        outs, vec, scales = outs[:-2], outs[-2], outs[-1]
        moves = []
        for out, chunks in zip(outs, finish):
            put = 0
            for begin, size in chunks:
                place = out.at[pl.ds(put, size)]
                moves.append(pltpu.make_async_copy(acc.at[pl.ds(begin, size)], place, out_sems.at[len(moves)]))
                put += size
        for move in moves:
            move.start()
        side = psi.shape[1]

        def add(s, total):
            for row in range(0, side, 32):
                total += acc[s, row : row + 32, :] * psi[s, row : row + 32, :].astype(jnp.float32)
            return total

        total = lax.fori_loop(0, psi.shape[0], add, jnp.zeros((32, side), jnp.float32))
        total = jnp.sum(total, axis=0, keepdims=True)
        vec[...] = vec_ref[...]
        vec[pl.ds(vec.shape[0] - 1, 1), :] = sum(total[:, c : c + 128] for c in range(0, side, 128))
        largest = jnp.max(top(psi, 0, psi.shape[0], jnp.zeros((16, side), psi.dtype)).astype(jnp.float32))
        bound = jnp.full((1, 128), limit * largest)
        power = jnp.clip(15.0 - jnp.ceil(jnp.log2(jnp.maximum(bound, 1e-30))), -60.0, 90.0)
        scales[...] = jnp.zeros_like(scales)
        scales[0:1, :] = jnp.exp2(power)
        scales[1:2, :] = 1.0 / jnp.exp2(power)
        for move in moves:
            move.wait()


def make_per_device(mesh):
    devices = mesh.shape["sector"]
    ring = ring_of(mesh)
    chips = len(ring)
    reach = chips // 2
    rows_y = 2 if mesh.shape["groups"] == 2 else 1

    def shift(by):
        return [
            (ring[p] * CORES + c, ring[(p + by) % chips] * CORES + c) for p in range(chips) for c in range(CORES)
        ]

    to_right, to_left = shift(1), shift(-1)

    def right(x):
        return lax.ppermute(x, "sector", to_right)

    def left(x):
        return lax.ppermute(x, "sector", to_left)

    def pair(x, hop):
        return lax.ppermute(x, "sector", [(i, i ^ hop) for i in range(devices)])

    def across(x):
        return pair(x, 1)

    bits = [1 << b for b in range(devices.bit_length() - 1)]

    def per_device(wavefunction, lower_states, left_env, right_env, term_list):
        per, side, _ = wavefunction.shape
        terms = left_env.shape[0]
        sectors = per * devices
        part = per // 2
        lower = lower_states.shape[0]
        base = chips * per
        tie = lax.optimization_barrier
        me = lax.axis_index("sector")

        keep = dict(compiler_params=pltpu.CompilerParams(vmem_limit_bytes=8 * 1024 * 1024))
        stages = reach + 1
        cap = (terms + stages * (BATCH - 1) + BATCH - 1) // BATCH * BATCH
        groups = next(g for g in (4, 2, 1) if terms % g == 0)
        vec_rows = -(-(2 * lower + 2) // 8) * 8
        roomy = sectors * side * side * 4 <= 9 << 20
        left_hbm, right_hbm, psi_hbm, lower_hbm, list_hbm = [
            pltpu.with_memory_space_constraint(x, pltpu.HBM)
            for x in (left_env, right_env, wavefunction, lower_states, term_list.T)
        ]
        vec_shape = jax.ShapeDtypeStruct((vec_rows, 128), jnp.float32)
        acc_shape = pltpu.VMEM((sectors + 1, side, side), jnp.float32)
        psi_shape = pltpu.VMEM((sectors, side, side), wavefunction.dtype)

        def make_plan():
            return pl.pallas_call(
                functools.partial(plan_kernel, (chips, rows_y, per, cap, sectors)),
                in_specs=[INHBM, SCALAR, INHBM, INHBM, INHBM],
                out_specs=[KEEP] * 4 + [SCALAR] * 2,
                out_shape=[
                    pltpu.VMEM(left_env.shape, left_env.dtype),
                    vec_shape,
                    acc_shape,
                    psi_shape,
                    jax.ShapeDtypeStruct((cap,), jnp.int32),
                    jax.ShapeDtypeStruct((stages + 1,), jnp.int32),
                ],
                scratch_shapes=[
                    pltpu.SMEM((2, terms), jnp.int32),
                    pltpu.VMEM(wavefunction.shape, wavefunction.dtype),
                    pltpu.VMEM(lower_states.shape, lower_states.dtype),
                    pltpu.SMEM((terms,), jnp.int32),
                    pltpu.SMEM((terms,), jnp.int32),
                    pltpu.SMEM((stages,), jnp.int32),
                    pltpu.SemaphoreType.DMA((groups,)),
                    pltpu.SemaphoreType.DMA((3,)),
                ],
                cost_estimate=pl.CostEstimate(flops=0, bytes_accessed=12 << 20, transcendentals=0),
                **keep,
            )(list_hbm, me.reshape(1).astype(jnp.int32), left_hbm, psi_hbm, lower_hbm)

        def run_first(pieces, starts, acc, psi):
            n = len(pieces)
            return pl.pallas_call(
                functools.partial(first_kernel, starts, sectors),
                in_specs=[SCALAR, SCALAR, KEEP, INHBM] + [ANYWHERE] * n + [KEEP] * 2,
                out_specs=[KEEP] * 3,
                out_shape=[acc_shape, psi_shape, pltpu.VMEM(right_env.shape, right_env.dtype)],
                input_output_aliases={4 + n: 0, 5 + n: 1},
                scratch_shapes=[pltpu.SemaphoreType.DMA((n,)), pltpu.SemaphoreType.DMA((terms,))],
                cost_estimate=pl.CostEstimate(flops=0, bytes_accessed=12 << 20, transcendentals=0),
                **keep,
            )(plan, bounds, left_vmem, right_hbm, *pieces, acc, psi)

        sets = [[reach], [reach - 1, 1 - reach], [x for s in range(reach - 2, 0, -1) for x in (s, -s)] + [0]]

        def run_stage(stage, pieces, starts, acc, psi, vec=None):
            finish, sizes, more, small = [], [], [], []
            if stage == reach:
                finish = [[(base + rel % chips * per, per) for rel in rels] for rels in sets]
                shape_of = pltpu.VMEM if roomy else jax.ShapeDtypeStruct
                sizes = [shape_of((per * len(rels), side, side), jnp.float32) for rels in sets]
                more, small = [vec], [vec_shape, jax.ShapeDtypeStruct((8, 128), jnp.float32)]
            n, m = len(pieces), len(more)
            scratch = [pltpu.SemaphoreType.DMA((n,))]
            if finish:
                scratch = [pltpu.SemaphoreType.DMA((chips,))] + scratch
            if not roomy:
                scratch += [pltpu.VMEM((BATCH, side, side), right_env.dtype), pltpu.SemaphoreType.DMA((BATCH,))]
            limit = 1.02 * terms * devices * side * side * 0.375 * 0.0546875
            return pl.pallas_call(
                functools.partial(stage_kernel, stage, starts, finish, limit),
                in_specs=[SCALAR, SCALAR, KEEP, KEEP if roomy else INHBM] + [ANYWHERE] * n + [KEEP] * (m + 2),
                out_specs=[KEEP] * 2 + [KEEP if roomy else ANYWHERE] * len(sizes) + [KEEP] * len(small),
                out_shape=[acc_shape, psi_shape] + sizes + small,
                input_output_aliases={4 + n + m: 0, 5 + n + m: 1},
                scratch_shapes=scratch,
                cost_estimate=pl.CostEstimate(
                    flops=4 * side**3 * terms // stages, bytes_accessed=1 << 20, transcendentals=0
                ),
                **keep,
            )(plan, bounds, left_vmem, right_vmem, *pieces, *more, acc, psi)

        r, l, sib = right(wavefunction), left(wavefunction), across(wavefunction)
        left_vmem, vec, acc, psi, plan, bounds = make_plan()
        held, at = [], []
        for s in range(1, reach):
            r, l, acc, psi = tie((r, l, acc, psi))
            rel = [(chips - s) * per, s * per]
            held, at = held + [r, l, across(r), across(l)], at + rel + [base + x for x in rel]
            if s < reach - 1:
                r, l = right(r), left(l)
            else:
                r, l = right(r[:part]), left(l[part:])
            if s == 1 and roomy:
                acc, psi, right_vmem = run_first([wavefunction, sib], [0, base], acc, psi)
            elif s == 1:
                right_vmem = right_hbm
                acc, psi = run_stage(0, [wavefunction, sib], [0, base], acc, psi)
            else:
                acc, psi = run_stage(s, held, at, acc, psi)
                held, at = [], []
        r, l, acc, psi = tie((r, l, acc, psi))
        rel = [reach * per, reach * per + part]
        held, at = held + [r, l, across(r), across(l)], at + rel + [base + x for x in rel]
        acc, psi, *others, vec, scales = run_stage(reach, held, at, acc, psi, vec)
        scale, unscale = scales[0, 0], scales[1, 0]

        got = [across(x) for x in others[:-1]]
        *got, late = tie((*got, others[-1]))
        got.append(across(late))

        def pack(x):
            return (x * scale).astype(jnp.float16)

        def unpack(x):
            return x.astype(jnp.float32) * unscale

        halves = (slice(0, part), slice(part, per))

        def own(rel, half):
            part_of, at = next((n, rels.index(rel)) for n, rels in enumerate(sets) if rel in rels)
            begin = rel % chips * per
            return acc[begin : begin + per][halves[half]] + got[part_of][at * per : (at + 1) * per][halves[half]]

        hops, flying = list(bits), None
        route = [(reach, 0)] + [(d, h) for d in range(reach - 1, 0, -1) for h in (1, 0)]
        went, sent = [], []
        for n, (d, h) in enumerate(route):
            to_r, to_l = own(d, h), own(-d if d < reach else reach, 1 - h)
            if n >= 2:
                back, _ = tie((went[n - 2], sent[n - 1]))
                to_r, to_l = to_r + unpack(back[0]), to_l + unpack(back[1])
            sent.append((pack(to_r), pack(to_l)))
            went.append((right(sent[n][0]), left(sent[n][1])))
            if n % 2 == 0 and hops:
                if flying is not None:
                    flying, _ = tie((flying, sent[n]))
                    vec = vec + flying
                flying = pair(vec, hops.pop(0))
        if flying is not None:
            flying, _ = tie((flying, sent[-1]))
            vec = vec + flying
        for hop in hops:
            vec = vec + pair(vec, hop)
        sums = jnp.sum(vec, axis=1)
        correlation, own_norm, psi_norm = sums[:lower], sums[lower : 2 * lower], sums[2 * lower]
        coeffs = correlation / own_norm
        psi_local = wavefunction.astype(jnp.float32)
        lower_local = lower_states.astype(jnp.float32)
        ritz_value = (sums[-1] + shift_energy * jnp.sum(coeffs * correlation)) / psi_norm
        rest = jnp.concatenate([own(0, 0), own(0, 1)])
        rest = rest + shift_energy * jnp.sum(coeffs[:, None, None, None] * lower_local, axis=0)
        (r1, l0), (r0, l1) = went[-2], went[-1]
        arrived = jnp.concatenate([unpack(r0) + unpack(l0), unpack(r1) + unpack(l1)])
        residual = rest + arrived - ritz_value * psi_local
        return (residual, ritz_value.reshape(1))

    return per_device


def solution(mesh):
    return jax.shard_map(
        make_per_device(mesh),
        mesh=mesh,
        in_specs=(
            P(("groups", "sector"), None, None),
            P(None, ("groups", "sector"), None, None),
            P(("groups", "sector"), None, None),
            P(("groups", "sector"), None, None),
            P(("groups", "sector"), None),
        ),
        out_specs=(P(("groups", "sector"), None, None), P("groups")),
        check_vma=False,
    )
```

time: 303 us -> 87.5 us (0.29)
  waiting for transfers between devices: 159 us -> 14.9 us
  other arithmetic: 60 us -> 11.3 us
  blocking collectives: 32.8 us -> 0 us
  starting transfers between devices: 0.08 us -> 30.3 us
  Pallas kernels: 0 us -> 25.9 us
  matrix products: 20.5 us -> 0 us
  between operations: 17.2 us -> 3.9 us
  local copies, waits for them, and re-layouts: 13.2 us -> 1.2 us
    reduce_scatter x1 -> x0, waiting for transfers between devices: 103 us -> none  [per_device(): lax.psum_scatter(partial_sigma, 'sector', scatter_dimension=0, tiled=True)]
    all_gather x1 -> x0, waiting for transfers between devices: 54.7 us -> none  [per_device(): gathered = lax.all_gather(wavefunction, 'sector', axis=0, tiled=True)]
    scatter-add x1 -> x0, other arithmetic: 54.1 us -> none  [per_device(): partial_sigma = jax.ops.segment_sum(contrib, targets, num_segments=sectors)]
    psum x1 -> x0, blocking collectives: 32.8 us -> none  [per_device(): lax.psum((correlation_part, own_part, norm_part), 'sector')]
    ppermute x0 -> x38, starting transfers between devices: none -> 30.3 us  [the longest x11 16.2 us: left(): return lax.ppermute(x, 'sector', to_left)]
    pallas_call x0 -> x5, Pallas kernels: none -> 25.9 us  [the longest x3 14.4 us: run_stage(): pl.pallas_call(functools.partial(stage_kernel, stage, starts, finish, lim...]
    dot_general x1 -> x0, matrix products: 20.5 us -> none  [per_device(): jnp.einsum('kab,kbc->kac', half_block, right_env, preferred_element_type=...]
    ppermute x0 -> x38, waiting for transfers between devices: none -> 14.9 us  [the longest x11 8 us: right(): return lax.ppermute(x, 'sector', to_right)]
  transfers between devices with their start and end apart: 2 -> 38, of which waited for: 2 -> 14; matrix products, arithmetic and copies ran while one was open for 0% -> 12% of each run, Pallas kernels for 0% -> 23%
where the time goes in v2:
time: 87.5 us; the launch traced here: 87.4 us
  starting transfers between devices  30.3 us (35%)
  Pallas kernels  25.9 us (30%)
  waiting for transfers between devices  14.9 us (17%)
  other arithmetic  11.3 us (13%)
  between operations  3.9 us (4%)
  local copies, waits for them, and re-layouts  1.2 us (1%)
    ppermute x11, starting transfers between devices, left(): return lax.ppermute(x, 'sector', to_left)  16.2 us
    pallas_call x3, Pallas kernels, run_stage(): pl.pallas_call(functools.partial(stage_kernel, stage, starts, finish, lim...  14.4 us
    ppermute x11, waiting for transfers between devices, right(): return lax.ppermute(x, 'sector', to_right)  8 us
    convert_element_type x6, other arithmetic, pack(): return (x * scale).astype(jnp.float16)  7.97 us
    ppermute x11, starting transfers between devices, right(): return lax.ppermute(x, 'sector', to_right)  7.25 us
    ppermute x16, starting transfers between devices, pair(): return lax.ppermute(x, 'sector', [(i, i ^ hop) for i in range(devices)])  6.8 us
    pallas_call x1, Pallas kernels, run_first(): pl.pallas_call(functools.partial(first_kernel, starts, sectors), in_specs...  6.03 us
    pallas_call x1, Pallas kernels, make_plan(): pl.pallas_call(functools.partial(plan_kernel, (chips, rows_y, per, cap, s...  5.47 us
  transfers between devices with their start and end apart: 38, of which 14 were waited for; matrix products, arithmetic and copies ran while one was open for 12% of the time, Pallas kernels for 23%

profile of v2, /device:TPU:0, one launch (start us, length us, event | category | flops | bytes accessed | tf_op | source)
XLA Modules:
  0.0 87.4 jit_solution(12629184689276260292)
XLA Ops:
  0.6 3.0 %collective-permute-start.2 = (bf16[2,256,256]{2,1,0:T(8,128)(2,1)}, bf16[2,256,256]{2,1,0:T(8,128)(2,1)S(1)}, u32[]{:S(2)}, u32[]{:S(2)}) collective-permute-start(bf16[2,256,256]{2,1,0:T(8,128)(2,1)} %rest_0_.1), channel_id=1, source_target_pairs={{0,2},{1,3},{4,0},{5,1},{8,4},{9,5},{12,8},{13,9},{14,12},{15,13},... | collective-permute-start | bytes 786440 | tf_op jit(solution)/shard_map/ppermute | solution.py:293
  3.7 0.1 collective-permute-start.1
  3.8 5.5 %shard_map.68 = (bf16[92,256,256]{2,1,0:T(8,128)(2,1)S(1)}, f32[8,128]{1,0:T(8,128)S(1)}, f32[33,256,256]{2,1,0:T(8,128)S(1)}, bf16[32,256,256]{2,1,0:T(8,128)(2,1)S(1)}, s32[128]{0:T(128)S(1)}, /*index=5*/s32[6]{0:T(128)S(1)}) custom-call(s32[2,92]{1,0:T(2,128)} %bitcast.7, s32[1]{0:T(128)} %bitcast.1.me_ref, bf16[92,256,256]{2,1,0:T(8,128)(2,1)} %left_hbm.1, ...), custom_call_target="tpu_custom_call" | custom-call | bytes 12582912 | tf_op jit(solution)/shard_map/pallas_call | solution.py:328
  9.3 1.0 %collective-permute-done.2.rest_1_ = bf16[2,256,256]{2,1,0:T(8,128)(2,1)S(1)} collective-permute-done((bf16[2,256,256]{2,1,0:T(8,128)(2,1)}, bf16[2,256,256]{2,1,0:T(8,128)(2,1)S(1)}, u32[]{:S(2)}, u32[]{:S(2)}) %collective-permute-start.2) | collective-permute-done | bytes 262176 | tf_op jit(solution)/shard_map/ppermute | solution.py:293
  10.2 1.4 %collective-permute-done.1.rest_0_ = bf16[2,256,256]{2,1,0:T(8,128)(2,1)S(1)} collective-permute-done((bf16[2,256,256]{2,1,0:T(8,128)(2,1)}, bf16[2,256,256]{2,1,0:T(8,128)(2,1)S(1)}, u32[]{:S(2)}, u32[]{:S(2)}) %collective-permute-start.1) | collective-permute-done | bytes 262176 | tf_op jit(solution)/shard_map/ppermute | solution.py:290
  11.6 0.4 collective-permute-start.3
  12.0 1.6 %collective-permute-start.4 = (bf16[2,256,256]{2,1,0:T(8,128)(2,1)S(1)}, bf16[2,256,256]{2,1,0:T(8,128)(2,1)S(1)}, u32[]{:S(2)}, u32[]{:S(2)}) collective-permute-start(bf16[2,256,256]{2,1,0:T(8,128)(2,1)S(1)} %collective-permute-done.2.rest_1_), channel_id=1, source_target_pairs={{0,2},{1,3},{4,0},{5,1},{8,4},{9,5},{12,8},{13,9},{14,12},{15,13},... | collective-permute-start | bytes 786440 | tf_op jit(solution)/shard_map/ppermute | solution.py:293
  13.7 0.5 collective-permute-start.8
  14.2 6.0 %shard_map.69 = (f32[33,256,256]{2,1,0:T(8,128)S(1)}, bf16[32,256,256]{2,1,0:T(8,128)(2,1)S(1)}, bf16[92,256,256]{2,1,0:T(8,128)(2,1)S(1)}) custom-call(s32[128]{0:T(128)S(1)} %get-tuple-element.54.plan_ref, s32[6]{0:T(128)S(1)} %get-tuple-element.55.bounds_ref, ...), custom_call_target="tpu_custom_call", output_to_operand_aliasing={{0}: (6, {}), {1}: (7, {})} | custom-call | bytes 12582912 | tf_op jit(solution)/shard_map/pallas_call | solution.py:356
  20.2 0.1 collective-permute-start.9
  20.3 0.5 collective-permute-start.10
  20.8 1.0 %collective-permute-start.5 = (bf16[2,256,256]{2,1,0:T(8,128)(2,1)S(1)}, bf16[2,256,256]{2,1,0:T(8,128)(2,1)S(1)}, u32[]{:S(2)}, u32[]{:S(2)}) collective-permute-start(bf16[2,256,256]{2,1,0:T(8,128)(2,1)S(1)} %collective-permute-done.3.rest_4_), channel_id=1, source_target_pairs={{0,4},{1,5},{4,8},{5,9},{8,12},{9,13},{12,14},{13,15},{14,10},{15,... | collective-permute-start | bytes 786440 | tf_op jit(solution)/shard_map/ppermute | solution.py:290
  21.8 1.0 %collective-permute-start.6 = (bf16[2,256,256]{2,1,0:T(8,128)(2,1)S(1)}, bf16[2,256,256]{2,1,0:T(8,128)(2,1)S(1)}, u32[]{:S(2)}, u32[]{:S(2)}) collective-permute-start(bf16[2,256,256]{2,1,0:T(8,128)(2,1)S(1)} %collective-permute-done.4.rest_5_), channel_id=1, source_target_pairs={{0,2},{1,3},{4,0},{5,1},{8,4},{9,5},{12,8},{13,9},{14,12},{15,13},... | collective-permute-start | bytes 786440 | tf_op jit(solution)/shard_map/ppermute | solution.py:293
  22.9 4.8 %shard_map.70 = (f32[33,256,256]{2,1,0:T(8,128)S(1)}, bf16[32,256,256]{2,1,0:T(8,128)(2,1)S(1)}) custom-call(s32[128]{0:T(128)S(1)} %get-tuple-element.54.plan_ref, s32[6]{0:T(128)S(1)} %get-tuple-element.55.bounds_ref, bf16[92,256,256]{2,1,0:T(8,128)(2,1)S(1)} %get-tuple-element.56.left_ref, ...), custom_call_target="tpu_custom_call", output_to_operand_aliasing={{0}: (12, {}), {1}: (13, {})} | custom-call | flops 1234803072 | bytes 1048576 | tf_op jit(solution)/shard_map/pallas_call | solution.py:383
  27.7 1.5 %collective-permute-done.5.rest_0_ = bf16[2,256,256]{2,1,0:T(8,128)(2,1)S(1)} collective-permute-done((bf16[2,256,256]{2,1,0:T(8,128)(2,1)S(1)}, bf16[2,256,256]{2,1,0:T(8,128)(2,1)S(1)}, u32[]{:S(2)}, u32[]{:S(2)}) %collective-permute-start.5) | collective-permute-done | bytes 262176 | tf_op jit(solution)/shard_map/ppermute | solution.py:290
  29.1 0.6 collective-permute-done.6.rest_1_
  29.8 0.5 collective-permute-start.14
  30.3 1.2 %collective-permute-start.12 = (bf16[1,256,256]{2,1,0:T(8,128)(2,1)S(1)}, bf16[1,256,256]{2,1,0:T(8,128)(2,1)S(1)}, u32[]{:S(2)}, u32[]{:S(2)}) collective-permute-start(bf16[1,256,256]{2,1,0:T(8,128)(2,1)S(1)} %slice.181), channel_id=1, source_target_pairs={{0,2},{1,3},{4,0},{5,1},{8,4},{9,5},{12,8},{13,9},{14,12},{15,13},... | collective-permute-start | bytes 393224 | tf_op jit(solution)/shard_map/ppermute | solution.py:293
  31.5 0.9 collective-permute-start.11
  32.4 3.9 %shard_map.71 = (f32[33,256,256]{2,1,0:T(8,128)S(1)}, bf16[32,256,256]{2,1,0:T(8,128)(2,1)S(1)}) custom-call(s32[128]{0:T(128)S(1)} %get-tuple-element.54.plan_ref, s32[6]{0:T(128)S(1)} %get-tuple-element.55.bounds_ref, bf16[92,256,256]{2,1,0:T(8,128)(2,1)S(1)} %get-tuple-element.56.left_ref, ...), custom_call_target="tpu_custom_call", output_to_operand_aliasing={{0}: (8, {}), {1}: (9, {})} | custom-call | flops 1234803072 | bytes 1048576 | tf_op jit(solution)/shard_map/pallas_call | solution.py:383
  36.3 0.6 collective-permute-done.11.rest_0_
  36.9 0.5 collective-permute-start.16
  37.4 0.8 collective-permute-done.15.rest_2_
  38.3 0.2 collective-permute-done.16.rest_3_
  38.5 5.8 %shard_map.72 = (f32[33,256,256]{2,1,0:T(8,128)S(1)}, bf16[32,256,256]{2,1,0:T(8,128)(2,1)S(1)}, f32[2,256,256]{2,1,0:T(8,128)S(1)}, f32[4,256,256]{2,1,0:T(8,12...) custom-call(s32[128]{0:T(128)S(1)} %get-tuple-element.54.plan_ref, ...), custom_call_target="tpu_custom_call", output_to_operand_aliasing={{0}: (9, {}), {1}: (10, {})} | custom-call | flops 1234803072 | bytes 1048576 | tf_op jit(solution)/shard_map/pallas_call | solution.py:383
  44.3 0.5 collective-permute-start.17
  44.8 2.9 %collective-permute-done.17 = f32[2,256,256]{2,1,0:T(8,128)S(1)} collective-permute-done((f32[2,256,256]{2,1,0:T(8,128)S(1)}, f32[2,256,256]{2,1,0:T(8,128)S(1)}, u32[]{:S(2)}, u32[]{:S(2)}) %collective-permute-start.17) | collective-permute-done | bytes 524320 | tf_op jit(solution)/shard_map/ppermute | solution.py:296
  47.7 0.1 collective-permute-start.19
  47.9 0.5 fusion.26
  48.4 0.8 multiply_convert_fusion.2
  49.2 0.4 collective-permute-start.21
  49.6 1.7 %collective-permute-start.22 = (f16[1,256,256]{2,1,0:T(8,128)(2,1)S(1)}, f16[1,256,256]{2,1,0:T(8,128)(2,1)S(1)}, u32[]{:S(2)}, u32[]{:S(2)}) collective-permute-start(f16[1,256,256]{2,1,0:T(8,128)(2,1)S(1)} %get-tuple-element.125), channel_id=1, source_target_pairs={{0,2},{1,3},{4,0},{5,1},{8,4},{9,5},{12,8},{13,9},{14,12},{15,13},... | collective-permute-start | bytes 393224 | tf_op jit(solution)/shard_map/ppermute | solution.py:293
  51.3 1.1 %collective-permute-start.27 = (f16[1,256,256]{2,1,0:T(8,128)(2,1)S(1)}, f16[1,256,256]{2,1,0:T(8,128)(2,1)S(1)}, u32[]{:S(2)}, u32[]{:S(2)}) collective-permute-start(f16[1,256,256]{2,1,0:T(8,128)(2,1)S(1)} %get-tuple-element.120), channel_id=1, source_target_pairs={{0,2},{1,3},{4,0},{5,1},{8,4},{9,5},{12,8},{13,9},{14,12},{15,13},... | collective-permute-start | bytes 393224 | tf_op jit(solution)/shard_map/ppermute | solution.py:293
  52.4 2.6 %collective-permute-done.21 = f16[1,256,256]{2,1,0:T(8,128)(2,1)S(1)} collective-permute-done((f16[1,256,256]{2,1,0:T(8,128)(2,1)S(1)}, f16[1,256,256]{2,1,0:T(8,128)(2,1)S(1)}, u32[]{:S(2)}, u32[]{:S(2)}) %collective-permute-start.21) | collective-permute-done | bytes 131104 | tf_op jit(solution)/shard_map/ppermute | solution.py:290
  55.0 0.3 collective-permute-start.26
  55.3 0.4 collective-permute-done.22
  55.8 1.4 %multiply_convert_fusion = (f16[1,256,256]{2,1,0:T(8,128)(2,1)S(1)}, f16[1,256,256]{2,1,0:T(8,128)(2,1)S(1)}) fusion(f16[1,256,256]{2,1,0:T(8,128)(2,1)S(1)} %collective-permute-done.22, f32[4,256,256]{2,1,0:T(8,128)S(1)} %collective-permute-done.18, f32[33,256,256]{2,1,0:T(8,128)S(1)} %get-tuple-element.83, f32[]{:T(128)} %bitcast.3, f32[]{:T(128)} %bitcast.2, ...), kind=kLoop, calls=%fused_computation.40 | loop fusion | flops 786432 | bytes 1572872 | tf_op jit(solution)/shard_map/convert_element_type | solution.py:426
  57.2 1.9 %collective-permute-start.25 = (f16[1,256,256]{2,1,0:T(8,128)(2,1)S(1)}, f16[1,256,256]{2,1,0:T(8,128)(2,1)S(1)}, u32[]{:S(2)}, u32[]{:S(2)}) collective-permute-start(f16[1,256,256]{2,1,0:T(8,128)(2,1)S(1)} %get-tuple-element.118), channel_id=1, source_target_pairs={{0,2},{1,3},{4,0},{5,1},{8,4},{9,5},{12,8},{13,9},{14,12},{15,13},... | collective-permute-start | bytes 393224 | tf_op jit(solution)/shard_map/ppermute | solution.py:293
  59.1 0.1 collective-permute-start.24
  59.3 1.9 %collective-permute-start.23 = (f32[8,128]{1,0:T(8,128)S(1)}, f32[8,128]{1,0:T(8,128)S(1)}, u32[]{:S(2)}, u32[]{:S(2)}) collective-permute-start(f32[8,128]{1,0:T(8,128)S(1)} %add.115), channel_id=1, source_target_pairs={{0,2},{1,3},{2,0},{3,1},{4,6},{5,7},{6,4},{7,5},{8,10},{9,11},{10,... | collective-permute-start | bytes 12296 | tf_op jit(solution)/shard_map/ppermute | solution.py:296
  61.2 1.4 %fusion.19 = (f16[1,256,256]{2,1,0:T(8,128)(2,1)S(1)}, f16[1,256,256]{2,1,0:T(8,128)(2,1)S(1)}) fusion(f32[10,256,256]{2,1,0:T(8,128)S(1)} %collective-permute-done.19, f16[1,256,256]{2,1,0:T(8,128)(2,1)S(1)} %collective-permute-done.27, f32[33,256,256]{2,1,0:T(8,128)S(1)} %get-tuple-element.83, f32[]{:T(128)} %bitcast.3, f32[]{:T(128)} %bitcast.2, ...), kind=kLoop, calls=%fused_computation.27 | loop fusion | flops 786432 | bytes 1572872 | tf_op jit(solution)/shard_map/convert_element_type | solution.py:426
  62.6 0.2 collective-permute-start.32
  62.8 1.9 %collective-permute-start.31 = (f16[1,256,256]{2,1,0:T(8,128)(2,1)S(1)}, f16[1,256,256]{2,1,0:T(8,128)(2,1)S(1)}, u32[]{:S(2)}, u32[]{:S(2)}) collective-permute-start(f16[1,256,256]{2,1,0:T(8,128)(2,1)S(1)} %get-tuple-element.117), channel_id=1, source_target_pairs={{0,4},{1,5},{4,8},{5,9},{8,12},{9,13},{12,14},{13,15},{14,10},{15,... | collective-permute-start | bytes 393224 | tf_op jit(solution)/shard_map/ppermute | solution.py:290
  64.7 0.4 collective-permute-done.24
  65.1 1.4 %fusion.16 = (f16[1,256,256]{2,1,0:T(8,128)(2,1)S(1)}, f16[1,256,256]{2,1,0:T(8,128)(2,1)S(1)}) fusion(f32[10,256,256]{2,1,0:T(8,128)S(1)} %collective-permute-done.19, f16[1,256,256]{2,1,0:T(8,128)(2,1)S(1)} %collective-permute-done.25, f32[33,256,256]{2,1,0:T(8,128)S(1)} %get-tuple-element.83, f32[]{:T(128)} %bitcast.3, f32[]{:T(128)} %bitcast.2, ...), kind=kLoop, calls=%fused_computation.23 | loop fusion | flops 786432 | bytes 1572872 | tf_op jit(solution)/shard_map/convert_element_type | solution.py:426
  66.5 0.9 %collective-permute-start.30 = (f16[1,256,256]{2,1,0:T(8,128)(2,1)S(1)}, f16[1,256,256]{2,1,0:T(8,128)(2,1)S(1)}, u32[]{:S(2)}, u32[]{:S(2)}) collective-permute-start(f16[1,256,256]{2,1,0:T(8,128)(2,1)S(1)} %get-tuple-element.114), channel_id=1, source_target_pairs={{0,2},{1,3},{4,0},{5,1},{8,4},{9,5},{12,8},{13,9},{14,12},{15,13},... | collective-permute-start | bytes 393224 | tf_op jit(solution)/shard_map/ppermute | solution.py:293
  67.4 1.2 %collective-permute-start.29 = (f16[1,256,256]{2,1,0:T(8,128)(2,1)S(1)}, f16[1,256,256]{2,1,0:T(8,128)(2,1)S(1)}, u32[]{:S(2)}, u32[]{:S(2)}) collective-permute-start(f16[1,256,256]{2,1,0:T(8,128)(2,1)S(1)} %get-tuple-element.115), channel_id=1, source_target_pairs={{0,4},{1,5},{4,8},{5,9},{8,12},{9,13},{12,14},{13,15},{14,10},{15,... | collective-permute-start | bytes 393224 | tf_op jit(solution)/shard_map/ppermute | solution.py:290
  68.6 0.7 collective-permute-start.28
  69.3 1.4 %fusion.7 = (f16[1,256,256]{2,1,0:T(8,128)(2,1)S(1)}, f16[1,256,256]{2,1,0:T(8,128)(2,1)S(1)}) fusion(f32[10,256,256]{2,1,0:T(8,128)S(1)} %collective-permute-done.19, f16[1,256,256]{2,1,0:T(8,128)(2,1)S(1)} %collective-permute-done.32, f32[33,256,256]{2,1,0:T(8,128)S(1)} %get-tuple-element.83, f32[]{:T(128)} %bitcast.3, f32[]{:T(128)} %bitcast.2, ...), kind=kLoop, calls=%fused_computation.11 | loop fusion | flops 786432 | bytes 1572872 | tf_op jit(solution)/shard_map/convert_element_type | solution.py:426
  70.7 0.8 collective-permute-done.30
  71.5 0.8 collective-permute-done.29
  72.4 1.5 %fusion.13 = (f16[1,256,256]{2,1,0:T(8,128)(2,1)S(1)}, f16[1,256,256]{2,1,0:T(8,128)(2,1)S(1)}, f32[1,256,256]{2,1,0:T(8,128)S(1)}, f32[1,256,256]{2,1,0:T(8,128)S(1)}) fusion(f32[10,256,256]{2,1,0:T(8,128)S(1)} %collective-permute-done.19, f16[1,256,256]{2,1,0:T(8,128)(2,1)S(1)} %collective-permute-done.29, f32[33,256,256]{2,1,0:T(8,128)S(1)} %get-tuple-element.83, ...), kind=kLoop, calls=%fused_computation.19 | loop fusion | flops 917504 | bytes 3145736 | tf_op jit(solution)/shard_map/convert_element_type | solution.py:426
  73.9 1.4 %collective-permute-start.33 = (f32[8,128]{1,0:T(8,128)S(1)}, f32[8,128]{1,0:T(8,128)S(1)}, u32[]{:S(2)}, u32[]{:S(2)}) collective-permute-start(f32[8,128]{1,0:T(8,128)S(1)} %add.133), channel_id=1, source_target_pairs={{0,8},{1,9},{2,10},{3,11},{4,12},{5,13},{6,14},{7,15},{8,0},{9,1},... | collective-permute-start | bytes 12296 | tf_op jit(solution)/shard_map/ppermute | solution.py:296
  75.3 0.9 %collective-permute-start.34 = (f16[1,256,256]{2,1,0:T(8,128)(2,1)S(1)}, f16[1,256,256]{2,1,0:T(8,128)(2,1)S(1)}, u32[]{:S(2)}, u32[]{:S(2)}) collective-permute-start(f16[1,256,256]{2,1,0:T(8,128)(2,1)S(1)} %get-tuple-element.108), channel_id=1, source_target_pairs={{0,4},{1,5},{4,8},{5,9},{8,12},{9,13},{12,14},{13,15},{14,10},{15,... | collective-permute-start | bytes 393224 | tf_op jit(solution)/shard_map/ppermute | solution.py:290
  76.2 1.5 %collective-permute-start.37 = (f16[1,256,256]{2,1,0:T(8,128)(2,1)S(1)}, f16[1,256,256]{2,1,0:T(8,128)(2,1)S(1)}, u32[]{:S(2)}, u32[]{:S(2)}) collective-permute-start(f16[1,256,256]{2,1,0:T(8,128)(2,1)S(1)} %get-tuple-element.109), channel_id=1, source_target_pairs={{0,2},{1,3},{4,0},{5,1},{8,4},{9,5},{12,8},{13,9},{14,12},{15,13},... | collective-permute-start | bytes 393224 | tf_op jit(solution)/shard_map/ppermute | solution.py:293
  77.7 2.0 %collective-permute-start.35 = (f16[1,256,256]{2,1,0:T(8,128)(2,1)S(1)}, f16[1,256,256]{2,1,0:T(8,128)(2,1)S(1)}, u32[]{:S(2)}, u32[]{:S(2)}) collective-permute-start(f16[1,256,256]{2,1,0:T(8,128)(2,1)S(1)} %get-tuple-element.112), channel_id=1, source_target_pairs={{0,2},{1,3},{4,0},{5,1},{8,4},{9,5},{12,8},{13,9},{14,12},{15,13},... | collective-permute-start | bytes 393224 | tf_op jit(solution)/shard_map/ppermute | solution.py:293
  79.7 0.1 add_reduce_fusion
  79.9 0.7 fusion.27
  80.5 0.7 multiply_reduce_fusion.1
  83.1 0.2 multiply_reduce_fusion
  83.4 0.7 add_multiply_fusion.1
  84.1 0.6 collective-permute-done.36
  84.7 0.7 add_multiply_fusion
  85.4 0.9 %fusion.1 = f32[2,256,256]{2,1,0:T(8,128)} fusion(f32[1,256,256]{2,1,0:T(8,128)S(1)} %get-tuple-element.110, f32[1,256,256]{2,1,0:T(8,128)S(1)} %get-tuple-element.111, f32[1,256,256]{2,1,0:T(8,128)S(1)} %add_multiply_fusion, f32[1,256,256]{2,1,0:T(8,128)S(1)} %add_multiply_fusion.1, bf16[2,256,256]{2,1,0:T(8,128)(2,1)S(1)} %copy-done, ...), kind=kLoop, calls=%fused_computation.3 | loop fusion | flops 1048576 | bytes 2359300 | tf_op jit(solution)/shard_map/sub | solution.py:468
  (40 shorter events, 0.2 us)
Async XLA Ops:
  0.6 13.5 %copy-start = (bf16[2,256,256]{2,1,0:T(8,128)(2,1)S(1)}, bf16[2,256,256]{2,1,0:T(8,128)(2,1)}, u32[]{:S(2)}) copy-start(bf16[2,256,256]{2,1,0:T(8,128)(2,1)} %rest_0_.1) | copy-start | bytes 786436
  0.6 9.6 %collective-permute-start.2 = (bf16[2,256,256]{2,1,0:T(8,128)(2,1)}, bf16[2,256,256]{2,1,0:T(8,128)(2,1)S(1)}, u32[]{:S(2)}, u32[]{:S(2)}) collective-permute-start(bf16[2,256,256]{2,1,0:T(8,128)(2,1)} %rest_0_.1), channel_id=1, source_target_pairs={{0,2},{1,3},{4,0},{5,1},{8,4},{9,5},{12,8},{13,9},{14,12},{15,13},... | collective-permute-start | bytes 786440 | tf_op jit(solution)/shard_map/ppermute | solution.py:293
  3.7 8.0 %collective-permute-start.1 = (bf16[2,256,256]{2,1,0:T(8,128)(2,1)}, bf16[2,256,256]{2,1,0:T(8,128)(2,1)S(1)}, u32[]{:S(2)}, u32[]{:S(2)}) collective-permute-start(bf16[2,256,256]{2,1,0:T(8,128)(2,1)} %rest_0_.1), channel_id=1, source_target_pairs={{0,4},{1,5},{4,8},{5,9},{8,12},{9,13},{12,14},{13,15},{14,10},{15,... | collective-permute-start | bytes 786440 | tf_op jit(solution)/shard_map/ppermute | solution.py:290
  3.8 10.4 %collective-permute-start = (bf16[2,256,256]{2,1,0:T(8,128)(2,1)}, bf16[2,256,256]{2,1,0:T(8,128)(2,1)S(1)}, u32[]{:S(2)}, u32[]{:S(2)}) collective-permute-start(bf16[2,256,256]{2,1,0:T(8,128)(2,1)} %rest_0_.1), channel_id=1, source_target_pairs={{0,1},{1,0},{2,3},{3,2},{4,5},{5,4},{6,7},{7,6},{8,9},{9,8},{10,11... | collective-permute-start | bytes 786440 | tf_op jit(solution)/shard_map/ppermute | solution.py:296
  11.6 8.6 %collective-permute-start.3 = (bf16[2,256,256]{2,1,0:T(8,128)(2,1)S(1)}, bf16[2,256,256]{2,1,0:T(8,128)(2,1)S(1)}, u32[]{:S(2)}, u32[]{:S(2)}) collective-permute-start(bf16[2,256,256]{2,1,0:T(8,128)(2,1)S(1)} %collective-permute-done.1.rest_0_), channel_id=1, source_target_pairs={{0,4},{1,5},{4,8},{5,9},{8,12},{9,13},{12,14},{13,15},{14,10},{15,... | collective-permute-start | bytes 786440 | tf_op jit(solution)/shard_map/ppermute | solution.py:290
  12.0 8.2 %collective-permute-start.4 = (bf16[2,256,256]{2,1,0:T(8,128)(2,1)S(1)}, bf16[2,256,256]{2,1,0:T(8,128)(2,1)S(1)}, u32[]{:S(2)}, u32[]{:S(2)}) collective-permute-start(bf16[2,256,256]{2,1,0:T(8,128)(2,1)S(1)} %collective-permute-done.2.rest_1_), channel_id=1, source_target_pairs={{0,2},{1,3},{4,0},{5,1},{8,4},{9,5},{12,8},{13,9},{14,12},{15,13},... | collective-permute-start | bytes 786440 | tf_op jit(solution)/shard_map/ppermute | solution.py:293
  13.7 8.2 %collective-permute-start.7 = (bf16[2,256,256]{2,1,0:T(8,128)(2,1)S(1)}, bf16[2,256,256]{2,1,0:T(8,128)(2,1)S(1)}, u32[]{:S(2)}, u32[]{:S(2)}) collective-permute-start(bf16[2,256,256]{2,1,0:T(8,128)(2,1)S(1)} %collective-permute-done.1.rest_0_), channel_id=1, source_target_pairs={{0,1},{1,0},{2,3},{3,2},{4,5},{5,4},{6,7},{7,6},{8,9},{9,8},{10,11... | collective-permute-start | bytes 786440 | tf_op jit(solution)/shard_map/ppermute | solution.py:296
  13.7 9.2 %collective-permute-start.8 = (bf16[2,256,256]{2,1,0:T(8,128)(2,1)S(1)}, bf16[2,256,256]{2,1,0:T(8,128)(2,1)S(1)}, u32[]{:S(2)}, u32[]{:S(2)}) collective-permute-start(bf16[2,256,256]{2,1,0:T(8,128)(2,1)S(1)} %collective-permute-done.2.rest_1_), channel_id=1, source_target_pairs={{0,1},{1,0},{2,3},{3,2},{4,5},{5,4},{6,7},{7,6},{8,9},{9,8},{10,11... | collective-permute-start | bytes 786440 | tf_op jit(solution)/shard_map/ppermute | solution.py:296
  20.2 2.6 %collective-permute-start.9 = (bf16[2,256,256]{2,1,0:T(8,128)(2,1)S(1)}, bf16[2,256,256]{2,1,0:T(8,128)(2,1)S(1)}, u32[]{:S(2)}, u32[]{:S(2)}) collective-permute-start(bf16[2,256,256]{2,1,0:T(8,128)(2,1)S(1)} %collective-permute-done.3.rest_4_), channel_id=1, source_target_pairs={{0,1},{1,0},{2,3},{3,2},{4,5},{5,4},{6,7},{7,6},{8,9},{9,8},{10,11... | collective-permute-start | bytes 786440 | tf_op jit(solution)/shard_map/ppermute | solution.py:296
  20.3 2.5 %collective-permute-start.10 = (bf16[2,256,256]{2,1,0:T(8,128)(2,1)S(1)}, bf16[2,256,256]{2,1,0:T(8,128)(2,1)S(1)}, u32[]{:S(2)}, u32[]{:S(2)}) collective-permute-start(bf16[2,256,256]{2,1,0:T(8,128)(2,1)S(1)} %collective-permute-done.4.rest_5_), channel_id=1, source_target_pairs={{0,1},{1,0},{2,3},{3,2},{4,5},{5,4},{6,7},{7,6},{8,9},{9,8},{10,11... | collective-permute-start | bytes 786440 | tf_op jit(solution)/shard_map/ppermute | solution.py:296
  20.8 8.3 %collective-permute-start.5 = (bf16[2,256,256]{2,1,0:T(8,128)(2,1)S(1)}, bf16[2,256,256]{2,1,0:T(8,128)(2,1)S(1)}, u32[]{:S(2)}, u32[]{:S(2)}) collective-permute-start(bf16[2,256,256]{2,1,0:T(8,128)(2,1)S(1)} %collective-permute-done.3.rest_4_), channel_id=1, source_target_pairs={{0,4},{1,5},{4,8},{5,9},{8,12},{9,13},{12,14},{13,15},{14,10},{15,... | collective-permute-start | bytes 786440 | tf_op jit(solution)/shard_map/ppermute | solution.py:290
  21.8 7.9 %collective-permute-start.6 = (bf16[2,256,256]{2,1,0:T(8,128)(2,1)S(1)}, bf16[2,256,256]{2,1,0:T(8,128)(2,1)S(1)}, u32[]{:S(2)}, u32[]{:S(2)}) collective-permute-start(bf16[2,256,256]{2,1,0:T(8,128)(2,1)S(1)} %collective-permute-done.4.rest_5_), channel_id=1, source_target_pairs={{0,2},{1,3},{4,0},{5,1},{8,4},{9,5},{12,8},{13,9},{14,12},{15,13},... | collective-permute-start | bytes 786440 | tf_op jit(solution)/shard_map/ppermute | solution.py:293
  29.8 2.6 %collective-permute-start.13 = (bf16[2,256,256]{2,1,0:T(8,128)(2,1)S(1)}, bf16[2,256,256]{2,1,0:T(8,128)(2,1)S(1)}, u32[]{:S(2)}, u32[]{:S(2)}) collective-permute-start(bf16[2,256,256]{2,1,0:T(8,128)(2,1)S(1)} %collective-permute-done.5.rest_0_), channel_id=1, source_target_pairs={{0,1},{1,0},{2,3},{3,2},{4,5},{5,4},{6,7},{7,6},{8,9},{9,8},{10,11... | collective-permute-start | bytes 786440 | tf_op jit(solution)/shard_map/ppermute | solution.py:296
  29.8 2.6 %collective-permute-start.14 = (bf16[2,256,256]{2,1,0:T(8,128)(2,1)S(1)}, bf16[2,256,256]{2,1,0:T(8,128)(2,1)S(1)}, u32[]{:S(2)}, u32[]{:S(2)}) collective-permute-start(bf16[2,256,256]{2,1,0:T(8,128)(2,1)S(1)} %collective-permute-done.6.rest_1_), channel_id=1, source_target_pairs={{0,1},{1,0},{2,3},{3,2},{4,5},{5,4},{6,7},{7,6},{8,9},{9,8},{10,11... | collective-permute-start | bytes 786440 | tf_op jit(solution)/shard_map/ppermute | solution.py:296
  30.3 6.0 %collective-permute-start.12 = (bf16[1,256,256]{2,1,0:T(8,128)(2,1)S(1)}, bf16[1,256,256]{2,1,0:T(8,128)(2,1)S(1)}, u32[]{:S(2)}, u32[]{:S(2)}) collective-permute-start(bf16[1,256,256]{2,1,0:T(8,128)(2,1)S(1)} %slice.181), channel_id=1, source_target_pairs={{0,2},{1,3},{4,0},{5,1},{8,4},{9,5},{12,8},{13,9},{14,12},{15,13},... | collective-permute-start | bytes 393224 | tf_op jit(solution)/shard_map/ppermute | solution.py:293
  31.5 5.4 %collective-permute-start.11 = (bf16[1,256,256]{2,1,0:T(8,128)(2,1)S(1)}, bf16[1,256,256]{2,1,0:T(8,128)(2,1)S(1)}, u32[]{:S(2)}, u32[]{:S(2)}) collective-permute-start(bf16[1,256,256]{2,1,0:T(8,128)(2,1)S(1)} %slice.180), channel_id=1, source_target_pairs={{0,4},{1,5},{4,8},{5,9},{8,12},{9,13},{12,14},{13,15},{14,10},{15,... | collective-permute-start | bytes 393224 | tf_op jit(solution)/shard_map/ppermute | solution.py:290
  36.9 1.3 %collective-permute-start.15 = (bf16[1,256,256]{2,1,0:T(8,128)(2,1)S(1)}, bf16[1,256,256]{2,1,0:T(8,128)(2,1)S(1)}, u32[]{:S(2)}, u32[]{:S(2)}) collective-permute-start(bf16[1,256,256]{2,1,0:T(8,128)(2,1)S(1)} %collective-permute-done.11.rest_0_), channel_id=1, source_target_pairs={{0,1},{1,0},{2,3},{3,2},{4,5},{5,4},{6,7},{7,6},{8,9},{9,8},{10,11... | collective-permute-start | bytes 393224 | tf_op jit(solution)/shard_map/ppermute | solution.py:296
  36.9 1.5 %collective-permute-start.16 = (bf16[1,256,256]{2,1,0:T(8,128)(2,1)S(1)}, bf16[1,256,256]{2,1,0:T(8,128)(2,1)S(1)}, u32[]{:S(2)}, u32[]{:S(2)}) collective-permute-start(bf16[1,256,256]{2,1,0:T(8,128)(2,1)S(1)} %collective-permute-done.12.rest_1_), channel_id=1, source_target_pairs={{0,1},{1,0},{2,3},{3,2},{4,5},{5,4},{6,7},{7,6},{8,9},{9,8},{10,11... | collective-permute-start | bytes 393224 | tf_op jit(solution)/shard_map/ppermute | solution.py:296
  44.2 38.9 %copy-start.1 = (bf16[3,2,256,256]{3,2,1,0:T(8,128)(2,1)S(1)}, bf16[3,2,256,256]{3,2,1,0:T(8,128)(2,1)}, u32[]{:S(2)}) copy-start(bf16[3,2,256,256]{3,2,1,0:T(8,128)(2,1)} %lower_hbm.1) | copy-start | bytes 2359300
  44.2 3.5 %collective-permute-start.18 = (f32[4,256,256]{2,1,0:T(8,128)S(1)}, f32[4,256,256]{2,1,0:T(8,128)S(1)}, u32[]{:S(2)}, u32[]{:S(2)}) collective-permute-start(f32[4,256,256]{2,1,0:T(8,128)S(1)} %get-tuple-element.85), channel_id=1, source_target_pairs={{0,1},{1,0},{2,3},{3,2},{4,5},{5,4},{6,7},{7,6},{8,9},{9,8},{10,11... | collective-permute-start | bytes 3145736 | tf_op jit(solution)/shard_map/ppermute | solution.py:296
  44.3 3.4 %collective-permute-start.17 = (f32[2,256,256]{2,1,0:T(8,128)S(1)}, f32[2,256,256]{2,1,0:T(8,128)S(1)}, u32[]{:S(2)}, u32[]{:S(2)}) collective-permute-start(f32[2,256,256]{2,1,0:T(8,128)S(1)} %get-tuple-element.84), channel_id=1, source_target_pairs={{0,1},{1,0},{2,3},{3,2},{4,5},{5,4},{6,7},{7,6},{8,9},{9,8},{10,11... | collective-permute-start | bytes 1572872 | tf_op jit(solution)/shard_map/ppermute | solution.py:296
  47.7 13.4 %collective-permute-start.19 = (f32[10,256,256]{2,1,0:T(8,128)S(1)}, f32[10,256,256]{2,1,0:T(8,128)S(1)}, u32[]{:S(2)}, u32[]{:S(2)}) collective-permute-start(f32[10,256,256]{2,1,0:T(8,128)S(1)} %get-tuple-element.87), channel_id=1, source_target_pairs={{0,1},{1,0},{2,3},{3,2},{4,5},{5,4},{6,7},{7,6},{8,9},{9,8},{10,11... | collective-permute-start | bytes 7864328 | tf_op jit(solution)/shard_map/ppermute | solution.py:296
  49.2 5.8 %collective-permute-start.21 = (f16[1,256,256]{2,1,0:T(8,128)(2,1)S(1)}, f16[1,256,256]{2,1,0:T(8,128)(2,1)S(1)}, u32[]{:S(2)}, u32[]{:S(2)}) collective-permute-start(f16[1,256,256]{2,1,0:T(8,128)(2,1)S(1)} %get-tuple-element.124), channel_id=1, source_target_pairs={{0,4},{1,5},{4,8},{5,9},{8,12},{9,13},{12,14},{13,15},{14,10},{15,... | collective-permute-start | bytes 393224 | tf_op jit(solution)/shard_map/ppermute | solution.py:290
  49.6 6.1 %collective-permute-start.22 = (f16[1,256,256]{2,1,0:T(8,128)(2,1)S(1)}, f16[1,256,256]{2,1,0:T(8,128)(2,1)S(1)}, u32[]{:S(2)}, u32[]{:S(2)}) collective-permute-start(f16[1,256,256]{2,1,0:T(8,128)(2,1)S(1)} %get-tuple-element.125), channel_id=1, source_target_pairs={{0,2},{1,3},{4,0},{5,1},{8,4},{9,5},{12,8},{13,9},{14,12},{15,13},... | collective-permute-start | bytes 393224 | tf_op jit(solution)/shard_map/ppermute | solution.py:293
  51.3 7.8 %collective-permute-start.20 = (f32[8,128]{1,0:T(8,128)S(1)}, f32[8,128]{1,0:T(8,128)S(1)}, u32[]{:S(2)}, u32[]{:S(2)}) collective-permute-start(f32[8,128]{1,0:T(8,128)S(1)} %get-tuple-element.88), channel_id=1, source_target_pairs={{0,1},{1,0},{2,3},{3,2},{4,5},{5,4},{6,7},{7,6},{8,9},{9,8},{10,11... | collective-permute-start | bytes 12296 | tf_op jit(solution)/shard_map/ppermute | solution.py:296
  51.3 8.0 %collective-permute-start.27 = (f16[1,256,256]{2,1,0:T(8,128)(2,1)S(1)}, f16[1,256,256]{2,1,0:T(8,128)(2,1)S(1)}, u32[]{:S(2)}, u32[]{:S(2)}) collective-permute-start(f16[1,256,256]{2,1,0:T(8,128)(2,1)S(1)} %get-tuple-element.120), channel_id=1, source_target_pairs={{0,2},{1,3},{4,0},{5,1},{8,4},{9,5},{12,8},{13,9},{14,12},{15,13},... | collective-permute-start | bytes 393224 | tf_op jit(solution)/shard_map/ppermute | solution.py:293
  55.0 6.1 %collective-permute-start.26 = (f16[1,256,256]{2,1,0:T(8,128)(2,1)S(1)}, f16[1,256,256]{2,1,0:T(8,128)(2,1)S(1)}, u32[]{:S(2)}, u32[]{:S(2)}) collective-permute-start(f16[1,256,256]{2,1,0:T(8,128)(2,1)S(1)} %get-tuple-element.121), channel_id=1, source_target_pairs={{0,4},{1,5},{4,8},{5,9},{8,12},{9,13},{12,14},{13,15},{14,10},{15,... | collective-permute-start | bytes 393224 | tf_op jit(solution)/shard_map/ppermute | solution.py:290
  57.2 7.5 %collective-permute-start.25 = (f16[1,256,256]{2,1,0:T(8,128)(2,1)S(1)}, f16[1,256,256]{2,1,0:T(8,128)(2,1)S(1)}, u32[]{:S(2)}, u32[]{:S(2)}) collective-permute-start(f16[1,256,256]{2,1,0:T(8,128)(2,1)S(1)} %get-tuple-element.118), channel_id=1, source_target_pairs={{0,2},{1,3},{4,0},{5,1},{8,4},{9,5},{12,8},{13,9},{14,12},{15,13},... | collective-permute-start | bytes 393224 | tf_op jit(solution)/shard_map/ppermute | solution.py:293
  59.1 6.0 %collective-permute-start.24 = (f16[1,256,256]{2,1,0:T(8,128)(2,1)S(1)}, f16[1,256,256]{2,1,0:T(8,128)(2,1)S(1)}, u32[]{:S(2)}, u32[]{:S(2)}) collective-permute-start(f16[1,256,256]{2,1,0:T(8,128)(2,1)S(1)} %get-tuple-element.119), channel_id=1, source_target_pairs={{0,4},{1,5},{4,8},{5,9},{8,12},{9,13},{12,14},{13,15},{14,10},{15,... | collective-permute-start | bytes 393224 | tf_op jit(solution)/shard_map/ppermute | solution.py:290
  59.3 9.3 %collective-permute-start.23 = (f32[8,128]{1,0:T(8,128)S(1)}, f32[8,128]{1,0:T(8,128)S(1)}, u32[]{:S(2)}, u32[]{:S(2)}) collective-permute-start(f32[8,128]{1,0:T(8,128)S(1)} %add.115), channel_id=1, source_target_pairs={{0,2},{1,3},{2,0},{3,1},{4,6},{5,7},{6,4},{7,5},{8,10},{9,11},{10,... | collective-permute-start | bytes 12296 | tf_op jit(solution)/shard_map/ppermute | solution.py:296
  62.6 6.7 %collective-permute-start.32 = (f16[1,256,256]{2,1,0:T(8,128)(2,1)S(1)}, f16[1,256,256]{2,1,0:T(8,128)(2,1)S(1)}, u32[]{:S(2)}, u32[]{:S(2)}) collective-permute-start(f16[1,256,256]{2,1,0:T(8,128)(2,1)S(1)} %get-tuple-element.116), channel_id=1, source_target_pairs={{0,2},{1,3},{4,0},{5,1},{8,4},{9,5},{12,8},{13,9},{14,12},{15,13},... | collective-permute-start | bytes 393224 | tf_op jit(solution)/shard_map/ppermute | solution.py:293
  62.8 6.5 %collective-permute-start.31 = (f16[1,256,256]{2,1,0:T(8,128)(2,1)S(1)}, f16[1,256,256]{2,1,0:T(8,128)(2,1)S(1)}, u32[]{:S(2)}, u32[]{:S(2)}) collective-permute-start(f16[1,256,256]{2,1,0:T(8,128)(2,1)S(1)} %get-tuple-element.117), channel_id=1, source_target_pairs={{0,4},{1,5},{4,8},{5,9},{8,12},{9,13},{12,14},{13,15},{14,10},{15,... | collective-permute-start | bytes 393224 | tf_op jit(solution)/shard_map/ppermute | solution.py:290
  66.5 5.0 %collective-permute-start.30 = (f16[1,256,256]{2,1,0:T(8,128)(2,1)S(1)}, f16[1,256,256]{2,1,0:T(8,128)(2,1)S(1)}, u32[]{:S(2)}, u32[]{:S(2)}) collective-permute-start(f16[1,256,256]{2,1,0:T(8,128)(2,1)S(1)} %get-tuple-element.114), channel_id=1, source_target_pairs={{0,2},{1,3},{4,0},{5,1},{8,4},{9,5},{12,8},{13,9},{14,12},{15,13},... | collective-permute-start | bytes 393224 | tf_op jit(solution)/shard_map/ppermute | solution.py:293
  67.4 5.0 %collective-permute-start.29 = (f16[1,256,256]{2,1,0:T(8,128)(2,1)S(1)}, f16[1,256,256]{2,1,0:T(8,128)(2,1)S(1)}, u32[]{:S(2)}, u32[]{:S(2)}) collective-permute-start(f16[1,256,256]{2,1,0:T(8,128)(2,1)S(1)} %get-tuple-element.115), channel_id=1, source_target_pairs={{0,4},{1,5},{4,8},{5,9},{8,12},{9,13},{12,14},{13,15},{14,10},{15,... | collective-permute-start | bytes 393224 | tf_op jit(solution)/shard_map/ppermute | solution.py:290
  68.6 5.2 %collective-permute-start.28 = (f32[8,128]{1,0:T(8,128)S(1)}, f32[8,128]{1,0:T(8,128)S(1)}, u32[]{:S(2)}, u32[]{:S(2)}) collective-permute-start(f32[8,128]{1,0:T(8,128)S(1)} %add.124), channel_id=1, source_target_pairs={{0,4},{1,5},{2,6},{3,7},{4,0},{5,1},{6,2},{7,3},{8,12},{9,13},{10,... | collective-permute-start | bytes 12296 | tf_op jit(solution)/shard_map/ppermute | solution.py:296
  73.9 5.9 %collective-permute-start.33 = (f32[8,128]{1,0:T(8,128)S(1)}, f32[8,128]{1,0:T(8,128)S(1)}, u32[]{:S(2)}, u32[]{:S(2)}) collective-permute-start(f32[8,128]{1,0:T(8,128)S(1)} %add.133), channel_id=1, source_target_pairs={{0,8},{1,9},{2,10},{3,11},{4,12},{5,13},{6,14},{7,15},{8,0},{9,1},... | collective-permute-start | bytes 12296 | tf_op jit(solution)/shard_map/ppermute | solution.py:296
  75.3 8.1 %collective-permute-start.34 = (f16[1,256,256]{2,1,0:T(8,128)(2,1)S(1)}, f16[1,256,256]{2,1,0:T(8,128)(2,1)S(1)}, u32[]{:S(2)}, u32[]{:S(2)}) collective-permute-start(f16[1,256,256]{2,1,0:T(8,128)(2,1)S(1)} %get-tuple-element.108), channel_id=1, source_target_pairs={{0,4},{1,5},{4,8},{5,9},{8,12},{9,13},{12,14},{13,15},{14,10},{15,... | collective-permute-start | bytes 393224 | tf_op jit(solution)/shard_map/ppermute | solution.py:290
  76.2 7.9 %collective-permute-start.37 = (f16[1,256,256]{2,1,0:T(8,128)(2,1)S(1)}, f16[1,256,256]{2,1,0:T(8,128)(2,1)S(1)}, u32[]{:S(2)}, u32[]{:S(2)}) collective-permute-start(f16[1,256,256]{2,1,0:T(8,128)(2,1)S(1)} %get-tuple-element.109), channel_id=1, source_target_pairs={{0,2},{1,3},{4,0},{5,1},{8,4},{9,5},{12,8},{13,9},{14,12},{15,13},... | collective-permute-start | bytes 393224 | tf_op jit(solution)/shard_map/ppermute | solution.py:293
  77.7 5.7 %collective-permute-start.35 = (f16[1,256,256]{2,1,0:T(8,128)(2,1)S(1)}, f16[1,256,256]{2,1,0:T(8,128)(2,1)S(1)}, u32[]{:S(2)}, u32[]{:S(2)}) collective-permute-start(f16[1,256,256]{2,1,0:T(8,128)(2,1)S(1)} %get-tuple-element.112), channel_id=1, source_target_pairs={{0,2},{1,3},{4,0},{5,1},{8,4},{9,5},{12,8},{13,9},{14,12},{15,13},... | collective-permute-start | bytes 393224 | tf_op jit(solution)/shard_map/ppermute | solution.py:293
  79.7 5.0 %collective-permute-start.36 = (f16[1,256,256]{2,1,0:T(8,128)(2,1)S(1)}, f16[1,256,256]{2,1,0:T(8,128)(2,1)S(1)}, u32[]{:S(2)}, u32[]{:S(2)}) collective-permute-start(f16[1,256,256]{2,1,0:T(8,128)(2,1)S(1)} %get-tuple-element.113), channel_id=1, source_target_pairs={{0,4},{1,5},{4,8},{5,9},{8,12},{9,13},{12,14},{13,15},{14,10},{15,... | collective-permute-start | bytes 393224 | tf_op jit(solution)/shard_map/ppermute | solution.py:290

commit v3 on v2

v3 whole, which is shorter than its diff:
```python
import functools

import jax
import jax.numpy as jnp
import numpy as np
from jax import lax
from jax.experimental import pallas as pl
from jax.experimental.pallas import tpu as pltpu
from jax.sharding import PartitionSpec as P

shift_energy = 2.0
CORES = 2
BATCH = 8
SLOTS = 4
KEEP = pl.BlockSpec(memory_space=pltpu.VMEM)
SCALAR = pl.BlockSpec(memory_space=pltpu.SMEM)
INHBM = pl.BlockSpec(memory_space=pltpu.HBM)
ANYWHERE = pl.BlockSpec(memory_space=pl.ANY)


def ring_of(mesh):
    chips = mesh.shape["sector"] // CORES
    rows = 2 if mesh.shape["groups"] == 2 else 1
    cols = chips // rows
    order = [z * rows for z in range(cols)]
    for y in range(1, rows):
        order += [z * rows + y for z in reversed(range(cols))]
    return order


def over(x, n):
    return lax.shift_right_logical(x, n.bit_length() - 1) if n & (n - 1) == 0 else lax.div(x, n)


def left_over(x, n):
    return x & (n - 1) if n & (n - 1) == 0 else lax.rem(x, n)


def starts_of(pieces, psi, starts, sems):
    copies = [
        pltpu.make_async_copy(piece, psi.at[pl.ds(start, piece.shape[0])], sems.at[n])
        for n, (piece, start) in enumerate(zip(pieces, starts))
    ]
    for copy in copies:
        copy.start()
    return copies


def terms_of(begin, end, plan_ref, left_hbm, right_hbm, held, sems, ready, psi, acc):
    def bring(i):
        @pl.when(i < end)
        def _():
            at = left_over(i, SLOTS)
            ks = [over(plan_ref[i * BATCH + u], 65536) for u in range(BATCH)]
            for n, env in enumerate((left_hbm, right_hbm)):
                for u, k in enumerate(ks):
                    pltpu.make_async_copy(env.at[k], held.at[at, n, u], sems.at[at, n]).start()

    def batch(i, carry):
        bring(i + SLOTS - 1)
        at = left_over(i, SLOTS)
        for n in range(2):
            pltpu.make_async_copy(held.at[at, n], held.at[at, n], sems.at[at, n]).wait()
        codes = [plan_ref[i * BATCH + u] for u in range(BATCH)]
        halves = [
            jnp.dot(
                held[at, 0, u], psi[left_over(over(c, 256), 256)], preferred_element_type=jnp.float32
            ).astype(jnp.bfloat16)
            for u, c in enumerate(codes)
        ]
        whole = [jnp.dot(h, held[at, 1, u], preferred_element_type=jnp.float32) for u, h in enumerate(halves)]
        for c, w in zip(codes, whole):
            acc[left_over(c, 256)] += w
        return carry

    for ahead in range(SLOTS - 1):
        bring(begin + ahead)
    for copy in ready:
        copy.wait()
    lax.fori_loop(begin, end, batch, 0)


def plan_kernel(
    shape, tl_hbm, me_ref, psi_hbm, lower_hbm,
    vec, acc, psi, plan, bounds, tl_ref, psi_ref, lower_ref, codes, kinds, fill, small_sems,
):
    chips, rows_y, per, cap, empty = shape
    terms = tl_ref.shape[1]
    side = psi.shape[1]
    lower = lower_ref.shape[0]
    reach = chips // 2
    small = [
        pltpu.make_async_copy(a, b, small_sems.at[n])
        for n, (a, b) in enumerate(((tl_hbm, tl_ref), (psi_hbm, psi_ref), (lower_hbm, lower_ref)))
    ]
    for copy in small:
        copy.start()
    small[0].wait()

    def place(chip):
        if rows_y == 1:
            return chip
        z, y = over(chip, rows_y), left_over(chip, rows_y)
        return jnp.where(y == 0, z, chips - 1 - z)

    me = me_ref[0]
    my_place, my_core = place(over(me, CORES)), left_over(me, CORES)

    def slot(sector):
        chip, core, j = over(sector, per * CORES), left_over(over(sector, per), CORES), left_over(sector, per)
        rel = left_over(place(chip) - my_place + chips, chips)
        return rel, jnp.where(core == my_core, 0, chips * per) + rel * per + j

    for stage in range(reach + 1):
        fill[stage] = 0

    def classify(k, carry):
        rel, src = slot(tl_ref[0, k])
        _, dst = slot(tl_ref[1, k])
        stage = jnp.minimum(rel, chips - rel)
        codes[k] = k * 65536 + src * 256 + dst
        kinds[k] = stage
        fill[stage] += 1
        return carry

    lax.fori_loop(0, terms, classify, 0, unroll=4)
    at = jnp.int32(0)
    for stage in range(reach + 1):
        bounds[stage] = at
        count = fill[stage]
        fill[stage] = at * BATCH
        at = at + over(count + (BATCH - 1), BATCH)
    bounds[reach + 1] = at

    def put(k, carry):
        stage = kinds[k]
        plan[fill[stage]] = codes[k]
        fill[stage] += 1
        return carry

    lax.fori_loop(0, terms, put, 0, unroll=4)

    for stage in range(reach + 1):

        def pad(i, carry):
            before = plan[i - 1]
            plan[i] = before - left_over(before, 256) + empty
            return carry

        lax.fori_loop(fill[stage], bounds[stage + 1] * BATCH, pad, 0)

    def zero(i, carry):
        acc[i] = jnp.zeros(acc.shape[1:], jnp.float32)
        return carry

    lax.fori_loop(0, acc.shape[0], zero, 0)

    def fold(x):
        x = jnp.sum(x.reshape(-1, 8, side), axis=0)
        return jnp.sum(x, axis=0, keepdims=True)

    def rows(j):
        psi = psi_ref[j].astype(jnp.float32)
        low = [lower_ref[i, j].astype(jnp.float32) for i in range(lower)]
        return [fold(x * psi) for x in low] + [fold(x * x) for x in low] + [fold(psi * psi)]

    small[1].wait()
    small[2].wait()
    parts = rows(0)
    for j in range(1, psi_ref.shape[0]):
        parts = [a + b for a, b in zip(parts, rows(j))]
    psi[0, 0:16] = jnp.zeros((16, side), psi.dtype)
    vec[...] = jnp.zeros_like(vec)
    for i, x in enumerate(parts):
        vec[pl.ds(i, 1), :] = sum(x[:, c : c + 128] for c in range(0, side, 128))


def stage_kernel(stage, starts, finish, limit, digit, plan_ref, bounds_ref, left_hbm, right_hbm, *rest):
    count = len(starts)
    pieces, rest = rest[:count], rest[count:]
    if finish:
        vec_ref, digit_ref, _, _, acc, psi = rest[:6]
        outs, rest = rest[6 : 6 + len(finish)], rest[6 + len(finish) :]
        scales, digits_ref, vec, out_sems, *rest = rest
    else:
        _, _, acc, psi, *rest = rest
    sems, held, env_sems = rest
    copies = starts_of(pieces, psi, starts, sems)
    begin, end = bounds_ref[stage], bounds_ref[stage + 1]
    terms_of(begin, end, plan_ref, left_hbm, right_hbm, held, env_sems, copies, psi, acc)
    if finish:
        side = psi.shape[1]

        def add(s, carry):
            total, m = carry
            for row in range(0, side, 32):
                piece = psi[s, row : row + 32, :]
                total += acc[s, row : row + 32, :] * piece.astype(jnp.float32)
                m = jnp.maximum(m, jnp.abs(piece))
            return total, m

        moves = []
        for out, chunks in zip(outs, finish):
            put = 0
            for begin, size in chunks:
                place = out.at[pl.ds(put, size), pl.ds(0, side)]
                moves.append(pltpu.make_async_copy(acc.at[pl.ds(begin, size)], place, out_sems.at[len(moves)]))
                put += size
        for move in moves:
            move.start()
        begin = jnp.zeros((32, side), jnp.float32), jnp.zeros((32, side), psi.dtype)
        total, m = lax.fori_loop(0, psi.shape[0], add, begin)
        total = jnp.sum(total, axis=0, keepdims=True)
        vec[...] = vec_ref[...]
        vec[pl.ds(vec.shape[0] - 1, 1), :] = sum(total[:, c : c + 128] for c in range(0, side, 128))
        small = jnp.sum(vec[...], axis=1, keepdims=True)
        digits = jnp.floor(small * digit_ref[0] + 0.5) - digit * jnp.floor(small * digit_ref[1] + 0.5)

        digits_ref[...] = digits
        for out in outs:
            rows = out.shape[1] - side

            def under(i, carry):
                out[i, pl.ds(side, rows), :] = jnp.zeros((rows, side), jnp.float32)
                out[i, pl.ds(side, vec.shape[0]), pl.ds(0, 128)] = digits
                return carry

            lax.fori_loop(0, out.shape[0], under, 0)
        bound = jnp.full((1, 128), limit * jnp.max(m.astype(jnp.float32)))
        power = jnp.clip(15.0 - jnp.ceil(jnp.log2(jnp.maximum(bound, 1e-30))), -60.0, 90.0)
        scales[...] = jnp.zeros_like(scales)
        scales[0:1, :] = jnp.exp2(power)
        scales[1:2, :] = 1.0 / jnp.exp2(power)
        for move in moves:
            move.wait()


def combine_kernel(slots, acc, other, scales, digits, *outs):
    side = acc.shape[2]
    at = 0
    for out in outs:
        for i in range(out.shape[0]):
            out[i, 0:side] = (acc[slots[at]] + other[at, 0:side]) * scales[0:1, 0:1]
            out[i, side:] = other[at, side:]
            out[i, pl.ds(side, digits.shape[0]), pl.ds(0, 128)] += digits[...]
            at += 1


def finish_kernel(lower, digit_ref, scales, home, r0, r1, l0, l1, lower_ref, psi_ref, residual, ritz):
    side = psi_ref.shape[1]
    part = r0.shape[0]
    rows = -(-(2 * lower + 2) // 8) * 8
    place = (0, pl.ds(side, rows), pl.ds(0, 128))
    sums = jnp.sum((home[place] + r0[place] + l0[place]) * digit_ref[2], axis=1, keepdims=True)
    correlation = [sums[j : j + 1] for j in range(lower)]
    coeffs = [correlation[j] / sums[lower + j : lower + j + 1] for j in range(lower)]
    shifted = shift_energy * sum(c * x for c, x in zip(coeffs, correlation))
    value = (sums[rows - 1 : rows] + shifted) / sums[2 * lower : 2 * lower + 1]
    ritz[0] = jnp.sum(value)
    for s in range(psi_ref.shape[0]):
        r, l, at = (r0, l0, s) if s < part else (r1, l1, s - part)
        sigma = (home[s, 0:side] + r[at, 0:side] + l[at, 0:side]) * scales[1:2, 0:1]
        low = sum(c * lower_ref[j, s].astype(jnp.float32) for j, c in enumerate(coeffs))
        residual[s] = sigma + shift_energy * low - value * psi_ref[s].astype(jnp.float32)


def make_per_device(mesh):
    devices = mesh.shape["sector"]
    ring = ring_of(mesh)
    chips = len(ring)
    reach = chips // 2
    rows_y = 2 if mesh.shape["groups"] == 2 else 1

    def shift(by):
        return [
            (ring[p] * CORES + c, ring[(p + by) % chips] * CORES + c) for p in range(chips) for c in range(CORES)
        ]

    to_right, to_left = shift(1), shift(-1)

    def right(x):
        return lax.ppermute(x, "sector", to_right)

    def left(x):
        return lax.ppermute(x, "sector", to_left)

    def pair(x, hop):
        return lax.ppermute(x, "sector", [(i, i ^ hop) for i in range(devices)])

    def across(x):
        return pair(x, 1)

    def per_device(wavefunction, lower_states, left_env, right_env, term_list):
        per, side, _ = wavefunction.shape
        terms = left_env.shape[0]
        sectors = per * devices
        part = per // 2
        lower = lower_states.shape[0]
        base = chips * per
        tie = lax.optimization_barrier
        me = lax.axis_index("sector")

        keep = dict(compiler_params=pltpu.CompilerParams(vmem_limit_bytes=16 * 1024 * 1024))
        stages = reach + 1
        cap = (terms + stages * (BATCH - 1) + BATCH - 1) // BATCH * BATCH
        vec_rows = -(-(2 * lower + 2) // 8) * 8
        left_hbm, right_hbm, psi_hbm, lower_hbm, list_hbm = [
            pltpu.with_memory_space_constraint(x, pltpu.HBM)
            for x in (left_env, right_env, wavefunction, lower_states, term_list.T)
        ]
        vec_shape = jax.ShapeDtypeStruct((vec_rows, 128), jnp.float32)
        row_shape = jax.ShapeDtypeStruct((8, 128), jnp.float32)
        tall = side + -(-vec_rows // 16) * 16
        acc_shape = pltpu.VMEM((sectors + 1, side, side), jnp.float32)
        digit_bits = 12 - (devices.bit_length() - 1)
        weights = np.zeros((3, vec_rows, 128), np.float32)
        for n in range(144 // digit_bits):
            weight = 2.0 ** (digit_bits * n - 72)
            weights[0, :, n], weights[1, :, n], weights[2, :, n] = 1 / weight, 2.0**-digit_bits / weight, weight
        weights = jnp.asarray(weights)
        psi_shape = pltpu.VMEM((sectors, side, side), wavefunction.dtype)

        def make_plan():
            return pl.pallas_call(
                functools.partial(plan_kernel, (chips, rows_y, per, cap, sectors)),
                in_specs=[INHBM, SCALAR, INHBM, INHBM],
                out_specs=[KEEP] * 3 + [SCALAR] * 2,
                out_shape=[
                    vec_shape,
                    acc_shape,
                    psi_shape,
                    jax.ShapeDtypeStruct((cap,), jnp.int32),
                    jax.ShapeDtypeStruct((stages + 1,), jnp.int32),
                ],
                scratch_shapes=[
                    pltpu.SMEM((2, terms), jnp.int32),
                    pltpu.VMEM(wavefunction.shape, wavefunction.dtype),
                    pltpu.VMEM(lower_states.shape, lower_states.dtype),
                    pltpu.SMEM((terms,), jnp.int32),
                    pltpu.SMEM((terms,), jnp.int32),
                    pltpu.SMEM((stages,), jnp.int32),
                    pltpu.SemaphoreType.DMA((3,)),
                ],
                cost_estimate=pl.CostEstimate(flops=0, bytes_accessed=12 << 20, transcendentals=0),
                **keep,
            )(list_hbm, me.reshape(1).astype(jnp.int32), psi_hbm, lower_hbm)

        route = [(reach, 0)] + [(d, h) for d in range(reach - 1, 0, -1) for h in (1, 0)]
        route_left = [(-d if d < reach else reach, 1 - h) for d, h in route]
        need = [x for both in zip(route, route_left) for x in both] + [(0, 0), (0, 1)]
        sets = [need[:4], need[4:]]

        def run_stage(stage, pieces, starts, acc, psi, vec=None):
            finish, sizes, more, small = [], [], [], []
            if stage == reach:
                finish = [[(base + rel % chips * per + h * part, part) for rel, h in parts] for parts in sets]
                sizes = [pltpu.VMEM((part * len(parts), tall, side), jnp.float32) for parts in sets]
                more, small = [vec, weights], [row_shape, vec_shape]
            n, m = len(pieces), len(more)
            scratch = [pltpu.SemaphoreType.DMA((n,))]
            if finish:
                scratch = [pltpu.VMEM((vec_rows, 128), jnp.float32), pltpu.SemaphoreType.DMA((len(need),))] + scratch
            scratch += [
                pltpu.VMEM((SLOTS, 2, BATCH, side, side), left_env.dtype),
                pltpu.SemaphoreType.DMA((SLOTS, 2)),
            ]
            limit = 1.02 * terms * devices * side * side * 0.375 * 0.0546875
            return pl.pallas_call(
                functools.partial(stage_kernel, stage, starts, finish, limit, 2.0**digit_bits),
                in_specs=[SCALAR, SCALAR, INHBM, INHBM] + [INHBM if x is psi_hbm else ANYWHERE for x in pieces]
                + [KEEP] * (m + 2),
                out_specs=[KEEP] * 2 + [KEEP] * len(sizes) + [KEEP] * len(small),
                out_shape=[acc_shape, psi_shape] + sizes + small,
                input_output_aliases={4 + n + m: 0, 5 + n + m: 1},
                scratch_shapes=scratch,
                cost_estimate=pl.CostEstimate(
                    flops=4 * side**3 * terms // stages, bytes_accessed=1 << 20, transcendentals=0
                ),
                **keep,
            )(plan, bounds, left_hbm, right_hbm, *pieces, *more, acc, psi)

        r, l, sib = right(wavefunction), left(wavefunction), across(wavefunction)
        vec, acc, psi, plan, bounds = make_plan()
        acc, psi = run_stage(0, [psi_hbm, sib], [0, base], acc, psi)
        for s in range(1, reach + 1):
            r, l, acc, psi = tie((r, l, acc, psi))
            rel = [(chips - s) * per, s * per] if s < reach else [reach * per, reach * per + part]
            held, at = [r, l, across(r), across(l)], rel + [base + x for x in rel]
            if s < reach - 1:
                r, l = right(r), left(l)
            elif s < reach:
                r, l = right(r[:part]), left(l[part:])
            if s < reach:
                acc, psi = run_stage(s, held, at, acc, psi)
        acc, psi, *others, scales, digits = run_stage(reach, held, at, acc, psi, vec)

        first = across(others[0])
        first, waiting = tie((first, others[1]))
        got = [first, across(waiting)]
        own = {}
        for parts, there in zip(sets, got):
            keys = [key for key in parts if key[0] != 0]
            shapes = [(part, tall, side)] * len(keys)
            if len(keys) < len(parts):
                shapes.append((per, tall, side))
            slots = [rel % chips * per + h * part + i for rel, h in parts for i in range(part)]
            tiles = pl.pallas_call(
                functools.partial(combine_kernel, slots),
                in_specs=[KEEP] * 4,
                out_specs=[KEEP] * len(shapes),
                out_shape=[jax.ShapeDtypeStruct(shape, jnp.float32) for shape in shapes],
                cost_estimate=pl.CostEstimate(flops=0, bytes_accessed=1 << 20, transcendentals=0),
                **keep,
            )(acc, there, scales, digits)
            own.update(zip(keys, tiles))
            home = tiles[-1]

        went, sent = [], []
        for n, (here, there) in enumerate(zip(route, route_left)):
            to_r, to_l = own[here], own[there]
            if n >= 2:
                back, _ = tie((went[n - 2], sent[n - 1]))
                to_r, to_l = to_r + back[0].astype(jnp.float32), to_l + back[1].astype(jnp.float32)
            sent.append((to_r.astype(jnp.float16), to_l.astype(jnp.float16)))
            went.append((right(sent[n][0]), left(sent[n][1])))
        (r1, l0), (r0, l1) = went[-2], went[-1]
        arrived = [x.astype(jnp.float32) for x in (r0, r1, l0, l1)]
        residual, ritz_value = pl.pallas_call(
            functools.partial(finish_kernel, lower),
            in_specs=[KEEP] * 9,
            out_specs=[KEEP, SCALAR],
            out_shape=[
                jax.ShapeDtypeStruct((per, side, side), jnp.float32),
                jax.ShapeDtypeStruct((1,), jnp.float32),
            ],
            cost_estimate=pl.CostEstimate(flops=0, bytes_accessed=2 << 20, transcendentals=0),
            **keep,
        )(weights, scales, home, *arrived, lower_states, wavefunction)
        return (residual, ritz_value)

    return per_device


def solution(mesh):
    return jax.shard_map(
        make_per_device(mesh),
        mesh=mesh,
        in_specs=(
            P(("groups", "sector"), None, None),
            P(None, ("groups", "sector"), None, None),
            P(("groups", "sector"), None, None),
            P(("groups", "sector"), None, None),
            P(("groups", "sector"), None),
        ),
        out_specs=(P(("groups", "sector"), None, None), P("groups")),
        check_vma=False,
    )
```

time: 87.5 us -> 83.4 us (0.953)
  other arithmetic: 11.3 us -> 0.61 us
  waiting for transfers between devices: 14.9 us -> 22.4 us
  Pallas kernels: 25.9 us -> 31.6 us
  starting transfers between devices: 30.3 us -> 26.9 us
  between operations: 3.9 us -> 0.93 us
  local copies, waits for them, and re-layouts: 1.2 us -> 0.04 us
    pallas_call x3 -> x5, Pallas kernels: 14.4 us -> 25.4 us  [run_stage(): pl.pallas_call(functools.partial(stage_kernel, stage, starts, finish, lim...]
    ppermute x11, starting transfers between devices: 7.25 us -> 17.4 us  [right(): return lax.ppermute(x, 'sector', to_right)]
    ppermute x11, starting transfers between devices: 16.2 us -> 6.62 us  [left(): return lax.ppermute(x, 'sector', to_left)]
    ppermute x11, waiting for transfers between devices: 2.9 us -> 11.8 us  [left(): return lax.ppermute(x, 'sector', to_left)]
    convert_element_type x6 -> x18, other arithmetic: 7.97 us -> 0.61 us  [the longest x14 0.53 us: per_device(): sent.append((to_r.astype(jnp.float16), to_l.astype(jnp.float16)))]
    pallas_call x1 -> x3, Pallas kernels: 6.03 us -> 2 us  [the longest x1 1.29 us: per_device(): pl.pallas_call(functools.partial(finish_kernel, lower), in_specs=[KEEP] *...]
    ppermute x16 -> x11, starting transfers between devices: 6.8 us -> 2.92 us  [pair(): return lax.ppermute(x, 'sector', [(i, i ^ hop) for i in range(devices)])]
    add x5 -> x0, other arithmetic: 1.38 us -> none  [the longest x1 0.69 us: per_device(): unpack(r0) + unpack(l0)]
  transfers between devices with their start and end apart: 38 -> 33, of which waited for: 14 -> 17; matrix products, arithmetic and copies ran while one was open for 12% -> 1% of each run, Pallas kernels for 23% -> 29%
where the time goes in v3:
time: 83.4 us; the launch traced here: 82.5 us
  Pallas kernels  31.6 us (38%)
  starting transfers between devices  26.9 us (32%)
  waiting for transfers between devices  22.4 us (27%)
  between operations  0.93 us (1%)
    pallas_call x5, Pallas kernels, run_stage(): pl.pallas_call(functools.partial(stage_kernel, stage, starts, finish, lim...  25.4 us
    ppermute x11, starting transfers between devices, right(): return lax.ppermute(x, 'sector', to_right)  17.4 us
    ppermute x11, waiting for transfers between devices, left(): return lax.ppermute(x, 'sector', to_left)  11.8 us
    ppermute x11, waiting for transfers between devices, right(): return lax.ppermute(x, 'sector', to_right)  6.82 us
    ppermute x11, starting transfers between devices, left(): return lax.ppermute(x, 'sector', to_left)  6.62 us
    pallas_call x1, Pallas kernels, make_plan(): pl.pallas_call(functools.partial(plan_kernel, (chips, rows_y, per, cap, s...  4.13 us
    ppermute x11, waiting for transfers between devices, pair(): return lax.ppermute(x, 'sector', [(i, i ^ hop) for i in range(devices)])  3.79 us
    ppermute x11, starting transfers between devices, pair(): return lax.ppermute(x, 'sector', [(i, i ^ hop) for i in range(devices)])  2.92 us
  transfers between devices with their start and end apart: 33, of which 17 were waited for; matrix products, arithmetic and copies ran while one was open for 1% of the time, Pallas kernels for 29%

profile of v3, /device:TPU:0, one launch (start us, length us, event | category | flops | bytes accessed | tf_op | source)
XLA Modules:
  0.0 82.5 jit_solution(6833983484358228622)
XLA Ops:
  0.6 0.5 collective-permute-start.2
  1.1 2.6 %collective-permute-start.1 = (bf16[2,256,256]{2,1,0:T(8,128)(2,1)}, bf16[2,256,256]{2,1,0:T(8,128)(2,1)S(1)}, u32[]{:S(2)}, u32[]{:S(2)}) collective-permute-start(bf16[2,256,256]{2,1,0:T(8,128)(2,1)} %psi_ref.1), channel_id=1, source_target_pairs={{0,2},{1,3},{4,0},{5,1},{8,4},{9,5},{12,8},{13,9},{14,12},{15,13},... | collective-permute-start | bytes 786440 | tf_op jit(solution)/shard_map/ppermute | solution.py:285
  3.7 0.1 collective-permute-start
  3.9 4.1 %shard_map.77 = (f32[8,128]{1,0:T(8,128)S(1)}, f32[33,256,256]{2,1,0:T(8,128)S(1)}, bf16[32,256,256]{2,1,0:T(8,128)(2,1)S(1)}, s32[128]{0:T(128)S(1)}, s32[6]{0:T(128)S(1)}) custom-call(s32[2,92]{1,0:T(2,128)} %bitcast.2, s32[1]{0:T(128)} %bitcast.1.me_ref, bf16[2,256,256]{2,1,0:T(8,128)(2,1)} %psi_ref.1, bf16[3,2,256,256]{3,2,1,0:T(8,128)(2,1)} %lower_ref.1), custom_call_target="tpu_custom_call" | custom-call | bytes 12582912 | tf_op jit(solution)/shard_map/pallas_call | solution.py:324
  8.0 3.8 %shard_map.78 = (f32[33,256,256]{2,1,0:T(8,128)S(1)}, bf16[32,256,256]{2,1,0:T(8,128)(2,1)S(1)}) custom-call(s32[128]{0:T(128)S(1)} %get-tuple-element.63.plan_ref, s32[6]{0:T(128)S(1)} %get-tuple-element.64.bounds_ref, bf16[92,256,256]{2,1,0:T(8,128)(2,1)} %left_hbm.9, ...), custom_call_target="tpu_custom_call", output_to_operand_aliasing={{0}: (6, {}), {1}: (7, {})} | custom-call | flops 1234803072 | bytes 1048576 | tf_op jit(solution)/shard_map/pallas_call | solution.py:368
  11.9 0.4 collective-permute-done.rest_0_
  12.3 0.5 collective-permute-start.5
  12.8 0.1 collective-permute-start.6
  12.9 0.9 %collective-permute-start.3 = (bf16[2,256,256]{2,1,0:T(8,128)(2,1)S(1)}, bf16[2,256,256]{2,1,0:T(8,128)(2,1)S(1)}, u32[]{:S(2)}, u32[]{:S(2)}) collective-permute-start(bf16[2,256,256]{2,1,0:T(8,128)(2,1)S(1)} %collective-permute-done.rest_0_), channel_id=1, source_target_pairs={{0,4},{1,5},{4,8},{5,9},{8,12},{9,13},{12,14},{13,15},{14,10},{15,... | collective-permute-start | bytes 786440 | tf_op jit(solution)/shard_map/ppermute | solution.py:282
  13.9 1.1 %collective-permute-start.4 = (bf16[2,256,256]{2,1,0:T(8,128)(2,1)S(1)}, bf16[2,256,256]{2,1,0:T(8,128)(2,1)S(1)}, u32[]{:S(2)}, u32[]{:S(2)}) collective-permute-start(bf16[2,256,256]{2,1,0:T(8,128)(2,1)S(1)} %collective-permute-done.1.rest_1_), channel_id=1, source_target_pairs={{0,2},{1,3},{4,0},{5,1},{8,4},{9,5},{12,8},{13,9},{14,12},{15,13},... | collective-permute-start | bytes 786440 | tf_op jit(solution)/shard_map/ppermute | solution.py:285
  15.0 3.9 %shard_map.79 = (f32[33,256,256]{2,1,0:T(8,128)S(1)}, bf16[32,256,256]{2,1,0:T(8,128)(2,1)S(1)}) custom-call(s32[128]{0:T(128)S(1)} %get-tuple-element.63.plan_ref, s32[6]{0:T(128)S(1)} %get-tuple-element.64.bounds_ref, bf16[92,256,256]{2,1,0:T(8,128)(2,1)} %left_hbm.9, ...), custom_call_target="tpu_custom_call", output_to_operand_aliasing={{0}: (8, {}), {1}: (9, {})} | custom-call | flops 1234803072 | bytes 1048576 | tf_op jit(solution)/shard_map/pallas_call | solution.py:368
  18.9 2.7 %collective-permute-done.3.rest_0_ = bf16[2,256,256]{2,1,0:T(8,128)(2,1)S(1)} collective-permute-done((bf16[2,256,256]{2,1,0:T(8,128)(2,1)S(1)}, bf16[2,256,256]{2,1,0:T(8,128)(2,1)S(1)}, u32[]{:S(2)}, u32[]{:S(2)}) %collective-permute-start.3) | collective-permute-done | bytes 262176 | tf_op jit(solution)/shard_map/ppermute | solution.py:282
  21.6 0.7 collective-permute-done.4.rest_1_
  22.2 0.5 collective-permute-start.10
  22.7 2.4 %collective-permute-start.7 = (bf16[2,256,256]{2,1,0:T(8,128)(2,1)S(1)}, bf16[2,256,256]{2,1,0:T(8,128)(2,1)S(1)}, u32[]{:S(2)}, u32[]{:S(2)}) collective-permute-start(bf16[2,256,256]{2,1,0:T(8,128)(2,1)S(1)} %collective-permute-done.3.rest_0_), channel_id=1, source_target_pairs={{0,4},{1,5},{4,8},{5,9},{8,12},{9,13},{12,14},{13,15},{14,10},{15,... | collective-permute-start | bytes 786440 | tf_op jit(solution)/shard_map/ppermute | solution.py:282
  25.1 4.7 %shard_map.80 = (f32[33,256,256]{2,1,0:T(8,128)S(1)}, bf16[32,256,256]{2,1,0:T(8,128)(2,1)S(1)}) custom-call(s32[128]{0:T(128)S(1)} %get-tuple-element.63.plan_ref, s32[6]{0:T(128)S(1)} %get-tuple-element.64.bounds_ref, bf16[92,256,256]{2,1,0:T(8,128)(2,1)} %left_hbm.9, ...), custom_call_target="tpu_custom_call", output_to_operand_aliasing={{0}: (8, {}), {1}: (9, {})} | custom-call | flops 1234803072 | bytes 1048576 | tf_op jit(solution)/shard_map/pallas_call | solution.py:368
  29.9 1.1 %collective-permute-done.7.rest_0_ = bf16[2,256,256]{2,1,0:T(8,128)(2,1)S(1)} collective-permute-done((bf16[2,256,256]{2,1,0:T(8,128)(2,1)S(1)}, bf16[2,256,256]{2,1,0:T(8,128)(2,1)S(1)}, u32[]{:S(2)}, u32[]{:S(2)}) %collective-permute-start.7) | collective-permute-done | bytes 262176 | tf_op jit(solution)/shard_map/ppermute | solution.py:282
  31.0 2.1 %collective-permute-done.8.rest_1_ = bf16[2,256,256]{2,1,0:T(8,128)(2,1)S(1)} collective-permute-done((bf16[2,256,256]{2,1,0:T(8,128)(2,1)S(1)}, bf16[2,256,256]{2,1,0:T(8,128)(2,1)S(1)}, u32[]{:S(2)}, u32[]{:S(2)}) %collective-permute-start.8) | collective-permute-done | bytes 262176 | tf_op jit(solution)/shard_map/ppermute | solution.py:285
  33.1 0.5 collective-permute-start.14
  33.6 0.0 copy-start.2
  33.6 0.3 collective-permute-start.12
  34.0 1.7 %collective-permute-start.11 = (bf16[1,256,256]{2,1,0:T(8,128)(2,1)S(1)}, bf16[1,256,256]{2,1,0:T(8,128)(2,1)S(1)}, u32[]{:S(2)}, u32[]{:S(2)}) collective-permute-start(bf16[1,256,256]{2,1,0:T(8,128)(2,1)S(1)} %slice.6), channel_id=1, source_target_pairs={{0,4},{1,5},{4,8},{5,9},{8,12},{9,13},{12,14},{13,15},{14,10},{15,... | collective-permute-start | bytes 393224 | tf_op jit(solution)/shard_map/ppermute | solution.py:282
  35.7 6.3 %shard_map.81 = (f32[33,256,256]{2,1,0:T(8,128)S(1)}, bf16[32,256,256]{2,1,0:T(8,128)(2,1)S(1)}) custom-call(s32[128]{0:T(128)S(1)} %get-tuple-element.63.plan_ref, s32[6]{0:T(128)S(1)} %get-tuple-element.64.bounds_ref, bf16[92,256,256]{2,1,0:T(8,128)(2,1)} %left_hbm.9, ...), custom_call_target="tpu_custom_call", output_to_operand_aliasing={{0}: (8, {}), {1}: (9, {})} | custom-call | flops 1234803072 | bytes 1048576 | tf_op jit(solution)/shard_map/pallas_call | solution.py:368
  42.1 0.1 collective-permute-start.15
  42.1 0.5 collective-permute-start.16
  42.6 0.8 %collective-permute-done.15.rest_2_ = bf16[1,256,256]{2,1,0:T(8,128)(2,1)S(1)} collective-permute-done((bf16[1,256,256]{2,1,0:T(8,128)(2,1)S(1)}, bf16[1,256,256]{2,1,0:T(8,128)(2,1)S(1)}, u32[]{:S(2)}, u32[]{:S(2)}) %collective-permute-start.15) | collective-permute-done | bytes 131104 | tf_op jit(solution)/shard_map/ppermute | solution.py:288
  43.5 0.2 collective-permute-done.16.rest_3_
  43.7 6.7 %shard_map.82 = (f32[33,256,256]{2,1,0:T(8,128)S(1)}, bf16[32,256,256]{2,1,0:T(8,128)(2,1)S(1)}, f32[4,272,256]{2,1,0:T(8,128)S(1)}, f32[12,272,256]{2,1,0:T(8,1...) custom-call(s32[128]{0:T(128)S(1)} %get-tuple-element.63.plan_ref, ...), custom_call_target="tpu_custom_call", output_to_operand_aliasing={{0}: (10, {}), {1}: (11, {})} | custom-call | flops 1234803072 | bytes 1048576 | tf_op jit(solution)/shard_map/pallas_call | solution.py:368
  50.3 0.1 collective-permute-start.17
  50.4 2.7 %collective-permute-done.17.other = f32[4,272,256]{2,1,0:T(8,128)S(1)} collective-permute-done((f32[4,272,256]{2,1,0:T(8,128)S(1)}, f32[4,272,256]{2,1,0:T(8,128)S(1)}, u32[]{:S(2)}, u32[]{:S(2)}) %collective-permute-start.17) | collective-permute-done | bytes 1114144 | tf_op jit(solution)/shard_map/ppermute | solution.py:288
  53.2 0.1 collective-permute-start.18
  53.3 0.2 shard_map.84
  53.5 0.1 collective-permute-start.20
  53.6 2.0 %collective-permute-start.19 = (f16[1,272,256]{2,1,0:T(8,128)(2,1)S(1)}, f16[1,272,256]{2,1,0:T(8,128)(2,1)S(1)}, u32[]{:S(2)}, u32[]{:S(2)}) collective-permute-start(f16[1,272,256]{2,1,0:T(8,128)(2,1)S(1)} %convert_element_type.84), channel_id=1, source_target_pairs={{0,4},{1,5},{4,8},{5,9},{8,12},{9,13},{12,14},{13,15},{14,10},{15,... | collective-permute-start | bytes 417800 | tf_op jit(solution)/shard_map/ppermute | solution.py:282
  55.7 0.1 collective-permute-start.24
  55.8 2.0 %collective-permute-start.23 = (f16[1,272,256]{2,1,0:T(8,128)(2,1)S(1)}, f16[1,272,256]{2,1,0:T(8,128)(2,1)S(1)}, u32[]{:S(2)}, u32[]{:S(2)}) collective-permute-start(f16[1,272,256]{2,1,0:T(8,128)(2,1)S(1)} %convert_element_type.86), channel_id=1, source_target_pairs={{0,4},{1,5},{4,8},{5,9},{8,12},{9,13},{12,14},{13,15},{14,10},{15,... | collective-permute-start | bytes 417800 | tf_op jit(solution)/shard_map/ppermute | solution.py:282
  57.8 2.3 %collective-permute-done.20 = f16[1,272,256]{2,1,0:T(8,128)(2,1)S(1)} collective-permute-done((f16[1,272,256]{2,1,0:T(8,128)(2,1)S(1)}, f16[1,272,256]{2,1,0:T(8,128)(2,1)S(1)}, u32[]{:S(2)}, u32[]{:S(2)}) %collective-permute-start.20) | collective-permute-done | bytes 139296 | tf_op jit(solution)/shard_map/ppermute | solution.py:285
  60.1 0.1 collective-permute-done.19
  60.2 0.5 shard_map.83
  60.7 0.0 copy-start
  60.7 0.1 add_convert_fusion.9
  60.8 2.1 %collective-permute-start.21 = (f16[1,272,256]{2,1,0:T(8,128)(2,1)S(1)}, f16[1,272,256]{2,1,0:T(8,128)(2,1)S(1)}, u32[]{:S(2)}, u32[]{:S(2)}) collective-permute-start(f16[1,272,256]{2,1,0:T(8,128)(2,1)S(1)} %add_convert_fusion.9), channel_id=1, source_target_pairs={{0,4},{1,5},{4,8},{5,9},{8,12},{9,13},{12,14},{13,15},{14,10},{15,... | collective-permute-start | bytes 417800 | tf_op jit(solution)/shard_map/ppermute | solution.py:282
  62.8 0.1 add_convert_fusion.8
  62.9 0.1 collective-permute-start.22
  63.0 0.1 add_convert_fusion.7
  63.0 2.0 %collective-permute-start.27 = (f16[1,272,256]{2,1,0:T(8,128)(2,1)S(1)}, f16[1,272,256]{2,1,0:T(8,128)(2,1)S(1)}, u32[]{:S(2)}, u32[]{:S(2)}) collective-permute-start(f16[1,272,256]{2,1,0:T(8,128)(2,1)S(1)} %add_convert_fusion.7), channel_id=1, source_target_pairs={{0,4},{1,5},{4,8},{5,9},{8,12},{9,13},{12,14},{13,15},{14,10},{15,... | collective-permute-start | bytes 417800 | tf_op jit(solution)/shard_map/ppermute | solution.py:282
  65.1 0.1 collective-permute-start.28
  65.2 1.8 %collective-permute-done.21 = f16[1,272,256]{2,1,0:T(8,128)(2,1)S(1)} collective-permute-done((f16[1,272,256]{2,1,0:T(8,128)(2,1)S(1)}, f16[1,272,256]{2,1,0:T(8,128)(2,1)S(1)}, u32[]{:S(2)}, u32[]{:S(2)}) %collective-permute-start.21) | collective-permute-done | bytes 139296 | tf_op jit(solution)/shard_map/ppermute | solution.py:282
  67.0 2.4 %collective-permute-done.22 = f16[1,272,256]{2,1,0:T(8,128)(2,1)S(1)} collective-permute-done((f16[1,272,256]{2,1,0:T(8,128)(2,1)S(1)}, f16[1,272,256]{2,1,0:T(8,128)(2,1)S(1)}, u32[]{:S(2)}, u32[]{:S(2)}) %collective-permute-start.22) | collective-permute-done | bytes 139296 | tf_op jit(solution)/shard_map/ppermute | solution.py:285
  69.4 0.1 add_convert_fusion.4
  69.5 0.1 collective-permute-start.26
  69.6 2.1 %collective-permute-start.25 = (f16[1,272,256]{2,1,0:T(8,128)(2,1)S(1)}, f16[1,272,256]{2,1,0:T(8,128)(2,1)S(1)}, u32[]{:S(2)}, u32[]{:S(2)}) collective-permute-start(f16[1,272,256]{2,1,0:T(8,128)(2,1)S(1)} %add_convert_fusion.5), channel_id=1, source_target_pairs={{0,4},{1,5},{4,8},{5,9},{8,12},{9,13},{12,14},{13,15},{14,10},{15,... | collective-permute-start | bytes 417800 | tf_op jit(solution)/shard_map/ppermute | solution.py:282
  71.6 0.6 collective-permute-done.28
  72.3 0.1 add_convert_fusion.3
  72.3 0.4 collective-permute-start.30
  72.7 1.8 %collective-permute-start.31 = (f16[1,272,256]{2,1,0:T(8,128)(2,1)S(1)}, f16[1,272,256]{2,1,0:T(8,128)(2,1)S(1)}, u32[]{:S(2)}, u32[]{:S(2)}) collective-permute-start(f16[1,272,256]{2,1,0:T(8,128)(2,1)S(1)} %add_convert_fusion.2), channel_id=1, source_target_pairs={{0,2},{1,3},{4,0},{5,1},{8,4},{9,5},{12,8},{13,9},{14,12},{15,13},... | collective-permute-start | bytes 417800 | tf_op jit(solution)/shard_map/ppermute | solution.py:285
  74.5 1.0 %collective-permute-done.26 = f16[1,272,256]{2,1,0:T(8,128)(2,1)S(1)} collective-permute-done((f16[1,272,256]{2,1,0:T(8,128)(2,1)S(1)}, f16[1,272,256]{2,1,0:T(8,128)(2,1)S(1)}, u32[]{:S(2)}, u32[]{:S(2)}) %collective-permute-start.26) | collective-permute-done | bytes 139296 | tf_op jit(solution)/shard_map/ppermute | solution.py:285
  75.6 0.4 collective-permute-start.32
  76.0 0.1 add_convert_fusion.1
  76.1 1.7 %collective-permute-start.29 = (f16[1,272,256]{2,1,0:T(8,128)(2,1)S(1)}, f16[1,272,256]{2,1,0:T(8,128)(2,1)S(1)}, u32[]{:S(2)}, u32[]{:S(2)}) collective-permute-start(f16[1,272,256]{2,1,0:T(8,128)(2,1)S(1)} %add_convert_fusion.1), channel_id=1, source_target_pairs={{0,4},{1,5},{4,8},{5,9},{8,12},{9,13},{12,14},{13,15},{14,10},{15,... | collective-permute-start | bytes 417800 | tf_op jit(solution)/shard_map/ppermute | solution.py:282
  77.8 0.2 collective-permute-done.30
  78.0 2.6 %collective-permute-done.32 = f16[1,272,256]{2,1,0:T(8,128)(2,1)S(1)} collective-permute-done((f16[1,272,256]{2,1,0:T(8,128)(2,1)S(1)}, f16[1,272,256]{2,1,0:T(8,128)(2,1)S(1)}, u32[]{:S(2)}, u32[]{:S(2)}) %collective-permute-start.32) | collective-permute-done | bytes 139296 | tf_op jit(solution)/shard_map/ppermute | solution.py:285
  80.7 0.5 collective-permute-done.29
  81.2 1.3 %shard_map.85 = (f32[2,256,256]{2,1,0:T(8,128)}, f32[1]{0:T(128)}) custom-call(f32[3,8,128]{2,1,0:T(8,128)S(1)} %copy-done.2, f32[8,128]{1,0:T(8,128)S(1)} %get-tuple-element.92.scales, f32[2,272,256]{2,1,0:T(8,128)S(1)} %get-tuple-element.98.home, f32[1,272,256]{2,1,0:T(8,128)S(1)} %convert_element_type.106.r0, ...), custom_call_target="tpu_custom_call" | custom-call | bytes 2097152 | tf_op jit(solution)/shard_map/pallas_call | solution.py:428
  (37 shorter events, 0.4 us)
Async XLA Ops:
  0.6 7.4 %collective-permute-start.2 = (bf16[2,256,256]{2,1,0:T(8,128)(2,1)}, bf16[2,256,256]{2,1,0:T(8,128)(2,1)S(1)}, u32[]{:S(2)}, u32[]{:S(2)}) collective-permute-start(bf16[2,256,256]{2,1,0:T(8,128)(2,1)} %psi_ref.1), channel_id=1, source_target_pairs={{0,1},{1,0},{2,3},{3,2},{4,5},{5,4},{6,7},{7,6},{8,9},{9,8},{10,11... | collective-permute-start | bytes 786440 | tf_op jit(solution)/shard_map/ppermute | solution.py:288
  1.1 10.7 %collective-permute-start.1 = (bf16[2,256,256]{2,1,0:T(8,128)(2,1)}, bf16[2,256,256]{2,1,0:T(8,128)(2,1)S(1)}, u32[]{:S(2)}, u32[]{:S(2)}) collective-permute-start(bf16[2,256,256]{2,1,0:T(8,128)(2,1)} %psi_ref.1), channel_id=1, source_target_pairs={{0,2},{1,3},{4,0},{5,1},{8,4},{9,5},{12,8},{13,9},{14,12},{15,13},... | collective-permute-start | bytes 786440 | tf_op jit(solution)/shard_map/ppermute | solution.py:285
  3.7 8.6 %collective-permute-start = (bf16[2,256,256]{2,1,0:T(8,128)(2,1)}, bf16[2,256,256]{2,1,0:T(8,128)(2,1)S(1)}, u32[]{:S(2)}, u32[]{:S(2)}) collective-permute-start(bf16[2,256,256]{2,1,0:T(8,128)(2,1)} %psi_ref.1), channel_id=1, source_target_pairs={{0,4},{1,5},{4,8},{5,9},{8,12},{9,13},{12,14},{13,15},{14,10},{15,... | collective-permute-start | bytes 786440 | tf_op jit(solution)/shard_map/ppermute | solution.py:282
  12.3 2.6 %collective-permute-start.5 = (bf16[2,256,256]{2,1,0:T(8,128)(2,1)S(1)}, bf16[2,256,256]{2,1,0:T(8,128)(2,1)S(1)}, u32[]{:S(2)}, u32[]{:S(2)}) collective-permute-start(bf16[2,256,256]{2,1,0:T(8,128)(2,1)S(1)} %collective-permute-done.rest_0_), channel_id=1, source_target_pairs={{0,1},{1,0},{2,3},{3,2},{4,5},{5,4},{6,7},{7,6},{8,9},{9,8},{10,11... | collective-permute-start | bytes 786440 | tf_op jit(solution)/shard_map/ppermute | solution.py:288
  12.8 2.1 %collective-permute-start.6 = (bf16[2,256,256]{2,1,0:T(8,128)(2,1)S(1)}, bf16[2,256,256]{2,1,0:T(8,128)(2,1)S(1)}, u32[]{:S(2)}, u32[]{:S(2)}) collective-permute-start(bf16[2,256,256]{2,1,0:T(8,128)(2,1)S(1)} %collective-permute-done.1.rest_1_), channel_id=1, source_target_pairs={{0,1},{1,0},{2,3},{3,2},{4,5},{5,4},{6,7},{7,6},{8,9},{9,8},{10,11... | collective-permute-start | bytes 786440 | tf_op jit(solution)/shard_map/ppermute | solution.py:288
  12.9 8.7 %collective-permute-start.3 = (bf16[2,256,256]{2,1,0:T(8,128)(2,1)S(1)}, bf16[2,256,256]{2,1,0:T(8,128)(2,1)S(1)}, u32[]{:S(2)}, u32[]{:S(2)}) collective-permute-start(bf16[2,256,256]{2,1,0:T(8,128)(2,1)S(1)} %collective-permute-done.rest_0_), channel_id=1, source_target_pairs={{0,4},{1,5},{4,8},{5,9},{8,12},{9,13},{12,14},{13,15},{14,10},{15,... | collective-permute-start | bytes 786440 | tf_op jit(solution)/shard_map/ppermute | solution.py:282
  13.9 8.4 %collective-permute-start.4 = (bf16[2,256,256]{2,1,0:T(8,128)(2,1)S(1)}, bf16[2,256,256]{2,1,0:T(8,128)(2,1)S(1)}, u32[]{:S(2)}, u32[]{:S(2)}) collective-permute-start(bf16[2,256,256]{2,1,0:T(8,128)(2,1)S(1)} %collective-permute-done.1.rest_1_), channel_id=1, source_target_pairs={{0,2},{1,3},{4,0},{5,1},{8,4},{9,5},{12,8},{13,9},{14,12},{15,13},... | collective-permute-start | bytes 786440 | tf_op jit(solution)/shard_map/ppermute | solution.py:285
  22.2 2.9 %collective-permute-start.9 = (bf16[2,256,256]{2,1,0:T(8,128)(2,1)S(1)}, bf16[2,256,256]{2,1,0:T(8,128)(2,1)S(1)}, u32[]{:S(2)}, u32[]{:S(2)}) collective-permute-start(bf16[2,256,256]{2,1,0:T(8,128)(2,1)S(1)} %collective-permute-done.3.rest_0_), channel_id=1, source_target_pairs={{0,1},{1,0},{2,3},{3,2},{4,5},{5,4},{6,7},{7,6},{8,9},{9,8},{10,11... | collective-permute-start | bytes 786440 | tf_op jit(solution)/shard_map/ppermute | solution.py:288
  22.2 2.9 %collective-permute-start.10 = (bf16[2,256,256]{2,1,0:T(8,128)(2,1)S(1)}, bf16[2,256,256]{2,1,0:T(8,128)(2,1)S(1)}, u32[]{:S(2)}, u32[]{:S(2)}) collective-permute-start(bf16[2,256,256]{2,1,0:T(8,128)(2,1)S(1)} %collective-permute-done.4.rest_1_), channel_id=1, source_target_pairs={{0,1},{1,0},{2,3},{3,2},{4,5},{5,4},{6,7},{7,6},{8,9},{9,8},{10,11... | collective-permute-start | bytes 786440 | tf_op jit(solution)/shard_map/ppermute | solution.py:288
  22.7 8.2 %collective-permute-start.7 = (bf16[2,256,256]{2,1,0:T(8,128)(2,1)S(1)}, bf16[2,256,256]{2,1,0:T(8,128)(2,1)S(1)}, u32[]{:S(2)}, u32[]{:S(2)}) collective-permute-start(bf16[2,256,256]{2,1,0:T(8,128)(2,1)S(1)} %collective-permute-done.3.rest_0_), channel_id=1, source_target_pairs={{0,4},{1,5},{4,8},{5,9},{8,12},{9,13},{12,14},{13,15},{14,10},{15,... | collective-permute-start | bytes 786440 | tf_op jit(solution)/shard_map/ppermute | solution.py:282
  25.1 7.9 %collective-permute-start.8 = (bf16[2,256,256]{2,1,0:T(8,128)(2,1)S(1)}, bf16[2,256,256]{2,1,0:T(8,128)(2,1)S(1)}, u32[]{:S(2)}, u32[]{:S(2)}) collective-permute-start(bf16[2,256,256]{2,1,0:T(8,128)(2,1)S(1)} %collective-permute-done.4.rest_1_), channel_id=1, source_target_pairs={{0,2},{1,3},{4,0},{5,1},{8,4},{9,5},{12,8},{13,9},{14,12},{15,13},... | collective-permute-start | bytes 786440 | tf_op jit(solution)/shard_map/ppermute | solution.py:285
  33.1 2.6 %collective-permute-start.13 = (bf16[2,256,256]{2,1,0:T(8,128)(2,1)S(1)}, bf16[2,256,256]{2,1,0:T(8,128)(2,1)S(1)}, u32[]{:S(2)}, u32[]{:S(2)}) collective-permute-start(bf16[2,256,256]{2,1,0:T(8,128)(2,1)S(1)} %collective-permute-done.7.rest_0_), channel_id=1, source_target_pairs={{0,1},{1,0},{2,3},{3,2},{4,5},{5,4},{6,7},{7,6},{8,9},{9,8},{10,11... | collective-permute-start | bytes 786440 | tf_op jit(solution)/shard_map/ppermute | solution.py:288
  33.1 2.6 %collective-permute-start.14 = (bf16[2,256,256]{2,1,0:T(8,128)(2,1)S(1)}, bf16[2,256,256]{2,1,0:T(8,128)(2,1)S(1)}, u32[]{:S(2)}, u32[]{:S(2)}) collective-permute-start(bf16[2,256,256]{2,1,0:T(8,128)(2,1)S(1)} %collective-permute-done.8.rest_1_), channel_id=1, source_target_pairs={{0,1},{1,0},{2,3},{3,2},{4,5},{5,4},{6,7},{7,6},{8,9},{9,8},{10,11... | collective-permute-start | bytes 786440 | tf_op jit(solution)/shard_map/ppermute | solution.py:288
  33.6 10.0 %copy-start.2 = (f32[3,8,128]{2,1,0:T(8,128)S(1)}, f32[3,8,128]{2,1,0:T(8,128)}, u32[]{:S(2)}) copy-start(f32[3,8,128]{2,1,0:T(8,128)} %constant.6.clone.rest_5_.digit_ref) | copy-start | bytes 36868
  33.6 8.4 %collective-permute-start.12 = (bf16[1,256,256]{2,1,0:T(8,128)(2,1)S(1)}, bf16[1,256,256]{2,1,0:T(8,128)(2,1)S(1)}, u32[]{:S(2)}, u32[]{:S(2)}) collective-permute-start(bf16[1,256,256]{2,1,0:T(8,128)(2,1)S(1)} %slice.7), channel_id=1, source_target_pairs={{0,2},{1,3},{4,0},{5,1},{8,4},{9,5},{12,8},{13,9},{14,12},{15,13},... | collective-permute-start | bytes 393224 | tf_op jit(solution)/shard_map/ppermute | solution.py:285
  34.0 8.1 %collective-permute-start.11 = (bf16[1,256,256]{2,1,0:T(8,128)(2,1)S(1)}, bf16[1,256,256]{2,1,0:T(8,128)(2,1)S(1)}, u32[]{:S(2)}, u32[]{:S(2)}) collective-permute-start(bf16[1,256,256]{2,1,0:T(8,128)(2,1)S(1)} %slice.6), channel_id=1, source_target_pairs={{0,4},{1,5},{4,8},{5,9},{8,12},{9,13},{12,14},{13,15},{14,10},{15,... | collective-permute-start | bytes 393224 | tf_op jit(solution)/shard_map/ppermute | solution.py:282
  42.1 1.4 %collective-permute-start.15 = (bf16[1,256,256]{2,1,0:T(8,128)(2,1)S(1)}, bf16[1,256,256]{2,1,0:T(8,128)(2,1)S(1)}, u32[]{:S(2)}, u32[]{:S(2)}) collective-permute-start(bf16[1,256,256]{2,1,0:T(8,128)(2,1)S(1)} %collective-permute-done.11.rest_0_), channel_id=1, source_target_pairs={{0,1},{1,0},{2,3},{3,2},{4,5},{5,4},{6,7},{7,6},{8,9},{9,8},{10,11... | collective-permute-start | bytes 393224 | tf_op jit(solution)/shard_map/ppermute | solution.py:288
  42.1 1.5 %collective-permute-start.16 = (bf16[1,256,256]{2,1,0:T(8,128)(2,1)S(1)}, bf16[1,256,256]{2,1,0:T(8,128)(2,1)S(1)}, u32[]{:S(2)}, u32[]{:S(2)}) collective-permute-start(bf16[1,256,256]{2,1,0:T(8,128)(2,1)S(1)} %collective-permute-done.12.rest_1_), channel_id=1, source_target_pairs={{0,1},{1,0},{2,3},{3,2},{4,5},{5,4},{6,7},{7,6},{8,9},{9,8},{10,11... | collective-permute-start | bytes 393224 | tf_op jit(solution)/shard_map/ppermute | solution.py:288
  50.3 2.8 %collective-permute-start.17 = (f32[4,272,256]{2,1,0:T(8,128)S(1)}, f32[4,272,256]{2,1,0:T(8,128)S(1)}, u32[]{:S(2)}, u32[]{:S(2)}) collective-permute-start(f32[4,272,256]{2,1,0:T(8,128)S(1)} %get-tuple-element.94), channel_id=1, source_target_pairs={{0,1},{1,0},{2,3},{3,2},{4,5},{5,4},{6,7},{7,6},{8,9},{9,8},{10,11... | collective-permute-start | bytes 3342344 | tf_op jit(solution)/shard_map/ppermute | solution.py:288
  53.2 7.0 %collective-permute-start.18 = (f32[12,272,256]{2,1,0:T(8,128)S(1)}, f32[12,272,256]{2,1,0:T(8,128)S(1)}, u32[]{:S(2)}, u32[]{:S(2)}) collective-permute-start(f32[12,272,256]{2,1,0:T(8,128)S(1)} %get-tuple-element.96), channel_id=1, source_target_pairs={{0,1},{1,0},{2,3},{3,2},{4,5},{5,4},{6,7},{7,6},{8,9},{9,8},{10,11... | collective-permute-start | bytes 10027016 | tf_op jit(solution)/shard_map/ppermute | solution.py:288
  53.5 6.6 %collective-permute-start.20 = (f16[1,272,256]{2,1,0:T(8,128)(2,1)S(1)}, f16[1,272,256]{2,1,0:T(8,128)(2,1)S(1)}, u32[]{:S(2)}, u32[]{:S(2)}) collective-permute-start(f16[1,272,256]{2,1,0:T(8,128)(2,1)S(1)} %convert_element_type.85), channel_id=1, source_target_pairs={{0,2},{1,3},{4,0},{5,1},{8,4},{9,5},{12,8},{13,9},{14,12},{15,13},... | collective-permute-start | bytes 417800 | tf_op jit(solution)/shard_map/ppermute | solution.py:285
  53.6 6.6 %collective-permute-start.19 = (f16[1,272,256]{2,1,0:T(8,128)(2,1)S(1)}, f16[1,272,256]{2,1,0:T(8,128)(2,1)S(1)}, u32[]{:S(2)}, u32[]{:S(2)}) collective-permute-start(f16[1,272,256]{2,1,0:T(8,128)(2,1)S(1)} %convert_element_type.84), channel_id=1, source_target_pairs={{0,4},{1,5},{4,8},{5,9},{8,12},{9,13},{12,14},{13,15},{14,10},{15,... | collective-permute-start | bytes 417800 | tf_op jit(solution)/shard_map/ppermute | solution.py:282
  55.7 7.3 %collective-permute-start.24 = (f16[1,272,256]{2,1,0:T(8,128)(2,1)S(1)}, f16[1,272,256]{2,1,0:T(8,128)(2,1)S(1)}, u32[]{:S(2)}, u32[]{:S(2)}) collective-permute-start(f16[1,272,256]{2,1,0:T(8,128)(2,1)S(1)} %convert_element_type.87), channel_id=1, source_target_pairs={{0,2},{1,3},{4,0},{5,1},{8,4},{9,5},{12,8},{13,9},{14,12},{15,13},... | collective-permute-start | bytes 417800 | tf_op jit(solution)/shard_map/ppermute | solution.py:285
  55.8 7.2 %collective-permute-start.23 = (f16[1,272,256]{2,1,0:T(8,128)(2,1)S(1)}, f16[1,272,256]{2,1,0:T(8,128)(2,1)S(1)}, u32[]{:S(2)}, u32[]{:S(2)}) collective-permute-start(f16[1,272,256]{2,1,0:T(8,128)(2,1)S(1)} %convert_element_type.86), channel_id=1, source_target_pairs={{0,4},{1,5},{4,8},{5,9},{8,12},{9,13},{12,14},{13,15},{14,10},{15,... | collective-permute-start | bytes 417800 | tf_op jit(solution)/shard_map/ppermute | solution.py:282
  60.7 20.5 %copy-start = (bf16[3,2,256,256]{3,2,1,0:T(8,128)(2,1)S(1)}, bf16[3,2,256,256]{3,2,1,0:T(8,128)(2,1)}, u32[]{:S(2)}) copy-start(bf16[3,2,256,256]{3,2,1,0:T(8,128)(2,1)} %lower_ref.1) | copy-start | bytes 2359300
  60.7 20.5 %copy-start.1 = (bf16[2,256,256]{2,1,0:T(8,128)(2,1)S(1)}, bf16[2,256,256]{2,1,0:T(8,128)(2,1)}, u32[]{:S(2)}) copy-start(bf16[2,256,256]{2,1,0:T(8,128)(2,1)} %psi_ref.1) | copy-start | bytes 786436
  60.8 6.2 %collective-permute-start.21 = (f16[1,272,256]{2,1,0:T(8,128)(2,1)S(1)}, f16[1,272,256]{2,1,0:T(8,128)(2,1)S(1)}, u32[]{:S(2)}, u32[]{:S(2)}) collective-permute-start(f16[1,272,256]{2,1,0:T(8,128)(2,1)S(1)} %add_convert_fusion.9), channel_id=1, source_target_pairs={{0,4},{1,5},{4,8},{5,9},{8,12},{9,13},{12,14},{13,15},{14,10},{15,... | collective-permute-start | bytes 417800 | tf_op jit(solution)/shard_map/ppermute | solution.py:282
  62.9 6.5 %collective-permute-start.22 = (f16[1,272,256]{2,1,0:T(8,128)(2,1)S(1)}, f16[1,272,256]{2,1,0:T(8,128)(2,1)S(1)}, u32[]{:S(2)}, u32[]{:S(2)}) collective-permute-start(f16[1,272,256]{2,1,0:T(8,128)(2,1)S(1)} %add_convert_fusion.8), channel_id=1, source_target_pairs={{0,2},{1,3},{4,0},{5,1},{8,4},{9,5},{12,8},{13,9},{14,12},{15,13},... | collective-permute-start | bytes 417800 | tf_op jit(solution)/shard_map/ppermute | solution.py:285
  63.0 8.6 %collective-permute-start.27 = (f16[1,272,256]{2,1,0:T(8,128)(2,1)S(1)}, f16[1,272,256]{2,1,0:T(8,128)(2,1)S(1)}, u32[]{:S(2)}, u32[]{:S(2)}) collective-permute-start(f16[1,272,256]{2,1,0:T(8,128)(2,1)S(1)} %add_convert_fusion.7), channel_id=1, source_target_pairs={{0,4},{1,5},{4,8},{5,9},{8,12},{9,13},{12,14},{13,15},{14,10},{15,... | collective-permute-start | bytes 417800 | tf_op jit(solution)/shard_map/ppermute | solution.py:282
  65.1 7.1 %collective-permute-start.28 = (f16[1,272,256]{2,1,0:T(8,128)(2,1)S(1)}, f16[1,272,256]{2,1,0:T(8,128)(2,1)S(1)}, u32[]{:S(2)}, u32[]{:S(2)}) collective-permute-start(f16[1,272,256]{2,1,0:T(8,128)(2,1)S(1)} %add_convert_fusion.6), channel_id=1, source_target_pairs={{0,2},{1,3},{4,0},{5,1},{8,4},{9,5},{12,8},{13,9},{14,12},{15,13},... | collective-permute-start | bytes 417800 | tf_op jit(solution)/shard_map/ppermute | solution.py:285
  69.5 6.1 %collective-permute-start.26 = (f16[1,272,256]{2,1,0:T(8,128)(2,1)S(1)}, f16[1,272,256]{2,1,0:T(8,128)(2,1)S(1)}, u32[]{:S(2)}, u32[]{:S(2)}) collective-permute-start(f16[1,272,256]{2,1,0:T(8,128)(2,1)S(1)} %add_convert_fusion.4), channel_id=1, source_target_pairs={{0,2},{1,3},{4,0},{5,1},{8,4},{9,5},{12,8},{13,9},{14,12},{15,13},... | collective-permute-start | bytes 417800 | tf_op jit(solution)/shard_map/ppermute | solution.py:285
  69.6 5.9 %collective-permute-start.25 = (f16[1,272,256]{2,1,0:T(8,128)(2,1)S(1)}, f16[1,272,256]{2,1,0:T(8,128)(2,1)S(1)}, u32[]{:S(2)}, u32[]{:S(2)}) collective-permute-start(f16[1,272,256]{2,1,0:T(8,128)(2,1)S(1)} %add_convert_fusion.5), channel_id=1, source_target_pairs={{0,4},{1,5},{4,8},{5,9},{8,12},{9,13},{12,14},{13,15},{14,10},{15,... | collective-permute-start | bytes 417800 | tf_op jit(solution)/shard_map/ppermute | solution.py:282
  72.3 5.6 %collective-permute-start.30 = (f16[1,272,256]{2,1,0:T(8,128)(2,1)S(1)}, f16[1,272,256]{2,1,0:T(8,128)(2,1)S(1)}, u32[]{:S(2)}, u32[]{:S(2)}) collective-permute-start(f16[1,272,256]{2,1,0:T(8,128)(2,1)S(1)} %add_convert_fusion.3), channel_id=1, source_target_pairs={{0,4},{1,5},{4,8},{5,9},{8,12},{9,13},{12,14},{13,15},{14,10},{15,... | collective-permute-start | bytes 417800 | tf_op jit(solution)/shard_map/ppermute | solution.py:282
  72.7 5.3 %collective-permute-start.31 = (f16[1,272,256]{2,1,0:T(8,128)(2,1)S(1)}, f16[1,272,256]{2,1,0:T(8,128)(2,1)S(1)}, u32[]{:S(2)}, u32[]{:S(2)}) collective-permute-start(f16[1,272,256]{2,1,0:T(8,128)(2,1)S(1)} %add_convert_fusion.2), channel_id=1, source_target_pairs={{0,2},{1,3},{4,0},{5,1},{8,4},{9,5},{12,8},{13,9},{14,12},{15,13},... | collective-permute-start | bytes 417800 | tf_op jit(solution)/shard_map/ppermute | solution.py:285
  75.6 5.1 %collective-permute-start.32 = (f16[1,272,256]{2,1,0:T(8,128)(2,1)S(1)}, f16[1,272,256]{2,1,0:T(8,128)(2,1)S(1)}, u32[]{:S(2)}, u32[]{:S(2)}) collective-permute-start(f16[1,272,256]{2,1,0:T(8,128)(2,1)S(1)} %add_convert_fusion), channel_id=1, source_target_pairs={{0,2},{1,3},{4,0},{5,1},{8,4},{9,5},{12,8},{13,9},{14,12},{15,13},... | collective-permute-start | bytes 417800 | tf_op jit(solution)/shard_map/ppermute | solution.py:285
  76.1 5.1 %collective-permute-start.29 = (f16[1,272,256]{2,1,0:T(8,128)(2,1)S(1)}, f16[1,272,256]{2,1,0:T(8,128)(2,1)S(1)}, u32[]{:S(2)}, u32[]{:S(2)}) collective-permute-start(f16[1,272,256]{2,1,0:T(8,128)(2,1)S(1)} %add_convert_fusion.1), channel_id=1, source_target_pairs={{0,4},{1,5},{4,8},{5,9},{8,12},{9,13},{12,14},{13,15},{14,10},{15,... | collective-permute-start | bytes 417800 | tf_op jit(solution)/shard_map/ppermute | solution.py:282

commit v4 on v3

--- a/solution.py
+++ b/solution.py
@@ -11,7 +11,7 @@
 shift_energy = 2.0
 CORES = 2
 BATCH = 8
-SLOTS = 4
+SLOTS = 3
 KEEP = pl.BlockSpec(memory_space=pltpu.VMEM)
 SCALAR = pl.BlockSpec(memory_space=pltpu.SMEM)
 INHBM = pl.BlockSpec(memory_space=pltpu.HBM)
@@ -46,29 +46,27 @@
     return copies
 
 
-def terms_of(begin, end, plan_ref, left_hbm, right_hbm, held, sems, ready, psi, acc):
+def terms_of(begin, end, plan_ref, left, right_hbm, held, sems, ready, psi, acc):
     def bring(i):
         @pl.when(i < end)
         def _():
             at = left_over(i, SLOTS)
             ks = [over(plan_ref[i * BATCH + u], 65536) for u in range(BATCH)]
-            for n, env in enumerate((left_hbm, right_hbm)):
-                for u, k in enumerate(ks):
-                    pltpu.make_async_copy(env.at[k], held.at[at, n, u], sems.at[at, n]).start()
+            for u, k in enumerate(ks):
+                pltpu.make_async_copy(right_hbm.at[k], held.at[at, u], sems.at[at]).start()
 
     def batch(i, carry):
         bring(i + SLOTS - 1)
         at = left_over(i, SLOTS)
-        for n in range(2):
-            pltpu.make_async_copy(held.at[at, n], held.at[at, n], sems.at[at, n]).wait()
+        pltpu.make_async_copy(held.at[at], held.at[at], sems.at[at]).wait()
         codes = [plan_ref[i * BATCH + u] for u in range(BATCH)]
         halves = [
             jnp.dot(
-                held[at, 0, u], psi[left_over(over(c, 256), 256)], preferred_element_type=jnp.float32
+                left[over(c, 65536)], psi[left_over(over(c, 256), 256)], preferred_element_type=jnp.float32
             ).astype(jnp.bfloat16)
-            for u, c in enumerate(codes)
+            for c in codes
         ]
-        whole = [jnp.dot(h, held[at, 1, u], preferred_element_type=jnp.float32) for u, h in enumerate(halves)]
+        whole = [jnp.dot(h, held[at, u], preferred_element_type=jnp.float32) for u, h in enumerate(halves)]
         for c, w in zip(codes, whole):
             acc[left_over(c, 256)] += w
         return carry
@@ -81,8 +79,8 @@
 
 
 def plan_kernel(
-    shape, tl_hbm, me_ref, psi_hbm, lower_hbm,
-    vec, acc, psi, plan, bounds, tl_ref, psi_ref, lower_ref, codes, kinds, fill, small_sems,
+    shape, tl_hbm, me_ref, psi_hbm, lower_hbm, left_hbm,
+    left, vec, acc, psi, plan, bounds, tl_ref, psi_ref, lower_ref, codes, kinds, fill, small_sems, sems,
 ):
     chips, rows_y, per, cap, empty = shape
     terms = tl_ref.shape[1]
@@ -93,7 +91,12 @@
         pltpu.make_async_copy(a, b, small_sems.at[n])
         for n, (a, b) in enumerate(((tl_hbm, tl_ref), (psi_hbm, psi_ref), (lower_hbm, lower_ref)))
     ]
-    for copy in small:
+    group = terms // sems.shape[0]
+    copies = [
+        pltpu.make_async_copy(left_hbm.at[pl.ds(g * group, group)], left.at[pl.ds(g * group, group)], sems.at[g])
+        for g in range(sems.shape[0])
+    ]
+    for copy in small + copies:
         copy.start()
     small[0].wait()
 
@@ -117,7 +120,7 @@
     def classify(k, carry):
         rel, src = slot(tl_ref[0, k])
         _, dst = slot(tl_ref[1, k])
-        stage = jnp.minimum(rel, chips - rel)
+        stage = jnp.maximum(jnp.minimum(rel, chips - rel), 1)
         codes[k] = k * 65536 + src * 256 + dst
         kinds[k] = stage
         fill[stage] += 1
@@ -173,9 +176,11 @@
     vec[...] = jnp.zeros_like(vec)
     for i, x in enumerate(parts):
         vec[pl.ds(i, 1), :] = sum(x[:, c : c + 128] for c in range(0, side, 128))
-
-
-def stage_kernel(stage, starts, finish, limit, digit, plan_ref, bounds_ref, left_hbm, right_hbm, *rest):
+    for copy in copies:
+        copy.wait()
+
+
+def stage_kernel(stage, starts, finish, limit, digit, plan_ref, bounds_ref, left, right_hbm, *rest):
     count = len(starts)
     pieces, rest = rest[:count], rest[count:]
     if finish:
@@ -187,7 +192,7 @@
     sems, held, env_sems = rest
     copies = starts_of(pieces, psi, starts, sems)
     begin, end = bounds_ref[stage], bounds_ref[stage + 1]
-    terms_of(begin, end, plan_ref, left_hbm, right_hbm, held, env_sems, copies, psi, acc)
+    terms_of(begin, end, plan_ref, left, right_hbm, held, env_sems, copies, psi, acc)
     if finish:
         side = psi.shape[1]
 
@@ -300,9 +305,10 @@
         tie = lax.optimization_barrier
         me = lax.axis_index("sector")
 
-        keep = dict(compiler_params=pltpu.CompilerParams(vmem_limit_bytes=16 * 1024 * 1024))
+        keep = dict(compiler_params=pltpu.CompilerParams(vmem_limit_bytes=9 * 1024 * 1024))
         stages = reach + 1
         cap = (terms + stages * (BATCH - 1) + BATCH - 1) // BATCH * BATCH
+        groups = next(g for g in (4, 2, 1) if terms % g == 0)
         vec_rows = -(-(2 * lower + 2) // 8) * 8
         left_hbm, right_hbm, psi_hbm, lower_hbm, list_hbm = [
             pltpu.with_memory_space_constraint(x, pltpu.HBM)
@@ -323,9 +329,10 @@
         def make_plan():
             return pl.pallas_call(
                 functools.partial(plan_kernel, (chips, rows_y, per, cap, sectors)),
-                in_specs=[INHBM, SCALAR, INHBM, INHBM],
-                out_specs=[KEEP] * 3 + [SCALAR] * 2,
+                in_specs=[INHBM, SCALAR, INHBM, INHBM, INHBM],
+                out_specs=[KEEP] * 4 + [SCALAR] * 2,
                 out_shape=[
+                    pltpu.VMEM(left_env.shape, left_env.dtype),
                     vec_shape,
                     acc_shape,
                     psi_shape,
@@ -340,10 +347,11 @@
                     pltpu.SMEM((terms,), jnp.int32),
                     pltpu.SMEM((stages,), jnp.int32),
                     pltpu.SemaphoreType.DMA((3,)),
+                    pltpu.SemaphoreType.DMA((groups,)),
                 ],
                 cost_estimate=pl.CostEstimate(flops=0, bytes_accessed=12 << 20, transcendentals=0),
                 **keep,
-            )(list_hbm, me.reshape(1).astype(jnp.int32), psi_hbm, lower_hbm)
+            )(list_hbm, me.reshape(1).astype(jnp.int32), psi_hbm, lower_hbm, left_hbm)
 
         route = [(reach, 0)] + [(d, h) for d in range(reach - 1, 0, -1) for h in (1, 0)]
         route_left = [(-d if d < reach else reach, 1 - h) for d, h in route]
@@ -361,13 +369,13 @@
             if finish:
                 scratch = [pltpu.VMEM((vec_rows, 128), jnp.float32), pltpu.SemaphoreType.DMA((len(need),))] + scratch
             scratch += [
-                pltpu.VMEM((SLOTS, 2, BATCH, side, side), left_env.dtype),
-                pltpu.SemaphoreType.DMA((SLOTS, 2)),
+                pltpu.VMEM((SLOTS, BATCH, side, side), right_env.dtype),
+                pltpu.SemaphoreType.DMA((SLOTS,)),
             ]
             limit = 1.02 * terms * devices * side * side * 0.375 * 0.0546875
             return pl.pallas_call(
                 functools.partial(stage_kernel, stage, starts, finish, limit, 2.0**digit_bits),
-                in_specs=[SCALAR, SCALAR, INHBM, INHBM] + [INHBM if x is psi_hbm else ANYWHERE for x in pieces]
+                in_specs=[SCALAR, SCALAR, KEEP, INHBM] + [INHBM if x is psi_hbm else ANYWHERE for x in pieces]
                 + [KEEP] * (m + 2),
                 out_specs=[KEEP] * 2 + [KEEP] * len(sizes) + [KEEP] * len(small),
                 out_shape=[acc_shape, psi_shape] + sizes + small,
@@ -377,15 +385,16 @@
                     flops=4 * side**3 * terms // stages, bytes_accessed=1 << 20, transcendentals=0
                 ),
                 **keep,
-            )(plan, bounds, left_hbm, right_hbm, *pieces, *more, acc, psi)
+            )(plan, bounds, left_vmem, right_hbm, *pieces, *more, acc, psi)
 
         r, l, sib = right(wavefunction), left(wavefunction), across(wavefunction)
-        vec, acc, psi, plan, bounds = make_plan()
-        acc, psi = run_stage(0, [psi_hbm, sib], [0, base], acc, psi)
+        left_vmem, vec, acc, psi, plan, bounds = make_plan()
+        late, late_at = [psi_hbm, sib], [0, base]
         for s in range(1, reach + 1):
             r, l, acc, psi = tie((r, l, acc, psi))
             rel = [(chips - s) * per, s * per] if s < reach else [reach * per, reach * per + part]
-            held, at = [r, l, across(r), across(l)], rel + [base + x for x in rel]
+            held, at = late + [r, l, across(r), across(l)], late_at + rel + [base + x for x in rel]
+            late, late_at = [], []
             if s < reach - 1:
                 r, l = right(r), left(l)
             elif s < reach:

time: 83.4 us -> 81.8 us (0.981)
  Pallas kernels: 31.6 us -> 29.2 us
  waiting for transfers between devices: 22.4 us -> 23.8 us
    ppermute x11, starting transfers between devices: 6.62 us -> 11.6 us  [left(): return lax.ppermute(x, 'sector', to_left)]
    ppermute x11, starting transfers between devices: 17.4 us -> 12.5 us  [right(): return lax.ppermute(x, 'sector', to_right)]
    pallas_call x5 -> x4, Pallas kernels: 25.4 us -> 21.7 us  [run_stage(): pl.pallas_call(functools.partial(stage_kernel, stage, starts, finish, lim...]
    ppermute x11, waiting for transfers between devices: 6.82 us -> 8.84 us  [right(): return lax.ppermute(x, 'sector', to_right)]
    pallas_call x1, Pallas kernels: 4.13 us -> 5.47 us  [make_plan(): pl.pallas_call(functools.partial(plan_kernel, (chips, rows_y, per, cap, s...]
  transfers between devices with their start and end apart: 33 -> 33, of which waited for: 17 -> 20; matrix products, arithmetic and copies ran while one was open for 1% -> 1% of each run, Pallas kernels for 29% -> 27%
where the time goes in v4:
time: 81.8 us; the launch traced here: 80.9 us
  Pallas kernels  29.2 us (36%)
  starting transfers between devices  26.4 us (32%)
  waiting for transfers between devices  23.8 us (29%)
  between operations  0.88 us (1%)
    pallas_call x4, Pallas kernels, run_stage(): pl.pallas_call(functools.partial(stage_kernel, stage, starts, finish, lim...  21.7 us
    ppermute x11, starting transfers between devices, right(): return lax.ppermute(x, 'sector', to_right)  12.5 us
    ppermute x11, starting transfers between devices, left(): return lax.ppermute(x, 'sector', to_left)  11.6 us
    ppermute x11, waiting for transfers between devices, left(): return lax.ppermute(x, 'sector', to_left)  11.2 us
    ppermute x11, waiting for transfers between devices, right(): return lax.ppermute(x, 'sector', to_right)  8.84 us
    pallas_call x1, Pallas kernels, make_plan(): pl.pallas_call(functools.partial(plan_kernel, (chips, rows_y, per, cap, s...  5.47 us
    ppermute x11, waiting for transfers between devices, pair(): return lax.ppermute(x, 'sector', [(i, i ^ hop) for i in range(devices)])  3.79 us
    ppermute x11, starting transfers between devices, pair(): return lax.ppermute(x, 'sector', [(i, i ^ hop) for i in range(devices)])  2.31 us
  transfers between devices with their start and end apart: 33, of which 20 were waited for; matrix products, arithmetic and copies ran while one was open for 1% of the time, Pallas kernels for 27%

profile of v4, /device:TPU:0, one launch (start us, length us, event | category | flops | bytes accessed | tf_op | source)
XLA Modules:
  0.0 80.9 jit_solution(463567387565676509)
XLA Ops:
  0.6 3.0 %collective-permute-start.1 = (bf16[2,256,256]{2,1,0:T(8,128)(2,1)}, bf16[2,256,256]{2,1,0:T(8,128)(2,1)S(1)}, u32[]{:S(2)}, u32[]{:S(2)}) collective-permute-start(bf16[2,256,256]{2,1,0:T(8,128)(2,1)} %psi_ref.1), channel_id=1, source_target_pairs={{0,2},{1,3},{4,0},{5,1},{8,4},{9,5},{12,8},{13,9},{14,12},{15,13},... | collective-permute-start | bytes 786440 | tf_op jit(solution)/shard_map/ppermute | solution.py:290
  3.6 0.1 collective-permute-start
  3.8 5.5 %shard_map.77 = (bf16[92,256,256]{2,1,0:T(8,128)(2,1)S(1)}, f32[8,128]{1,0:T(8,128)S(1)}, f32[33,256,256]{2,1,0:T(8,128)S(1)}, bf16[32,256,256]{2,1,0:T(8,128)(2,1)S(1)}, s32[128]{0:T(128)S(1)}, /*index=5*/s32[6]{0:T(128)S(1)}) custom-call(s32[2,92]{1,0:T(2,128)} %bitcast.2, s32[1]{0:T(128)} %bitcast.1.me_ref, bf16[2,256,256]{2,1,0:T(8,128)(2,1)} %psi_ref.1, ...), custom_call_target="tpu_custom_call" | custom-call | bytes 12582912 | tf_op jit(solution)/shard_map/pallas_call | solution.py:330
  9.3 1.0 %collective-permute-done.1.rest_3_ = bf16[2,256,256]{2,1,0:T(8,128)(2,1)S(1)} collective-permute-done((bf16[2,256,256]{2,1,0:T(8,128)(2,1)}, bf16[2,256,256]{2,1,0:T(8,128)(2,1)S(1)}, u32[]{:S(2)}, u32[]{:S(2)}) %collective-permute-start.1) | collective-permute-done | bytes 262176 | tf_op jit(solution)/shard_map/ppermute | solution.py:290
  10.2 1.4 %collective-permute-done.rest_2_ = bf16[2,256,256]{2,1,0:T(8,128)(2,1)S(1)} collective-permute-done((bf16[2,256,256]{2,1,0:T(8,128)(2,1)}, bf16[2,256,256]{2,1,0:T(8,128)(2,1)S(1)}, u32[]{:S(2)}, u32[]{:S(2)}) %collective-permute-start) | collective-permute-done | bytes 262176 | tf_op jit(solution)/shard_map/ppermute | solution.py:287
  11.6 0.5 collective-permute-start.6
  12.1 0.4 collective-permute-start.2
  12.5 1.6 %collective-permute-start.3 = (bf16[2,256,256]{2,1,0:T(8,128)(2,1)S(1)}, bf16[2,256,256]{2,1,0:T(8,128)(2,1)S(1)}, u32[]{:S(2)}, u32[]{:S(2)}) collective-permute-start(bf16[2,256,256]{2,1,0:T(8,128)(2,1)S(1)} %collective-permute-done.1.rest_3_), channel_id=1, source_target_pairs={{0,2},{1,3},{4,0},{5,1},{8,4},{9,5},{12,8},{13,9},{14,12},{15,13},... | collective-permute-start | bytes 786440 | tf_op jit(solution)/shard_map/ppermute | solution.py:290
  14.2 5.2 %shard_map.78 = (f32[33,256,256]{2,1,0:T(8,128)S(1)}, bf16[32,256,256]{2,1,0:T(8,128)(2,1)S(1)}) custom-call(s32[128]{0:T(128)S(1)} %get-tuple-element.62.plan_ref, s32[6]{0:T(128)S(1)} %get-tuple-element.63.bounds_ref, bf16[92,256,256]{2,1,0:T(8,128)(2,1)S(1)} %get-tuple-element.64.left, ...), custom_call_target="tpu_custom_call", output_to_operand_aliasing={{0}: (10, {}), {1}: (11, {})} | custom-call | flops 1234803072 | bytes 1048576 | tf_op jit(solution)/shard_map/pallas_call | solution.py:376
  19.3 1.0 %collective-permute-done.2.rest_0_ = bf16[2,256,256]{2,1,0:T(8,128)(2,1)S(1)} collective-permute-done((bf16[2,256,256]{2,1,0:T(8,128)(2,1)S(1)}, bf16[2,256,256]{2,1,0:T(8,128)(2,1)S(1)}, u32[]{:S(2)}, u32[]{:S(2)}) %collective-permute-start.2) | collective-permute-done | bytes 262176 | tf_op jit(solution)/shard_map/ppermute | solution.py:287
  20.4 0.1 collective-permute-done.3.rest_1_
  20.5 0.5 collective-permute-start.10
  21.0 1.7 %collective-permute-start.7 = (bf16[2,256,256]{2,1,0:T(8,128)(2,1)S(1)}, bf16[2,256,256]{2,1,0:T(8,128)(2,1)S(1)}, u32[]{:S(2)}, u32[]{:S(2)}) collective-permute-start(bf16[2,256,256]{2,1,0:T(8,128)(2,1)S(1)} %collective-permute-done.2.rest_0_), channel_id=1, source_target_pairs={{0,4},{1,5},{4,8},{5,9},{8,12},{9,13},{12,14},{13,15},{14,10},{15,... | collective-permute-start | bytes 786440 | tf_op jit(solution)/shard_map/ppermute | solution.py:287
  22.7 0.3 collective-permute-start.8
  23.0 4.3 %shard_map.79 = (f32[33,256,256]{2,1,0:T(8,128)S(1)}, bf16[32,256,256]{2,1,0:T(8,128)(2,1)S(1)}) custom-call(s32[128]{0:T(128)S(1)} %get-tuple-element.62.plan_ref, s32[6]{0:T(128)S(1)} %get-tuple-element.63.bounds_ref, bf16[92,256,256]{2,1,0:T(8,128)(2,1)S(1)} %get-tuple-element.64.left, ...), custom_call_target="tpu_custom_call", output_to_operand_aliasing={{0}: (8, {}), {1}: (9, {})} | custom-call | flops 1234803072 | bytes 1048576 | tf_op jit(solution)/shard_map/pallas_call | solution.py:376
  27.4 1.8 %collective-permute-done.7.rest_0_ = bf16[2,256,256]{2,1,0:T(8,128)(2,1)S(1)} collective-permute-done((bf16[2,256,256]{2,1,0:T(8,128)(2,1)S(1)}, bf16[2,256,256]{2,1,0:T(8,128)(2,1)S(1)}, u32[]{:S(2)}, u32[]{:S(2)}) %collective-permute-start.7) | collective-permute-done | bytes 262176 | tf_op jit(solution)/shard_map/ppermute | solution.py:287
  29.2 1.4 %collective-permute-done.8.rest_1_ = bf16[2,256,256]{2,1,0:T(8,128)(2,1)S(1)} collective-permute-done((bf16[2,256,256]{2,1,0:T(8,128)(2,1)S(1)}, bf16[2,256,256]{2,1,0:T(8,128)(2,1)S(1)}, u32[]{:S(2)}, u32[]{:S(2)}) %collective-permute-start.8) | collective-permute-done | bytes 262176 | tf_op jit(solution)/shard_map/ppermute | solution.py:290
  30.6 0.5 collective-permute-start.14
  31.1 0.0 copy-start.2
  31.2 0.7 collective-permute-start.12
  31.8 1.4 %collective-permute-start.11 = (bf16[1,256,256]{2,1,0:T(8,128)(2,1)S(1)}, bf16[1,256,256]{2,1,0:T(8,128)(2,1)S(1)}, u32[]{:S(2)}, u32[]{:S(2)}) collective-permute-start(bf16[1,256,256]{2,1,0:T(8,128)(2,1)S(1)} %slice.6), channel_id=1, source_target_pairs={{0,4},{1,5},{4,8},{5,9},{8,12},{9,13},{12,14},{13,15},{14,10},{15,... | collective-permute-start | bytes 393224 | tf_op jit(solution)/shard_map/ppermute | solution.py:287
  33.2 5.9 %shard_map.80 = (f32[33,256,256]{2,1,0:T(8,128)S(1)}, bf16[32,256,256]{2,1,0:T(8,128)(2,1)S(1)}) custom-call(s32[128]{0:T(128)S(1)} %get-tuple-element.62.plan_ref, s32[6]{0:T(128)S(1)} %get-tuple-element.63.bounds_ref, bf16[92,256,256]{2,1,0:T(8,128)(2,1)S(1)} %get-tuple-element.64.left, ...), custom_call_target="tpu_custom_call", output_to_operand_aliasing={{0}: (8, {}), {1}: (9, {})} | custom-call | flops 1234803072 | bytes 1048576 | tf_op jit(solution)/shard_map/pallas_call | solution.py:376
  39.2 0.1 collective-permute-start.15
  39.3 0.5 collective-permute-start.16
  39.8 0.8 %collective-permute-done.15.rest_2_ = bf16[1,256,256]{2,1,0:T(8,128)(2,1)S(1)} collective-permute-done((bf16[1,256,256]{2,1,0:T(8,128)(2,1)S(1)}, bf16[1,256,256]{2,1,0:T(8,128)(2,1)S(1)}, u32[]{:S(2)}, u32[]{:S(2)}) %collective-permute-start.15) | collective-permute-done | bytes 131104 | tf_op jit(solution)/shard_map/ppermute | solution.py:293
  40.6 0.2 collective-permute-done.16.rest_3_
  40.8 6.2 %shard_map.81 = (f32[33,256,256]{2,1,0:T(8,128)S(1)}, bf16[32,256,256]{2,1,0:T(8,128)(2,1)S(1)}, f32[4,272,256]{2,1,0:T(8,128)S(1)}, f32[12,272,256]{2,1,0:T(8,1...) custom-call(s32[128]{0:T(128)S(1)} %get-tuple-element.62.plan_ref, ...), custom_call_target="tpu_custom_call", output_to_operand_aliasing={{0}: (10, {}), {1}: (11, {})} | custom-call | flops 1234803072 | bytes 1048576 | tf_op jit(solution)/shard_map/pallas_call | solution.py:376
  47.1 0.1 collective-permute-start.17
  47.1 2.7 %collective-permute-done.17.other = f32[4,272,256]{2,1,0:T(8,128)S(1)} collective-permute-done((f32[4,272,256]{2,1,0:T(8,128)S(1)}, f32[4,272,256]{2,1,0:T(8,128)S(1)}, u32[]{:S(2)}, u32[]{:S(2)}) %collective-permute-start.17) | collective-permute-done | bytes 1114144 | tf_op jit(solution)/shard_map/ppermute | solution.py:293
  49.9 0.1 collective-permute-start.18
  50.0 0.2 shard_map.83
  50.2 0.9 %collective-permute-start.20 = (f16[1,272,256]{2,1,0:T(8,128)(2,1)S(1)}, f16[1,272,256]{2,1,0:T(8,128)(2,1)S(1)}, u32[]{:S(2)}, u32[]{:S(2)}) collective-permute-start(f16[1,272,256]{2,1,0:T(8,128)(2,1)S(1)} %convert_element_type.85), channel_id=1, source_target_pairs={{0,2},{1,3},{4,0},{5,1},{8,4},{9,5},{12,8},{13,9},{14,12},{15,13},... | collective-permute-start | bytes 417800 | tf_op jit(solution)/shard_map/ppermute | solution.py:290
  51.1 1.2 %collective-permute-start.19 = (f16[1,272,256]{2,1,0:T(8,128)(2,1)S(1)}, f16[1,272,256]{2,1,0:T(8,128)(2,1)S(1)}, u32[]{:S(2)}, u32[]{:S(2)}) collective-permute-start(f16[1,272,256]{2,1,0:T(8,128)(2,1)S(1)} %convert_element_type.84), channel_id=1, source_target_pairs={{0,4},{1,5},{4,8},{5,9},{8,12},{9,13},{12,14},{13,15},{14,10},{15,... | collective-permute-start | bytes 417800 | tf_op jit(solution)/shard_map/ppermute | solution.py:287
  52.4 0.9 %collective-permute-start.24 = (f16[1,272,256]{2,1,0:T(8,128)(2,1)S(1)}, f16[1,272,256]{2,1,0:T(8,128)(2,1)S(1)}, u32[]{:S(2)}, u32[]{:S(2)}) collective-permute-start(f16[1,272,256]{2,1,0:T(8,128)(2,1)S(1)} %convert_element_type.87), channel_id=1, source_target_pairs={{0,2},{1,3},{4,0},{5,1},{8,4},{9,5},{12,8},{13,9},{14,12},{15,13},... | collective-permute-start | bytes 417800 | tf_op jit(solution)/shard_map/ppermute | solution.py:290
  53.3 1.2 %collective-permute-start.23 = (f16[1,272,256]{2,1,0:T(8,128)(2,1)S(1)}, f16[1,272,256]{2,1,0:T(8,128)(2,1)S(1)}, u32[]{:S(2)}, u32[]{:S(2)}) collective-permute-start(f16[1,272,256]{2,1,0:T(8,128)(2,1)S(1)} %convert_element_type.86), channel_id=1, source_target_pairs={{0,4},{1,5},{4,8},{5,9},{8,12},{9,13},{12,14},{13,15},{14,10},{15,... | collective-permute-start | bytes 417800 | tf_op jit(solution)/shard_map/ppermute | solution.py:287
  54.5 2.3 %collective-permute-done.20 = f16[1,272,256]{2,1,0:T(8,128)(2,1)S(1)} collective-permute-done((f16[1,272,256]{2,1,0:T(8,128)(2,1)S(1)}, f16[1,272,256]{2,1,0:T(8,128)(2,1)S(1)}, u32[]{:S(2)}, u32[]{:S(2)}) %collective-permute-start.20) | collective-permute-done | bytes 139296 | tf_op jit(solution)/shard_map/ppermute | solution.py:290
  56.8 0.9 %collective-permute-done.19 = f16[1,272,256]{2,1,0:T(8,128)(2,1)S(1)} collective-permute-done((f16[1,272,256]{2,1,0:T(8,128)(2,1)S(1)}, f16[1,272,256]{2,1,0:T(8,128)(2,1)S(1)}, u32[]{:S(2)}, u32[]{:S(2)}) %collective-permute-start.19) | collective-permute-done | bytes 139296 | tf_op jit(solution)/shard_map/ppermute | solution.py:287
  57.7 0.6 shard_map.82
  58.3 0.0 copy-start
  58.3 1.2 %collective-permute-start.21 = (f16[1,272,256]{2,1,0:T(8,128)(2,1)S(1)}, f16[1,272,256]{2,1,0:T(8,128)(2,1)S(1)}, u32[]{:S(2)}, u32[]{:S(2)}) collective-permute-start(f16[1,272,256]{2,1,0:T(8,128)(2,1)S(1)} %add_convert_fusion.9), channel_id=1, source_target_pairs={{0,4},{1,5},{4,8},{5,9},{8,12},{9,13},{12,14},{13,15},{14,10},{15,... | collective-permute-start | bytes 417800 | tf_op jit(solution)/shard_map/ppermute | solution.py:287
  59.6 0.1 add_convert_fusion.8
  59.6 0.9 %collective-permute-start.22 = (f16[1,272,256]{2,1,0:T(8,128)(2,1)S(1)}, f16[1,272,256]{2,1,0:T(8,128)(2,1)S(1)}, u32[]{:S(2)}, u32[]{:S(2)}) collective-permute-start(f16[1,272,256]{2,1,0:T(8,128)(2,1)S(1)} %add_convert_fusion.8), channel_id=1, source_target_pairs={{0,2},{1,3},{4,0},{5,1},{8,4},{9,5},{12,8},{13,9},{14,12},{15,13},... | collective-permute-start | bytes 417800 | tf_op jit(solution)/shard_map/ppermute | solution.py:290
  60.5 0.1 add_convert_fusion.7
  60.6 1.2 %collective-permute-start.27 = (f16[1,272,256]{2,1,0:T(8,128)(2,1)S(1)}, f16[1,272,256]{2,1,0:T(8,128)(2,1)S(1)}, u32[]{:S(2)}, u32[]{:S(2)}) collective-permute-start(f16[1,272,256]{2,1,0:T(8,128)(2,1)S(1)} %add_convert_fusion.7), channel_id=1, source_target_pairs={{0,4},{1,5},{4,8},{5,9},{8,12},{9,13},{12,14},{13,15},{14,10},{15,... | collective-permute-start | bytes 417800 | tf_op jit(solution)/shard_map/ppermute | solution.py:287
  61.9 0.9 %collective-permute-start.28 = (f16[1,272,256]{2,1,0:T(8,128)(2,1)S(1)}, f16[1,272,256]{2,1,0:T(8,128)(2,1)S(1)}, u32[]{:S(2)}, u32[]{:S(2)}) collective-permute-start(f16[1,272,256]{2,1,0:T(8,128)(2,1)S(1)} %add_convert_fusion.6), channel_id=1, source_target_pairs={{0,2},{1,3},{4,0},{5,1},{8,4},{9,5},{12,8},{13,9},{14,12},{15,13},... | collective-permute-start | bytes 417800 | tf_op jit(solution)/shard_map/ppermute | solution.py:290
  62.8 1.7 %collective-permute-done.21 = f16[1,272,256]{2,1,0:T(8,128)(2,1)S(1)} collective-permute-done((f16[1,272,256]{2,1,0:T(8,128)(2,1)S(1)}, f16[1,272,256]{2,1,0:T(8,128)(2,1)S(1)}, u32[]{:S(2)}, u32[]{:S(2)}) %collective-permute-start.21) | collective-permute-done | bytes 139296 | tf_op jit(solution)/shard_map/ppermute | solution.py:287
  64.5 1.7 %collective-permute-done.22 = f16[1,272,256]{2,1,0:T(8,128)(2,1)S(1)} collective-permute-done((f16[1,272,256]{2,1,0:T(8,128)(2,1)S(1)}, f16[1,272,256]{2,1,0:T(8,128)(2,1)S(1)}, u32[]{:S(2)}, u32[]{:S(2)}) %collective-permute-start.22) | collective-permute-done | bytes 139296 | tf_op jit(solution)/shard_map/ppermute | solution.py:290
  66.2 0.1 add_convert_fusion.4
  66.3 0.9 %collective-permute-start.26 = (f16[1,272,256]{2,1,0:T(8,128)(2,1)S(1)}, f16[1,272,256]{2,1,0:T(8,128)(2,1)S(1)}, u32[]{:S(2)}, u32[]{:S(2)}) collective-permute-start(f16[1,272,256]{2,1,0:T(8,128)(2,1)S(1)} %add_convert_fusion.4), channel_id=1, source_target_pairs={{0,2},{1,3},{4,0},{5,1},{8,4},{9,5},{12,8},{13,9},{14,12},{15,13},... | collective-permute-start | bytes 417800 | tf_op jit(solution)/shard_map/ppermute | solution.py:290
  67.2 1.3 %collective-permute-start.25 = (f16[1,272,256]{2,1,0:T(8,128)(2,1)S(1)}, f16[1,272,256]{2,1,0:T(8,128)(2,1)S(1)}, u32[]{:S(2)}, u32[]{:S(2)}) collective-permute-start(f16[1,272,256]{2,1,0:T(8,128)(2,1)S(1)} %add_convert_fusion.5), channel_id=1, source_target_pairs={{0,4},{1,5},{4,8},{5,9},{8,12},{9,13},{12,14},{13,15},{14,10},{15,... | collective-permute-start | bytes 417800 | tf_op jit(solution)/shard_map/ppermute | solution.py:287
  68.5 0.5 collective-permute-done.28
  69.0 0.1 add_convert_fusion.3
  69.0 1.4 %collective-permute-start.30 = (f16[1,272,256]{2,1,0:T(8,128)(2,1)S(1)}, f16[1,272,256]{2,1,0:T(8,128)(2,1)S(1)}, u32[]{:S(2)}, u32[]{:S(2)}) collective-permute-start(f16[1,272,256]{2,1,0:T(8,128)(2,1)S(1)} %add_convert_fusion.3), channel_id=1, source_target_pairs={{0,4},{1,5},{4,8},{5,9},{8,12},{9,13},{12,14},{13,15},{14,10},{15,... | collective-permute-start | bytes 417800 | tf_op jit(solution)/shard_map/ppermute | solution.py:287
  70.5 0.8 collective-permute-start.31
  71.2 1.4 %collective-permute-done.26 = f16[1,272,256]{2,1,0:T(8,128)(2,1)S(1)} collective-permute-done((f16[1,272,256]{2,1,0:T(8,128)(2,1)S(1)}, f16[1,272,256]{2,1,0:T(8,128)(2,1)S(1)}, u32[]{:S(2)}, u32[]{:S(2)}) %collective-permute-start.26) | collective-permute-done | bytes 139296 | tf_op jit(solution)/shard_map/ppermute | solution.py:290
  72.6 0.3 collective-permute-done.25
  72.9 0.8 %collective-permute-start.32 = (f16[1,272,256]{2,1,0:T(8,128)(2,1)S(1)}, f16[1,272,256]{2,1,0:T(8,128)(2,1)S(1)}, u32[]{:S(2)}, u32[]{:S(2)}) collective-permute-start(f16[1,272,256]{2,1,0:T(8,128)(2,1)S(1)} %add_convert_fusion), channel_id=1, source_target_pairs={{0,2},{1,3},{4,0},{5,1},{8,4},{9,5},{12,8},{13,9},{14,12},{15,13},... | collective-permute-start | bytes 417800 | tf_op jit(solution)/shard_map/ppermute | solution.py:290
  73.8 0.1 add_convert_fusion.1
  73.8 1.3 %collective-permute-start.29 = (f16[1,272,256]{2,1,0:T(8,128)(2,1)S(1)}, f16[1,272,256]{2,1,0:T(8,128)(2,1)S(1)}, u32[]{:S(2)}, u32[]{:S(2)}) collective-permute-start(f16[1,272,256]{2,1,0:T(8,128)(2,1)S(1)} %add_convert_fusion.1), channel_id=1, source_target_pairs={{0,4},{1,5},{4,8},{5,9},{8,12},{9,13},{12,14},{13,15},{14,10},{15,... | collective-permute-start | bytes 417800 | tf_op jit(solution)/shard_map/ppermute | solution.py:287
  75.1 0.1 collective-permute-done.30
  75.3 0.6 collective-permute-done.31
  75.9 2.2 %collective-permute-done.32 = f16[1,272,256]{2,1,0:T(8,128)(2,1)S(1)} collective-permute-done((f16[1,272,256]{2,1,0:T(8,128)(2,1)S(1)}, f16[1,272,256]{2,1,0:T(8,128)(2,1)S(1)}, u32[]{:S(2)}, u32[]{:S(2)}) %collective-permute-start.32) | collective-permute-done | bytes 139296 | tf_op jit(solution)/shard_map/ppermute | solution.py:290
  78.1 1.5 %collective-permute-done.29 = f16[1,272,256]{2,1,0:T(8,128)(2,1)S(1)} collective-permute-done((f16[1,272,256]{2,1,0:T(8,128)(2,1)S(1)}, f16[1,272,256]{2,1,0:T(8,128)(2,1)S(1)}, u32[]{:S(2)}, u32[]{:S(2)}) %collective-permute-start.29) | collective-permute-done | bytes 139296 | tf_op jit(solution)/shard_map/ppermute | solution.py:287
  79.6 1.3 %shard_map.84 = (f32[2,256,256]{2,1,0:T(8,128)}, f32[1]{0:T(128)}) custom-call(f32[3,8,128]{2,1,0:T(8,128)S(1)} %copy-done.2, f32[8,128]{1,0:T(8,128)S(1)} %get-tuple-element.90.scales, f32[2,272,256]{2,1,0:T(8,128)S(1)} %get-tuple-element.96.home, f32[1,272,256]{2,1,0:T(8,128)S(1)} %convert_element_type.106.r0, ...), custom_call_target="tpu_custom_call" | custom-call | bytes 2097152 | tf_op jit(solution)/shard_map/pallas_call | solution.py:437
  (36 shorter events, 0.4 us)
Async XLA Ops:
  0.6 9.6 %collective-permute-start.1 = (bf16[2,256,256]{2,1,0:T(8,128)(2,1)}, bf16[2,256,256]{2,1,0:T(8,128)(2,1)S(1)}, u32[]{:S(2)}, u32[]{:S(2)}) collective-permute-start(bf16[2,256,256]{2,1,0:T(8,128)(2,1)} %psi_ref.1), channel_id=1, source_target_pairs={{0,2},{1,3},{4,0},{5,1},{8,4},{9,5},{12,8},{13,9},{14,12},{15,13},... | collective-permute-start | bytes 786440 | tf_op jit(solution)/shard_map/ppermute | solution.py:290
  3.6 8.0 %collective-permute-start = (bf16[2,256,256]{2,1,0:T(8,128)(2,1)}, bf16[2,256,256]{2,1,0:T(8,128)(2,1)S(1)}, u32[]{:S(2)}, u32[]{:S(2)}) collective-permute-start(bf16[2,256,256]{2,1,0:T(8,128)(2,1)} %psi_ref.1), channel_id=1, source_target_pairs={{0,4},{1,5},{4,8},{5,9},{8,12},{9,13},{12,14},{13,15},{14,10},{15,... | collective-permute-start | bytes 786440 | tf_op jit(solution)/shard_map/ppermute | solution.py:287
  3.8 10.4 %collective-permute-start.4 = (bf16[2,256,256]{2,1,0:T(8,128)(2,1)}, bf16[2,256,256]{2,1,0:T(8,128)(2,1)S(1)}, u32[]{:S(2)}, u32[]{:S(2)}) collective-permute-start(bf16[2,256,256]{2,1,0:T(8,128)(2,1)} %psi_ref.1), channel_id=1, source_target_pairs={{0,1},{1,0},{2,3},{3,2},{4,5},{5,4},{6,7},{7,6},{8,9},{9,8},{10,11... | collective-permute-start | bytes 786440 | tf_op jit(solution)/shard_map/ppermute | solution.py:293
  11.6 2.5 %collective-permute-start.5 = (bf16[2,256,256]{2,1,0:T(8,128)(2,1)S(1)}, bf16[2,256,256]{2,1,0:T(8,128)(2,1)S(1)}, u32[]{:S(2)}, u32[]{:S(2)}) collective-permute-start(bf16[2,256,256]{2,1,0:T(8,128)(2,1)S(1)} %collective-permute-done.rest_2_), channel_id=1, source_target_pairs={{0,1},{1,0},{2,3},{3,2},{4,5},{5,4},{6,7},{7,6},{8,9},{9,8},{10,11... | collective-permute-start | bytes 786440 | tf_op jit(solution)/shard_map/ppermute | solution.py:293
  11.6 2.5 %collective-permute-start.6 = (bf16[2,256,256]{2,1,0:T(8,128)(2,1)S(1)}, bf16[2,256,256]{2,1,0:T(8,128)(2,1)S(1)}, u32[]{:S(2)}, u32[]{:S(2)}) collective-permute-start(bf16[2,256,256]{2,1,0:T(8,128)(2,1)S(1)} %collective-permute-done.1.rest_3_), channel_id=1, source_target_pairs={{0,1},{1,0},{2,3},{3,2},{4,5},{5,4},{6,7},{7,6},{8,9},{9,8},{10,11... | collective-permute-start | bytes 786440 | tf_op jit(solution)/shard_map/ppermute | solution.py:293
  12.1 8.2 %collective-permute-start.2 = (bf16[2,256,256]{2,1,0:T(8,128)(2,1)S(1)}, bf16[2,256,256]{2,1,0:T(8,128)(2,1)S(1)}, u32[]{:S(2)}, u32[]{:S(2)}) collective-permute-start(bf16[2,256,256]{2,1,0:T(8,128)(2,1)S(1)} %collective-permute-done.rest_2_), channel_id=1, source_target_pairs={{0,4},{1,5},{4,8},{5,9},{8,12},{9,13},{12,14},{13,15},{14,10},{15,... | collective-permute-start | bytes 786440 | tf_op jit(solution)/shard_map/ppermute | solution.py:287
  12.5 7.9 %collective-permute-start.3 = (bf16[2,256,256]{2,1,0:T(8,128)(2,1)S(1)}, bf16[2,256,256]{2,1,0:T(8,128)(2,1)S(1)}, u32[]{:S(2)}, u32[]{:S(2)}) collective-permute-start(bf16[2,256,256]{2,1,0:T(8,128)(2,1)S(1)} %collective-permute-done.1.rest_3_), channel_id=1, source_target_pairs={{0,2},{1,3},{4,0},{5,1},{8,4},{9,5},{12,8},{13,9},{14,12},{15,13},... | collective-permute-start | bytes 786440 | tf_op jit(solution)/shard_map/ppermute | solution.py:290
  20.5 2.5 %collective-permute-start.9 = (bf16[2,256,256]{2,1,0:T(8,128)(2,1)S(1)}, bf16[2,256,256]{2,1,0:T(8,128)(2,1)S(1)}, u32[]{:S(2)}, u32[]{:S(2)}) collective-permute-start(bf16[2,256,256]{2,1,0:T(8,128)(2,1)S(1)} %collective-permute-done.2.rest_0_), channel_id=1, source_target_pairs={{0,1},{1,0},{2,3},{3,2},{4,5},{5,4},{6,7},{7,6},{8,9},{9,8},{10,11... | collective-permute-start | bytes 786440 | tf_op jit(solution)/shard_map/ppermute | solution.py:293
  20.5 2.5 %collective-permute-start.10 = (bf16[2,256,256]{2,1,0:T(8,128)(2,1)S(1)}, bf16[2,256,256]{2,1,0:T(8,128)(2,1)S(1)}, u32[]{:S(2)}, u32[]{:S(2)}) collective-permute-start(bf16[2,256,256]{2,1,0:T(8,128)(2,1)S(1)} %collective-permute-done.3.rest_1_), channel_id=1, source_target_pairs={{0,1},{1,0},{2,3},{3,2},{4,5},{5,4},{6,7},{7,6},{8,9},{9,8},{10,11... | collective-permute-start | bytes 786440 | tf_op jit(solution)/shard_map/ppermute | solution.py:293
  21.0 8.2 %collective-permute-start.7 = (bf16[2,256,256]{2,1,0:T(8,128)(2,1)S(1)}, bf16[2,256,256]{2,1,0:T(8,128)(2,1)S(1)}, u32[]{:S(2)}, u32[]{:S(2)}) collective-permute-start(bf16[2,256,256]{2,1,0:T(8,128)(2,1)S(1)} %collective-permute-done.2.rest_0_), channel_id=1, source_target_pairs={{0,4},{1,5},{4,8},{5,9},{8,12},{9,13},{12,14},{13,15},{14,10},{15,... | collective-permute-start | bytes 786440 | tf_op jit(solution)/shard_map/ppermute | solution.py:287
  22.7 7.9 %collective-permute-start.8 = (bf16[2,256,256]{2,1,0:T(8,128)(2,1)S(1)}, bf16[2,256,256]{2,1,0:T(8,128)(2,1)S(1)}, u32[]{:S(2)}, u32[]{:S(2)}) collective-permute-start(bf16[2,256,256]{2,1,0:T(8,128)(2,1)S(1)} %collective-permute-done.3.rest_1_), channel_id=1, source_target_pairs={{0,2},{1,3},{4,0},{5,1},{8,4},{9,5},{12,8},{13,9},{14,12},{15,13},... | collective-permute-start | bytes 786440 | tf_op jit(solution)/shard_map/ppermute | solution.py:290
  30.6 2.6 %collective-permute-start.13 = (bf16[2,256,256]{2,1,0:T(8,128)(2,1)S(1)}, bf16[2,256,256]{2,1,0:T(8,128)(2,1)S(1)}, u32[]{:S(2)}, u32[]{:S(2)}) collective-permute-start(bf16[2,256,256]{2,1,0:T(8,128)(2,1)S(1)} %collective-permute-done.7.rest_0_), channel_id=1, source_target_pairs={{0,1},{1,0},{2,3},{3,2},{4,5},{5,4},{6,7},{7,6},{8,9},{9,8},{10,11... | collective-permute-start | bytes 786440 | tf_op jit(solution)/shard_map/ppermute | solution.py:293
  30.6 2.6 %collective-permute-start.14 = (bf16[2,256,256]{2,1,0:T(8,128)(2,1)S(1)}, bf16[2,256,256]{2,1,0:T(8,128)(2,1)S(1)}, u32[]{:S(2)}, u32[]{:S(2)}) collective-permute-start(bf16[2,256,256]{2,1,0:T(8,128)(2,1)S(1)} %collective-permute-done.8.rest_1_), channel_id=1, source_target_pairs={{0,1},{1,0},{2,3},{3,2},{4,5},{5,4},{6,7},{7,6},{8,9},{9,8},{10,11... | collective-permute-start | bytes 786440 | tf_op jit(solution)/shard_map/ppermute | solution.py:293
  31.1 9.7 %copy-start.2 = (f32[3,8,128]{2,1,0:T(8,128)S(1)}, f32[3,8,128]{2,1,0:T(8,128)}, u32[]{:S(2)}) copy-start(f32[3,8,128]{2,1,0:T(8,128)} %constant.6.clone.rest_5_.digit_ref) | copy-start | bytes 36868
  31.2 8.0 %collective-permute-start.12 = (bf16[1,256,256]{2,1,0:T(8,128)(2,1)S(1)}, bf16[1,256,256]{2,1,0:T(8,128)(2,1)S(1)}, u32[]{:S(2)}, u32[]{:S(2)}) collective-permute-start(bf16[1,256,256]{2,1,0:T(8,128)(2,1)S(1)} %slice.7), channel_id=1, source_target_pairs={{0,2},{1,3},{4,0},{5,1},{8,4},{9,5},{12,8},{13,9},{14,12},{15,13},... | collective-permute-start | bytes 393224 | tf_op jit(solution)/shard_map/ppermute | solution.py:290
  31.8 7.4 %collective-permute-start.11 = (bf16[1,256,256]{2,1,0:T(8,128)(2,1)S(1)}, bf16[1,256,256]{2,1,0:T(8,128)(2,1)S(1)}, u32[]{:S(2)}, u32[]{:S(2)}) collective-permute-start(bf16[1,256,256]{2,1,0:T(8,128)(2,1)S(1)} %slice.6), channel_id=1, source_target_pairs={{0,4},{1,5},{4,8},{5,9},{8,12},{9,13},{12,14},{13,15},{14,10},{15,... | collective-permute-start | bytes 393224 | tf_op jit(solution)/shard_map/ppermute | solution.py:287
  39.2 1.4 %collective-permute-start.15 = (bf16[1,256,256]{2,1,0:T(8,128)(2,1)S(1)}, bf16[1,256,256]{2,1,0:T(8,128)(2,1)S(1)}, u32[]{:S(2)}, u32[]{:S(2)}) collective-permute-start(bf16[1,256,256]{2,1,0:T(8,128)(2,1)S(1)} %collective-permute-done.11.rest_0_), channel_id=1, source_target_pairs={{0,1},{1,0},{2,3},{3,2},{4,5},{5,4},{6,7},{7,6},{8,9},{9,8},{10,11... | collective-permute-start | bytes 393224 | tf_op jit(solution)/shard_map/ppermute | solution.py:293
  39.3 1.5 %collective-permute-start.16 = (bf16[1,256,256]{2,1,0:T(8,128)(2,1)S(1)}, bf16[1,256,256]{2,1,0:T(8,128)(2,1)S(1)}, u32[]{:S(2)}, u32[]{:S(2)}) collective-permute-start(bf16[1,256,256]{2,1,0:T(8,128)(2,1)S(1)} %collective-permute-done.12.rest_1_), channel_id=1, source_target_pairs={{0,1},{1,0},{2,3},{3,2},{4,5},{5,4},{6,7},{7,6},{8,9},{9,8},{10,11... | collective-permute-start | bytes 393224 | tf_op jit(solution)/shard_map/ppermute | solution.py:293
  47.1 2.8 %collective-permute-start.17 = (f32[4,272,256]{2,1,0:T(8,128)S(1)}, f32[4,272,256]{2,1,0:T(8,128)S(1)}, u32[]{:S(2)}, u32[]{:S(2)}) collective-permute-start(f32[4,272,256]{2,1,0:T(8,128)S(1)} %get-tuple-element.92), channel_id=1, source_target_pairs={{0,1},{1,0},{2,3},{3,2},{4,5},{5,4},{6,7},{7,6},{8,9},{9,8},{10,11... | collective-permute-start | bytes 3342344 | tf_op jit(solution)/shard_map/ppermute | solution.py:293
  49.9 7.8 %collective-permute-start.18 = (f32[12,272,256]{2,1,0:T(8,128)S(1)}, f32[12,272,256]{2,1,0:T(8,128)S(1)}, u32[]{:S(2)}, u32[]{:S(2)}) collective-permute-start(f32[12,272,256]{2,1,0:T(8,128)S(1)} %get-tuple-element.94), channel_id=1, source_target_pairs={{0,1},{1,0},{2,3},{3,2},{4,5},{5,4},{6,7},{7,6},{8,9},{9,8},{10,11... | collective-permute-start | bytes 10027016 | tf_op jit(solution)/shard_map/ppermute | solution.py:293
  50.2 6.6 %collective-permute-start.20 = (f16[1,272,256]{2,1,0:T(8,128)(2,1)S(1)}, f16[1,272,256]{2,1,0:T(8,128)(2,1)S(1)}, u32[]{:S(2)}, u32[]{:S(2)}) collective-permute-start(f16[1,272,256]{2,1,0:T(8,128)(2,1)S(1)} %convert_element_type.85), channel_id=1, source_target_pairs={{0,2},{1,3},{4,0},{5,1},{8,4},{9,5},{12,8},{13,9},{14,12},{15,13},... | collective-permute-start | bytes 417800 | tf_op jit(solution)/shard_map/ppermute | solution.py:290
  51.1 6.6 %collective-permute-start.19 = (f16[1,272,256]{2,1,0:T(8,128)(2,1)S(1)}, f16[1,272,256]{2,1,0:T(8,128)(2,1)S(1)}, u32[]{:S(2)}, u32[]{:S(2)}) collective-permute-start(f16[1,272,256]{2,1,0:T(8,128)(2,1)S(1)} %convert_element_type.84), channel_id=1, source_target_pairs={{0,4},{1,5},{4,8},{5,9},{8,12},{9,13},{12,14},{13,15},{14,10},{15,... | collective-permute-start | bytes 417800 | tf_op jit(solution)/shard_map/ppermute | solution.py:287
  52.4 8.1 %collective-permute-start.24 = (f16[1,272,256]{2,1,0:T(8,128)(2,1)S(1)}, f16[1,272,256]{2,1,0:T(8,128)(2,1)S(1)}, u32[]{:S(2)}, u32[]{:S(2)}) collective-permute-start(f16[1,272,256]{2,1,0:T(8,128)(2,1)S(1)} %convert_element_type.87), channel_id=1, source_target_pairs={{0,2},{1,3},{4,0},{5,1},{8,4},{9,5},{12,8},{13,9},{14,12},{15,13},... | collective-permute-start | bytes 417800 | tf_op jit(solution)/shard_map/ppermute | solution.py:290
  53.3 7.3 %collective-permute-start.23 = (f16[1,272,256]{2,1,0:T(8,128)(2,1)S(1)}, f16[1,272,256]{2,1,0:T(8,128)(2,1)S(1)}, u32[]{:S(2)}, u32[]{:S(2)}) collective-permute-start(f16[1,272,256]{2,1,0:T(8,128)(2,1)S(1)} %convert_element_type.86), channel_id=1, source_target_pairs={{0,4},{1,5},{4,8},{5,9},{8,12},{9,13},{12,14},{13,15},{14,10},{15,... | collective-permute-start | bytes 417800 | tf_op jit(solution)/shard_map/ppermute | solution.py:287
  58.3 21.4 %copy-start = (bf16[3,2,256,256]{3,2,1,0:T(8,128)(2,1)S(1)}, bf16[3,2,256,256]{3,2,1,0:T(8,128)(2,1)}, u32[]{:S(2)}) copy-start(bf16[3,2,256,256]{3,2,1,0:T(8,128)(2,1)} %lower_ref.1) | copy-start | bytes 2359300
  58.3 21.4 %copy-start.1 = (bf16[2,256,256]{2,1,0:T(8,128)(2,1)S(1)}, bf16[2,256,256]{2,1,0:T(8,128)(2,1)}, u32[]{:S(2)}) copy-start(bf16[2,256,256]{2,1,0:T(8,128)(2,1)} %psi_ref.1) | copy-start | bytes 786436
  58.3 6.1 %collective-permute-start.21 = (f16[1,272,256]{2,1,0:T(8,128)(2,1)S(1)}, f16[1,272,256]{2,1,0:T(8,128)(2,1)S(1)}, u32[]{:S(2)}, u32[]{:S(2)}) collective-permute-start(f16[1,272,256]{2,1,0:T(8,128)(2,1)S(1)} %add_convert_fusion.9), channel_id=1, source_target_pairs={{0,4},{1,5},{4,8},{5,9},{8,12},{9,13},{12,14},{13,15},{14,10},{15,... | collective-permute-start | bytes 417800 | tf_op jit(solution)/shard_map/ppermute | solution.py:287
  59.6 6.6 %collective-permute-start.22 = (f16[1,272,256]{2,1,0:T(8,128)(2,1)S(1)}, f16[1,272,256]{2,1,0:T(8,128)(2,1)S(1)}, u32[]{:S(2)}, u32[]{:S(2)}) collective-permute-start(f16[1,272,256]{2,1,0:T(8,128)(2,1)S(1)} %add_convert_fusion.8), channel_id=1, source_target_pairs={{0,2},{1,3},{4,0},{5,1},{8,4},{9,5},{12,8},{13,9},{14,12},{15,13},... | collective-permute-start | bytes 417800 | tf_op jit(solution)/shard_map/ppermute | solution.py:290
  60.6 7.9 %collective-permute-start.27 = (f16[1,272,256]{2,1,0:T(8,128)(2,1)S(1)}, f16[1,272,256]{2,1,0:T(8,128)(2,1)S(1)}, u32[]{:S(2)}, u32[]{:S(2)}) collective-permute-start(f16[1,272,256]{2,1,0:T(8,128)(2,1)S(1)} %add_convert_fusion.7), channel_id=1, source_target_pairs={{0,4},{1,5},{4,8},{5,9},{8,12},{9,13},{12,14},{13,15},{14,10},{15,... | collective-permute-start | bytes 417800 | tf_op jit(solution)/shard_map/ppermute | solution.py:287
  61.9 7.1 %collective-permute-start.28 = (f16[1,272,256]{2,1,0:T(8,128)(2,1)S(1)}, f16[1,272,256]{2,1,0:T(8,128)(2,1)S(1)}, u32[]{:S(2)}, u32[]{:S(2)}) collective-permute-start(f16[1,272,256]{2,1,0:T(8,128)(2,1)S(1)} %add_convert_fusion.6), channel_id=1, source_target_pairs={{0,2},{1,3},{4,0},{5,1},{8,4},{9,5},{12,8},{13,9},{14,12},{15,13},... | collective-permute-start | bytes 417800 | tf_op jit(solution)/shard_map/ppermute | solution.py:290
  66.3 6.3 %collective-permute-start.26 = (f16[1,272,256]{2,1,0:T(8,128)(2,1)S(1)}, f16[1,272,256]{2,1,0:T(8,128)(2,1)S(1)}, u32[]{:S(2)}, u32[]{:S(2)}) collective-permute-start(f16[1,272,256]{2,1,0:T(8,128)(2,1)S(1)} %add_convert_fusion.4), channel_id=1, source_target_pairs={{0,2},{1,3},{4,0},{5,1},{8,4},{9,5},{12,8},{13,9},{14,12},{15,13},... | collective-permute-start | bytes 417800 | tf_op jit(solution)/shard_map/ppermute | solution.py:290
  67.2 5.7 %collective-permute-start.25 = (f16[1,272,256]{2,1,0:T(8,128)(2,1)S(1)}, f16[1,272,256]{2,1,0:T(8,128)(2,1)S(1)}, u32[]{:S(2)}, u32[]{:S(2)}) collective-permute-start(f16[1,272,256]{2,1,0:T(8,128)(2,1)S(1)} %add_convert_fusion.5), channel_id=1, source_target_pairs={{0,4},{1,5},{4,8},{5,9},{8,12},{9,13},{12,14},{13,15},{14,10},{15,... | collective-permute-start | bytes 417800 | tf_op jit(solution)/shard_map/ppermute | solution.py:287
  69.0 6.2 %collective-permute-start.30 = (f16[1,272,256]{2,1,0:T(8,128)(2,1)S(1)}, f16[1,272,256]{2,1,0:T(8,128)(2,1)S(1)}, u32[]{:S(2)}, u32[]{:S(2)}) collective-permute-start(f16[1,272,256]{2,1,0:T(8,128)(2,1)S(1)} %add_convert_fusion.3), channel_id=1, source_target_pairs={{0,4},{1,5},{4,8},{5,9},{8,12},{9,13},{12,14},{13,15},{14,10},{15,... | collective-permute-start | bytes 417800 | tf_op jit(solution)/shard_map/ppermute | solution.py:287
  70.5 5.4 %collective-permute-start.31 = (f16[1,272,256]{2,1,0:T(8,128)(2,1)S(1)}, f16[1,272,256]{2,1,0:T(8,128)(2,1)S(1)}, u32[]{:S(2)}, u32[]{:S(2)}) collective-permute-start(f16[1,272,256]{2,1,0:T(8,128)(2,1)S(1)} %add_convert_fusion.2), channel_id=1, source_target_pairs={{0,2},{1,3},{4,0},{5,1},{8,4},{9,5},{12,8},{13,9},{14,12},{15,13},... | collective-permute-start | bytes 417800 | tf_op jit(solution)/shard_map/ppermute | solution.py:290
  72.9 5.1 %collective-permute-start.32 = (f16[1,272,256]{2,1,0:T(8,128)(2,1)S(1)}, f16[1,272,256]{2,1,0:T(8,128)(2,1)S(1)}, u32[]{:S(2)}, u32[]{:S(2)}) collective-permute-start(f16[1,272,256]{2,1,0:T(8,128)(2,1)S(1)} %add_convert_fusion), channel_id=1, source_target_pairs={{0,2},{1,3},{4,0},{5,1},{8,4},{9,5},{12,8},{13,9},{14,12},{15,13},... | collective-permute-start | bytes 417800 | tf_op jit(solution)/shard_map/ppermute | solution.py:290
  73.8 5.8 %collective-permute-start.29 = (f16[1,272,256]{2,1,0:T(8,128)(2,1)S(1)}, f16[1,272,256]{2,1,0:T(8,128)(2,1)S(1)}, u32[]{:S(2)}, u32[]{:S(2)}) collective-permute-start(f16[1,272,256]{2,1,0:T(8,128)(2,1)S(1)} %add_convert_fusion.1), channel_id=1, source_target_pairs={{0,4},{1,5},{4,8},{5,9},{8,12},{9,13},{12,14},{13,15},{14,10},{15,... | collective-permute-start | bytes 417800 | tf_op jit(solution)/shard_map/ppermute | solution.py:287

commit v5 on v4

--- a/solution.py
+++ b/solution.py
@@ -246,8 +246,9 @@
     for out in outs:
         for i in range(out.shape[0]):
             out[i, 0:side] = (acc[slots[at]] + other[at, 0:side]) * scales[0:1, 0:1]
-            out[i, side:] = other[at, side:]
-            out[i, pl.ds(side, digits.shape[0]), pl.ds(0, 128)] += digits[...]
+            if out.shape[1] > side:
+                out[i, side:] = other[at, side:]
+                out[i, pl.ds(side, digits.shape[0]), pl.ds(0, 128)] += digits[...]
             at += 1
 
 
@@ -409,7 +410,7 @@
         own = {}
         for parts, there in zip(sets, got):
             keys = [key for key in parts if key[0] != 0]
-            shapes = [(part, tall, side)] * len(keys)
+            shapes = [(part, side if half else tall, side) for _, half in keys]
             if len(keys) < len(parts):
                 shapes.append((per, tall, side))
             slots = [rel % chips * per + h * part + i for rel, h in parts for i in range(part)]

time: 81.8 us -> 79.7 us (0.974)
  waiting for transfers between devices: 23.8 us -> 21.1 us
  starting transfers between devices: 26.4 us -> 27.9 us
    ppermute x11, waiting for transfers between devices: 8.84 us -> 3.68 us  [right(): return lax.ppermute(x, 'sector', to_right)]
    ppermute x11, waiting for transfers between devices: 11.2 us -> 13.9 us  [left(): return lax.ppermute(x, 'sector', to_left)]
    ppermute x11, starting transfers between devices: 2.31 us -> 3.63 us  [pair(): return lax.ppermute(x, 'sector', [(i, i ^ hop) for i in range(devices)])]
    ppermute x11, starting transfers between devices: 12.5 us -> 13.8 us  [right(): return lax.ppermute(x, 'sector', to_right)]
    ppermute x11, starting transfers between devices: 11.6 us -> 10.5 us  [left(): return lax.ppermute(x, 'sector', to_left)]
  transfers between devices with their start and end apart: 33 -> 33, of which waited for: 20 -> 18; matrix products, arithmetic and copies ran while one was open for 1% -> 1% of each run, Pallas kernels for 27% -> 26%
where the time goes in v5:
time: 79.7 us; the launch traced here: 78.9 us
  Pallas kernels  28.4 us (36%)
  starting transfers between devices  27.9 us (35%)
  waiting for transfers between devices  21.1 us (26%)
  between operations  0.88 us (1%)
    pallas_call x4, Pallas kernels, run_stage(): pl.pallas_call(functools.partial(stage_kernel, stage, starts, finish, lim...  20.9 us
    ppermute x11, waiting for transfers between devices, left(): return lax.ppermute(x, 'sector', to_left)  13.9 us
    ppermute x11, starting transfers between devices, right(): return lax.ppermute(x, 'sector', to_right)  13.8 us
    ppermute x11, starting transfers between devices, left(): return lax.ppermute(x, 'sector', to_left)  10.5 us
    pallas_call x1, Pallas kernels, make_plan(): pl.pallas_call(functools.partial(plan_kernel, (chips, rows_y, per, cap, s...  5.47 us
    ppermute x11, waiting for transfers between devices, right(): return lax.ppermute(x, 'sector', to_right)  3.68 us
    ppermute x11, starting transfers between devices, pair(): return lax.ppermute(x, 'sector', [(i, i ^ hop) for i in range(devices)])  3.63 us
    ppermute x11, waiting for transfers between devices, pair(): return lax.ppermute(x, 'sector', [(i, i ^ hop) for i in range(devices)])  3.48 us
  transfers between devices with their start and end apart: 33, of which 18 were waited for; matrix products, arithmetic and copies ran while one was open for 1% of the time, Pallas kernels for 26%

profile of v5, /device:TPU:0, one launch (start us, length us, event | category | flops | bytes accessed | tf_op | source)
XLA Modules:
  0.0 78.9 jit_solution(6739479239873055574)
XLA Ops:
  0.6 3.0 %collective-permute-start.1 = (bf16[2,256,256]{2,1,0:T(8,128)(2,1)}, bf16[2,256,256]{2,1,0:T(8,128)(2,1)S(1)}, u32[]{:S(2)}, u32[]{:S(2)}) collective-permute-start(bf16[2,256,256]{2,1,0:T(8,128)(2,1)} %psi_ref.1), channel_id=1, source_target_pairs={{0,2},{1,3},{4,0},{5,1},{8,4},{9,5},{12,8},{13,9},{14,12},{15,13},... | collective-permute-start | bytes 786440 | tf_op jit(solution)/shard_map/ppermute | solution.py:291
  3.6 0.1 collective-permute-start
  3.8 0.0 collective-permute-start.4
  3.8 5.5 %shard_map.77 = (bf16[92,256,256]{2,1,0:T(8,128)(2,1)S(1)}, f32[8,128]{1,0:T(8,128)S(1)}, f32[33,256,256]{2,1,0:T(8,128)S(1)}, bf16[32,256,256]{2,1,0:T(8,128)(2,1)S(1)}, s32[128]{0:T(128)S(1)}, /*index=5*/s32[6]{0:T(128)S(1)}) custom-call(s32[2,92]{1,0:T(2,128)} %bitcast.2, s32[1]{0:T(128)} %bitcast.1.me_ref, bf16[2,256,256]{2,1,0:T(8,128)(2,1)} %psi_ref.1, ...), custom_call_target="tpu_custom_call" | custom-call | bytes 12582912 | tf_op jit(solution)/shard_map/pallas_call | solution.py:331
  9.3 1.0 %collective-permute-done.1.rest_3_ = bf16[2,256,256]{2,1,0:T(8,128)(2,1)S(1)} collective-permute-done((bf16[2,256,256]{2,1,0:T(8,128)(2,1)}, bf16[2,256,256]{2,1,0:T(8,128)(2,1)S(1)}, u32[]{:S(2)}, u32[]{:S(2)}) %collective-permute-start.1) | collective-permute-done | bytes 262176 | tf_op jit(solution)/shard_map/ppermute | solution.py:291
  10.2 1.4 %collective-permute-done.rest_2_ = bf16[2,256,256]{2,1,0:T(8,128)(2,1)S(1)} collective-permute-done((bf16[2,256,256]{2,1,0:T(8,128)(2,1)}, bf16[2,256,256]{2,1,0:T(8,128)(2,1)S(1)}, u32[]{:S(2)}, u32[]{:S(2)}) %collective-permute-start) | collective-permute-done | bytes 262176 | tf_op jit(solution)/shard_map/ppermute | solution.py:288
  11.6 0.5 collective-permute-start.6
  12.1 0.4 collective-permute-start.2
  12.5 1.6 %collective-permute-start.3 = (bf16[2,256,256]{2,1,0:T(8,128)(2,1)S(1)}, bf16[2,256,256]{2,1,0:T(8,128)(2,1)S(1)}, u32[]{:S(2)}, u32[]{:S(2)}) collective-permute-start(bf16[2,256,256]{2,1,0:T(8,128)(2,1)S(1)} %collective-permute-done.1.rest_3_), channel_id=1, source_target_pairs={{0,2},{1,3},{4,0},{5,1},{8,4},{9,5},{12,8},{13,9},{14,12},{15,13},... | collective-permute-start | bytes 786440 | tf_op jit(solution)/shard_map/ppermute | solution.py:291
  14.2 0.0 collective-permute-done.4.rest_1_
  14.2 5.2 %shard_map.78 = (f32[33,256,256]{2,1,0:T(8,128)S(1)}, bf16[32,256,256]{2,1,0:T(8,128)(2,1)S(1)}) custom-call(s32[128]{0:T(128)S(1)} %get-tuple-element.62.plan_ref, s32[6]{0:T(128)S(1)} %get-tuple-element.63.bounds_ref, bf16[92,256,256]{2,1,0:T(8,128)(2,1)S(1)} %get-tuple-element.64.left, ...), custom_call_target="tpu_custom_call", output_to_operand_aliasing={{0}: (10, {}), {1}: (11, {})} | custom-call | flops 1234803072 | bytes 1048576 | tf_op jit(solution)/shard_map/pallas_call | solution.py:377
  19.3 1.0 %collective-permute-done.2.rest_0_ = bf16[2,256,256]{2,1,0:T(8,128)(2,1)S(1)} collective-permute-done((bf16[2,256,256]{2,1,0:T(8,128)(2,1)S(1)}, bf16[2,256,256]{2,1,0:T(8,128)(2,1)S(1)}, u32[]{:S(2)}, u32[]{:S(2)}) %collective-permute-start.2) | collective-permute-done | bytes 262176 | tf_op jit(solution)/shard_map/ppermute | solution.py:288
  20.4 0.1 collective-permute-done.3.rest_1_
  20.5 0.5 collective-permute-start.10
  21.0 1.7 %collective-permute-start.7 = (bf16[2,256,256]{2,1,0:T(8,128)(2,1)S(1)}, bf16[2,256,256]{2,1,0:T(8,128)(2,1)S(1)}, u32[]{:S(2)}, u32[]{:S(2)}) collective-permute-start(bf16[2,256,256]{2,1,0:T(8,128)(2,1)S(1)} %collective-permute-done.2.rest_0_), channel_id=1, source_target_pairs={{0,4},{1,5},{4,8},{5,9},{8,12},{9,13},{12,14},{13,15},{14,10},{15,... | collective-permute-start | bytes 786440 | tf_op jit(solution)/shard_map/ppermute | solution.py:288
  22.7 0.3 collective-permute-start.8
  23.0 5.9 %shard_map.79 = (f32[33,256,256]{2,1,0:T(8,128)S(1)}, bf16[32,256,256]{2,1,0:T(8,128)(2,1)S(1)}) custom-call(s32[128]{0:T(128)S(1)} %get-tuple-element.62.plan_ref, s32[6]{0:T(128)S(1)} %get-tuple-element.63.bounds_ref, bf16[92,256,256]{2,1,0:T(8,128)(2,1)S(1)} %get-tuple-element.64.left, ...), custom_call_target="tpu_custom_call", output_to_operand_aliasing={{0}: (8, {}), {1}: (9, {})} | custom-call | flops 1234803072 | bytes 1048576 | tf_op jit(solution)/shard_map/pallas_call | solution.py:377
  29.0 0.2 collective-permute-done.7.rest_0_
  29.2 1.4 %collective-permute-done.8.rest_1_ = bf16[2,256,256]{2,1,0:T(8,128)(2,1)S(1)} collective-permute-done((bf16[2,256,256]{2,1,0:T(8,128)(2,1)S(1)}, bf16[2,256,256]{2,1,0:T(8,128)(2,1)S(1)}, u32[]{:S(2)}, u32[]{:S(2)}) %collective-permute-start.8) | collective-permute-done | bytes 262176 | tf_op jit(solution)/shard_map/ppermute | solution.py:291
  30.6 0.5 collective-permute-start.14
  31.1 0.0 copy-start.2
  31.2 0.4 collective-permute-start.12
  31.6 1.7 %collective-permute-start.11 = (bf16[1,256,256]{2,1,0:T(8,128)(2,1)S(1)}, bf16[1,256,256]{2,1,0:T(8,128)(2,1)S(1)}, u32[]{:S(2)}, u32[]{:S(2)}) collective-permute-start(bf16[1,256,256]{2,1,0:T(8,128)(2,1)S(1)} %slice.6), channel_id=1, source_target_pairs={{0,4},{1,5},{4,8},{5,9},{8,12},{9,13},{12,14},{13,15},{14,10},{15,... | collective-permute-start | bytes 393224 | tf_op jit(solution)/shard_map/ppermute | solution.py:288
  33.2 3.5 %shard_map.80 = (f32[33,256,256]{2,1,0:T(8,128)S(1)}, bf16[32,256,256]{2,1,0:T(8,128)(2,1)S(1)}) custom-call(s32[128]{0:T(128)S(1)} %get-tuple-element.62.plan_ref, s32[6]{0:T(128)S(1)} %get-tuple-element.63.bounds_ref, bf16[92,256,256]{2,1,0:T(8,128)(2,1)S(1)} %get-tuple-element.64.left, ...), custom_call_target="tpu_custom_call", output_to_operand_aliasing={{0}: (8, {}), {1}: (9, {})} | custom-call | flops 1234803072 | bytes 1048576 | tf_op jit(solution)/shard_map/pallas_call | solution.py:377
  36.8 0.0 collective-permute-done.11.rest_0_
  36.8 0.3 collective-permute-start.15
  37.1 0.3 collective-permute-start.16
  37.4 0.8 %collective-permute-done.15.rest_2_ = bf16[1,256,256]{2,1,0:T(8,128)(2,1)S(1)} collective-permute-done((bf16[1,256,256]{2,1,0:T(8,128)(2,1)S(1)}, bf16[1,256,256]{2,1,0:T(8,128)(2,1)S(1)}, u32[]{:S(2)}, u32[]{:S(2)}) %collective-permute-start.15) | collective-permute-done | bytes 131104 | tf_op jit(solution)/shard_map/ppermute | solution.py:294
  38.2 0.2 collective-permute-done.16.rest_3_
  38.5 6.2 %shard_map.81 = (f32[33,256,256]{2,1,0:T(8,128)S(1)}, bf16[32,256,256]{2,1,0:T(8,128)(2,1)S(1)}, f32[4,272,256]{2,1,0:T(8,128)S(1)}, f32[12,272,256]{2,1,0:T(8,1...) custom-call(s32[128]{0:T(128)S(1)} %get-tuple-element.62.plan_ref, ...), custom_call_target="tpu_custom_call", output_to_operand_aliasing={{0}: (10, {}), {1}: (11, {})} | custom-call | flops 1234803072 | bytes 1048576 | tf_op jit(solution)/shard_map/pallas_call | solution.py:377
  44.7 1.2 %collective-permute-start.17 = (f32[4,272,256]{2,1,0:T(8,128)S(1)}, f32[4,272,256]{2,1,0:T(8,128)S(1)}, u32[]{:S(2)}, u32[]{:S(2)}) collective-permute-start(f32[4,272,256]{2,1,0:T(8,128)S(1)} %get-tuple-element.92), channel_id=1, source_target_pairs={{0,1},{1,0},{2,3},{3,2},{4,5},{5,4},{6,7},{7,6},{8,9},{9,8},{10,11... | collective-permute-start | bytes 3342344 | tf_op jit(solution)/shard_map/ppermute | solution.py:294
  45.9 2.4 %collective-permute-done.17.other = f32[4,272,256]{2,1,0:T(8,128)S(1)} collective-permute-done((f32[4,272,256]{2,1,0:T(8,128)S(1)}, f32[4,272,256]{2,1,0:T(8,128)S(1)}, u32[]{:S(2)}, u32[]{:S(2)}) %collective-permute-start.17) | collective-permute-done | bytes 1114144 | tf_op jit(solution)/shard_map/ppermute | solution.py:294
  48.2 0.4 collective-permute-start.18
  48.6 0.2 shard_map.83
  48.8 2.2 %collective-permute-start.19 = (f16[1,272,256]{2,1,0:T(8,128)(2,1)S(1)}, f16[1,272,256]{2,1,0:T(8,128)(2,1)S(1)}, u32[]{:S(2)}, u32[]{:S(2)}) collective-permute-start(f16[1,272,256]{2,1,0:T(8,128)(2,1)S(1)} %convert_element_type.84), channel_id=1, source_target_pairs={{0,4},{1,5},{4,8},{5,9},{8,12},{9,13},{12,14},{13,15},{14,10},{15,... | collective-permute-start | bytes 417800 | tf_op jit(solution)/shard_map/ppermute | solution.py:288
  51.1 0.1 collective-permute-start.20
  51.2 2.1 %collective-permute-start.23 = (f16[1,256,256]{2,1,0:T(8,128)(2,1)S(1)}, f16[1,256,256]{2,1,0:T(8,128)(2,1)S(1)}, u32[]{:S(2)}, u32[]{:S(2)}) collective-permute-start(f16[1,256,256]{2,1,0:T(8,128)(2,1)S(1)} %convert_element_type.86), channel_id=1, source_target_pairs={{0,4},{1,5},{4,8},{5,9},{8,12},{9,13},{12,14},{13,15},{14,10},{15,... | collective-permute-start | bytes 393224 | tf_op jit(solution)/shard_map/ppermute | solution.py:288
  53.3 0.0 collective-permute-start.24
  53.3 4.2 %collective-permute-done.20 = f16[1,256,256]{2,1,0:T(8,128)(2,1)S(1)} collective-permute-done((f16[1,256,256]{2,1,0:T(8,128)(2,1)S(1)}, f16[1,256,256]{2,1,0:T(8,128)(2,1)S(1)}, u32[]{:S(2)}, u32[]{:S(2)}) %collective-permute-start.20) | collective-permute-done | bytes 131104 | tf_op jit(solution)/shard_map/ppermute | solution.py:291
  57.5 0.6 shard_map.82
  58.1 0.0 copy-start
  58.1 0.0 copy-start.1
  58.1 0.1 add_convert_fusion.9
  58.1 0.1 collective-permute-start.22
  58.2 0.1 add_convert_fusion.4
  58.3 2.1 %collective-permute-start.21 = (f16[1,272,256]{2,1,0:T(8,128)(2,1)S(1)}, f16[1,272,256]{2,1,0:T(8,128)(2,1)S(1)}, u32[]{:S(2)}, u32[]{:S(2)}) collective-permute-start(f16[1,272,256]{2,1,0:T(8,128)(2,1)S(1)} %add_convert_fusion.4), channel_id=1, source_target_pairs={{0,4},{1,5},{4,8},{5,9},{8,12},{9,13},{12,14},{13,15},{14,10},{15,... | collective-permute-start | bytes 417800 | tf_op jit(solution)/shard_map/ppermute | solution.py:288
  60.4 0.6 collective-permute-start.27
  61.0 1.6 %collective-permute-start.28 = (f16[1,272,256]{2,1,0:T(8,128)(2,1)S(1)}, f16[1,272,256]{2,1,0:T(8,128)(2,1)S(1)}, u32[]{:S(2)}, u32[]{:S(2)}) collective-permute-start(f16[1,272,256]{2,1,0:T(8,128)(2,1)S(1)} %add_convert_fusion.3), channel_id=1, source_target_pairs={{0,2},{1,3},{4,0},{5,1},{8,4},{9,5},{12,8},{13,9},{14,12},{15,13},... | collective-permute-start | bytes 417800 | tf_op jit(solution)/shard_map/ppermute | solution.py:291
  62.6 1.4 %collective-permute-done.22 = f16[1,256,256]{2,1,0:T(8,128)(2,1)S(1)} collective-permute-done((f16[1,256,256]{2,1,0:T(8,128)(2,1)S(1)}, f16[1,256,256]{2,1,0:T(8,128)(2,1)S(1)}, u32[]{:S(2)}, u32[]{:S(2)}) %collective-permute-start.22) | collective-permute-done | bytes 131104 | tf_op jit(solution)/shard_map/ppermute | solution.py:291
  63.9 0.5 collective-permute-done.21
  64.5 1.1 %collective-permute-start.26 = (f16[1,256,256]{2,1,0:T(8,128)(2,1)S(1)}, f16[1,256,256]{2,1,0:T(8,128)(2,1)S(1)}, u32[]{:S(2)}, u32[]{:S(2)}) collective-permute-start(f16[1,256,256]{2,1,0:T(8,128)(2,1)S(1)} %add_convert_fusion.7), channel_id=1, source_target_pairs={{0,2},{1,3},{4,0},{5,1},{8,4},{9,5},{12,8},{13,9},{14,12},{15,13},... | collective-permute-start | bytes 393224 | tf_op jit(solution)/shard_map/ppermute | solution.py:291
  65.6 0.1 add_convert_fusion.2
  65.6 1.0 %collective-permute-start.25 = (f16[1,272,256]{2,1,0:T(8,128)(2,1)S(1)}, f16[1,272,256]{2,1,0:T(8,128)(2,1)S(1)}, u32[]{:S(2)}, u32[]{:S(2)}) collective-permute-start(f16[1,272,256]{2,1,0:T(8,128)(2,1)S(1)} %add_convert_fusion.2), channel_id=1, source_target_pairs={{0,4},{1,5},{4,8},{5,9},{8,12},{9,13},{12,14},{13,15},{14,10},{15,... | collective-permute-start | bytes 417800 | tf_op jit(solution)/shard_map/ppermute | solution.py:288
  66.7 0.9 %collective-permute-done.28 = f16[1,272,256]{2,1,0:T(8,128)(2,1)S(1)} collective-permute-done((f16[1,272,256]{2,1,0:T(8,128)(2,1)S(1)}, f16[1,272,256]{2,1,0:T(8,128)(2,1)S(1)}, u32[]{:S(2)}, u32[]{:S(2)}) %collective-permute-start.28) | collective-permute-done | bytes 139296 | tf_op jit(solution)/shard_map/ppermute | solution.py:291
  67.6 0.8 collective-permute-start.30
  68.4 1.3 %collective-permute-start.31 = (f16[1,272,256]{2,1,0:T(8,128)(2,1)S(1)}, f16[1,272,256]{2,1,0:T(8,128)(2,1)S(1)}, u32[]{:S(2)}, u32[]{:S(2)}) collective-permute-start(f16[1,272,256]{2,1,0:T(8,128)(2,1)S(1)} %add_convert_fusion.1), channel_id=1, source_target_pairs={{0,2},{1,3},{4,0},{5,1},{8,4},{9,5},{12,8},{13,9},{14,12},{15,13},... | collective-permute-start | bytes 417800 | tf_op jit(solution)/shard_map/ppermute | solution.py:291
  69.8 1.1 %collective-permute-done.26 = f16[1,256,256]{2,1,0:T(8,128)(2,1)S(1)} collective-permute-done((f16[1,256,256]{2,1,0:T(8,128)(2,1)S(1)}, f16[1,256,256]{2,1,0:T(8,128)(2,1)S(1)}, u32[]{:S(2)}, u32[]{:S(2)}) %collective-permute-start.26) | collective-permute-done | bytes 131104 | tf_op jit(solution)/shard_map/ppermute | solution.py:291
  70.9 0.3 collective-permute-done.25
  71.3 1.2 %collective-permute-start.29 = (f16[1,272,256]{2,1,0:T(8,128)(2,1)S(1)}, f16[1,272,256]{2,1,0:T(8,128)(2,1)S(1)}, u32[]{:S(2)}, u32[]{:S(2)}) collective-permute-start(f16[1,272,256]{2,1,0:T(8,128)(2,1)S(1)} %add_convert_fusion), channel_id=1, source_target_pairs={{0,4},{1,5},{4,8},{5,9},{8,12},{9,13},{12,14},{13,15},{14,10},{15,... | collective-permute-start | bytes 417800 | tf_op jit(solution)/shard_map/ppermute | solution.py:288
  72.5 1.0 %collective-permute-start.32 = (f16[1,256,256]{2,1,0:T(8,128)(2,1)S(1)}, f16[1,256,256]{2,1,0:T(8,128)(2,1)S(1)}, u32[]{:S(2)}, u32[]{:S(2)}) collective-permute-start(f16[1,256,256]{2,1,0:T(8,128)(2,1)S(1)} %add_convert_fusion.5), channel_id=1, source_target_pairs={{0,2},{1,3},{4,0},{5,1},{8,4},{9,5},{12,8},{13,9},{14,12},{15,13},... | collective-permute-start | bytes 393224 | tf_op jit(solution)/shard_map/ppermute | solution.py:291
  73.5 0.2 collective-permute-done.30
  73.7 0.2 collective-permute-done.31
  73.9 3.6 %collective-permute-done.32 = f16[1,256,256]{2,1,0:T(8,128)(2,1)S(1)} collective-permute-done((f16[1,256,256]{2,1,0:T(8,128)(2,1)S(1)}, f16[1,256,256]{2,1,0:T(8,128)(2,1)S(1)}, u32[]{:S(2)}, u32[]{:S(2)}) %collective-permute-start.32) | collective-permute-done | bytes 131104 | tf_op jit(solution)/shard_map/ppermute | solution.py:291
  77.6 1.3 %shard_map.84 = (f32[2,256,256]{2,1,0:T(8,128)}, f32[1]{0:T(128)}) custom-call(f32[3,8,128]{2,1,0:T(8,128)S(1)} %copy-done.2, f32[8,128]{1,0:T(8,128)S(1)} %get-tuple-element.90.scales, f32[2,272,256]{2,1,0:T(8,128)S(1)} %get-tuple-element.96.home, f32[1,272,256]{2,1,0:T(8,128)S(1)} %convert_element_type.106.r0, ...), custom_call_target="tpu_custom_call" | custom-call | bytes 2097152 | tf_op jit(solution)/shard_map/pallas_call | solution.py:438
  (36 shorter events, 0.5 us)
Async XLA Ops:
  0.6 9.6 %collective-permute-start.1 = (bf16[2,256,256]{2,1,0:T(8,128)(2,1)}, bf16[2,256,256]{2,1,0:T(8,128)(2,1)S(1)}, u32[]{:S(2)}, u32[]{:S(2)}) collective-permute-start(bf16[2,256,256]{2,1,0:T(8,128)(2,1)} %psi_ref.1), channel_id=1, source_target_pairs={{0,2},{1,3},{4,0},{5,1},{8,4},{9,5},{12,8},{13,9},{14,12},{15,13},... | collective-permute-start | bytes 786440 | tf_op jit(solution)/shard_map/ppermute | solution.py:291
  3.6 8.0 %collective-permute-start = (bf16[2,256,256]{2,1,0:T(8,128)(2,1)}, bf16[2,256,256]{2,1,0:T(8,128)(2,1)S(1)}, u32[]{:S(2)}, u32[]{:S(2)}) collective-permute-start(bf16[2,256,256]{2,1,0:T(8,128)(2,1)} %psi_ref.1), channel_id=1, source_target_pairs={{0,4},{1,5},{4,8},{5,9},{8,12},{9,13},{12,14},{13,15},{14,10},{15,... | collective-permute-start | bytes 786440 | tf_op jit(solution)/shard_map/ppermute | solution.py:288
  3.8 10.4 %collective-permute-start.4 = (bf16[2,256,256]{2,1,0:T(8,128)(2,1)}, bf16[2,256,256]{2,1,0:T(8,128)(2,1)S(1)}, u32[]{:S(2)}, u32[]{:S(2)}) collective-permute-start(bf16[2,256,256]{2,1,0:T(8,128)(2,1)} %psi_ref.1), channel_id=1, source_target_pairs={{0,1},{1,0},{2,3},{3,2},{4,5},{5,4},{6,7},{7,6},{8,9},{9,8},{10,11... | collective-permute-start | bytes 786440 | tf_op jit(solution)/shard_map/ppermute | solution.py:294
  11.6 2.5 %collective-permute-start.5 = (bf16[2,256,256]{2,1,0:T(8,128)(2,1)S(1)}, bf16[2,256,256]{2,1,0:T(8,128)(2,1)S(1)}, u32[]{:S(2)}, u32[]{:S(2)}) collective-permute-start(bf16[2,256,256]{2,1,0:T(8,128)(2,1)S(1)} %collective-permute-done.rest_2_), channel_id=1, source_target_pairs={{0,1},{1,0},{2,3},{3,2},{4,5},{5,4},{6,7},{7,6},{8,9},{9,8},{10,11... | collective-permute-start | bytes 786440 | tf_op jit(solution)/shard_map/ppermute | solution.py:294
  11.6 2.5 %collective-permute-start.6 = (bf16[2,256,256]{2,1,0:T(8,128)(2,1)S(1)}, bf16[2,256,256]{2,1,0:T(8,128)(2,1)S(1)}, u32[]{:S(2)}, u32[]{:S(2)}) collective-permute-start(bf16[2,256,256]{2,1,0:T(8,128)(2,1)S(1)} %collective-permute-done.1.rest_3_), channel_id=1, source_target_pairs={{0,1},{1,0},{2,3},{3,2},{4,5},{5,4},{6,7},{7,6},{8,9},{9,8},{10,11... | collective-permute-start | bytes 786440 | tf_op jit(solution)/shard_map/ppermute | solution.py:294
  12.1 8.2 %collective-permute-start.2 = (bf16[2,256,256]{2,1,0:T(8,128)(2,1)S(1)}, bf16[2,256,256]{2,1,0:T(8,128)(2,1)S(1)}, u32[]{:S(2)}, u32[]{:S(2)}) collective-permute-start(bf16[2,256,256]{2,1,0:T(8,128)(2,1)S(1)} %collective-permute-done.rest_2_), channel_id=1, source_target_pairs={{0,4},{1,5},{4,8},{5,9},{8,12},{9,13},{12,14},{13,15},{14,10},{15,... | collective-permute-start | bytes 786440 | tf_op jit(solution)/shard_map/ppermute | solution.py:288
  12.5 7.9 %collective-permute-start.3 = (bf16[2,256,256]{2,1,0:T(8,128)(2,1)S(1)}, bf16[2,256,256]{2,1,0:T(8,128)(2,1)S(1)}, u32[]{:S(2)}, u32[]{:S(2)}) collective-permute-start(bf16[2,256,256]{2,1,0:T(8,128)(2,1)S(1)} %collective-permute-done.1.rest_3_), channel_id=1, source_target_pairs={{0,2},{1,3},{4,0},{5,1},{8,4},{9,5},{12,8},{13,9},{14,12},{15,13},... | collective-permute-start | bytes 786440 | tf_op jit(solution)/shard_map/ppermute | solution.py:291
  20.5 2.5 %collective-permute-start.9 = (bf16[2,256,256]{2,1,0:T(8,128)(2,1)S(1)}, bf16[2,256,256]{2,1,0:T(8,128)(2,1)S(1)}, u32[]{:S(2)}, u32[]{:S(2)}) collective-permute-start(bf16[2,256,256]{2,1,0:T(8,128)(2,1)S(1)} %collective-permute-done.2.rest_0_), channel_id=1, source_target_pairs={{0,1},{1,0},{2,3},{3,2},{4,5},{5,4},{6,7},{7,6},{8,9},{9,8},{10,11... | collective-permute-start | bytes 786440 | tf_op jit(solution)/shard_map/ppermute | solution.py:294
  20.5 2.5 %collective-permute-start.10 = (bf16[2,256,256]{2,1,0:T(8,128)(2,1)S(1)}, bf16[2,256,256]{2,1,0:T(8,128)(2,1)S(1)}, u32[]{:S(2)}, u32[]{:S(2)}) collective-permute-start(bf16[2,256,256]{2,1,0:T(8,128)(2,1)S(1)} %collective-permute-done.3.rest_1_), channel_id=1, source_target_pairs={{0,1},{1,0},{2,3},{3,2},{4,5},{5,4},{6,7},{7,6},{8,9},{9,8},{10,11... | collective-permute-start | bytes 786440 | tf_op jit(solution)/shard_map/ppermute | solution.py:294
  21.0 8.2 %collective-permute-start.7 = (bf16[2,256,256]{2,1,0:T(8,128)(2,1)S(1)}, bf16[2,256,256]{2,1,0:T(8,128)(2,1)S(1)}, u32[]{:S(2)}, u32[]{:S(2)}) collective-permute-start(bf16[2,256,256]{2,1,0:T(8,128)(2,1)S(1)} %collective-permute-done.2.rest_0_), channel_id=1, source_target_pairs={{0,4},{1,5},{4,8},{5,9},{8,12},{9,13},{12,14},{13,15},{14,10},{15,... | collective-permute-start | bytes 786440 | tf_op jit(solution)/shard_map/ppermute | solution.py:288
  22.7 7.9 %collective-permute-start.8 = (bf16[2,256,256]{2,1,0:T(8,128)(2,1)S(1)}, bf16[2,256,256]{2,1,0:T(8,128)(2,1)S(1)}, u32[]{:S(2)}, u32[]{:S(2)}) collective-permute-start(bf16[2,256,256]{2,1,0:T(8,128)(2,1)S(1)} %collective-permute-done.3.rest_1_), channel_id=1, source_target_pairs={{0,2},{1,3},{4,0},{5,1},{8,4},{9,5},{12,8},{13,9},{14,12},{15,13},... | collective-permute-start | bytes 786440 | tf_op jit(solution)/shard_map/ppermute | solution.py:291
  30.6 2.6 %collective-permute-start.13 = (bf16[2,256,256]{2,1,0:T(8,128)(2,1)S(1)}, bf16[2,256,256]{2,1,0:T(8,128)(2,1)S(1)}, u32[]{:S(2)}, u32[]{:S(2)}) collective-permute-start(bf16[2,256,256]{2,1,0:T(8,128)(2,1)S(1)} %collective-permute-done.7.rest_0_), channel_id=1, source_target_pairs={{0,1},{1,0},{2,3},{3,2},{4,5},{5,4},{6,7},{7,6},{8,9},{9,8},{10,11... | collective-permute-start | bytes 786440 | tf_op jit(solution)/shard_map/ppermute | solution.py:294
  30.6 2.6 %collective-permute-start.14 = (bf16[2,256,256]{2,1,0:T(8,128)(2,1)S(1)}, bf16[2,256,256]{2,1,0:T(8,128)(2,1)S(1)}, u32[]{:S(2)}, u32[]{:S(2)}) collective-permute-start(bf16[2,256,256]{2,1,0:T(8,128)(2,1)S(1)} %collective-permute-done.8.rest_1_), channel_id=1, source_target_pairs={{0,1},{1,0},{2,3},{3,2},{4,5},{5,4},{6,7},{7,6},{8,9},{9,8},{10,11... | collective-permute-start | bytes 786440 | tf_op jit(solution)/shard_map/ppermute | solution.py:294
  31.1 7.3 %copy-start.2 = (f32[3,8,128]{2,1,0:T(8,128)S(1)}, f32[3,8,128]{2,1,0:T(8,128)}, u32[]{:S(2)}) copy-start(f32[3,8,128]{2,1,0:T(8,128)} %constant.6.clone.rest_5_.digit_ref) | copy-start | bytes 36868
  31.2 5.6 %collective-permute-start.12 = (bf16[1,256,256]{2,1,0:T(8,128)(2,1)S(1)}, bf16[1,256,256]{2,1,0:T(8,128)(2,1)S(1)}, u32[]{:S(2)}, u32[]{:S(2)}) collective-permute-start(bf16[1,256,256]{2,1,0:T(8,128)(2,1)S(1)} %slice.7), channel_id=1, source_target_pairs={{0,2},{1,3},{4,0},{5,1},{8,4},{9,5},{12,8},{13,9},{14,12},{15,13},... | collective-permute-start | bytes 393224 | tf_op jit(solution)/shard_map/ppermute | solution.py:291
  31.6 5.2 %collective-permute-start.11 = (bf16[1,256,256]{2,1,0:T(8,128)(2,1)S(1)}, bf16[1,256,256]{2,1,0:T(8,128)(2,1)S(1)}, u32[]{:S(2)}, u32[]{:S(2)}) collective-permute-start(bf16[1,256,256]{2,1,0:T(8,128)(2,1)S(1)} %slice.6), channel_id=1, source_target_pairs={{0,4},{1,5},{4,8},{5,9},{8,12},{9,13},{12,14},{13,15},{14,10},{15,... | collective-permute-start | bytes 393224 | tf_op jit(solution)/shard_map/ppermute | solution.py:288
  36.8 1.4 %collective-permute-start.15 = (bf16[1,256,256]{2,1,0:T(8,128)(2,1)S(1)}, bf16[1,256,256]{2,1,0:T(8,128)(2,1)S(1)}, u32[]{:S(2)}, u32[]{:S(2)}) collective-permute-start(bf16[1,256,256]{2,1,0:T(8,128)(2,1)S(1)} %collective-permute-done.11.rest_0_), channel_id=1, source_target_pairs={{0,1},{1,0},{2,3},{3,2},{4,5},{5,4},{6,7},{7,6},{8,9},{9,8},{10,11... | collective-permute-start | bytes 393224 | tf_op jit(solution)/shard_map/ppermute | solution.py:294
  37.1 1.3 %collective-permute-start.16 = (bf16[1,256,256]{2,1,0:T(8,128)(2,1)S(1)}, bf16[1,256,256]{2,1,0:T(8,128)(2,1)S(1)}, u32[]{:S(2)}, u32[]{:S(2)}) collective-permute-start(bf16[1,256,256]{2,1,0:T(8,128)(2,1)S(1)} %collective-permute-done.12.rest_1_), channel_id=1, source_target_pairs={{0,1},{1,0},{2,3},{3,2},{4,5},{5,4},{6,7},{7,6},{8,9},{9,8},{10,11... | collective-permute-start | bytes 393224 | tf_op jit(solution)/shard_map/ppermute | solution.py:294
  44.7 3.5 %collective-permute-start.17 = (f32[4,272,256]{2,1,0:T(8,128)S(1)}, f32[4,272,256]{2,1,0:T(8,128)S(1)}, u32[]{:S(2)}, u32[]{:S(2)}) collective-permute-start(f32[4,272,256]{2,1,0:T(8,128)S(1)} %get-tuple-element.92), channel_id=1, source_target_pairs={{0,1},{1,0},{2,3},{3,2},{4,5},{5,4},{6,7},{7,6},{8,9},{9,8},{10,11... | collective-permute-start | bytes 3342344 | tf_op jit(solution)/shard_map/ppermute | solution.py:294
  48.2 9.2 %collective-permute-start.18 = (f32[12,272,256]{2,1,0:T(8,128)S(1)}, f32[12,272,256]{2,1,0:T(8,128)S(1)}, u32[]{:S(2)}, u32[]{:S(2)}) collective-permute-start(f32[12,272,256]{2,1,0:T(8,128)S(1)} %get-tuple-element.94), channel_id=1, source_target_pairs={{0,1},{1,0},{2,3},{3,2},{4,5},{5,4},{6,7},{7,6},{8,9},{9,8},{10,11... | collective-permute-start | bytes 10027016 | tf_op jit(solution)/shard_map/ppermute | solution.py:294
  48.8 8.7 %collective-permute-start.19 = (f16[1,272,256]{2,1,0:T(8,128)(2,1)S(1)}, f16[1,272,256]{2,1,0:T(8,128)(2,1)S(1)}, u32[]{:S(2)}, u32[]{:S(2)}) collective-permute-start(f16[1,272,256]{2,1,0:T(8,128)(2,1)S(1)} %convert_element_type.84), channel_id=1, source_target_pairs={{0,4},{1,5},{4,8},{5,9},{8,12},{9,13},{12,14},{13,15},{14,10},{15,... | collective-permute-start | bytes 417800 | tf_op jit(solution)/shard_map/ppermute | solution.py:288
  51.1 6.4 %collective-permute-start.20 = (f16[1,256,256]{2,1,0:T(8,128)(2,1)S(1)}, f16[1,256,256]{2,1,0:T(8,128)(2,1)S(1)}, u32[]{:S(2)}, u32[]{:S(2)}) collective-permute-start(f16[1,256,256]{2,1,0:T(8,128)(2,1)S(1)} %convert_element_type.85), channel_id=1, source_target_pairs={{0,2},{1,3},{4,0},{5,1},{8,4},{9,5},{12,8},{13,9},{14,12},{15,13},... | collective-permute-start | bytes 393224 | tf_op jit(solution)/shard_map/ppermute | solution.py:291
  51.2 9.1 %collective-permute-start.23 = (f16[1,256,256]{2,1,0:T(8,128)(2,1)S(1)}, f16[1,256,256]{2,1,0:T(8,128)(2,1)S(1)}, u32[]{:S(2)}, u32[]{:S(2)}) collective-permute-start(f16[1,256,256]{2,1,0:T(8,128)(2,1)S(1)} %convert_element_type.86), channel_id=1, source_target_pairs={{0,4},{1,5},{4,8},{5,9},{8,12},{9,13},{12,14},{13,15},{14,10},{15,... | collective-permute-start | bytes 393224 | tf_op jit(solution)/shard_map/ppermute | solution.py:288
  53.3 7.1 %collective-permute-start.24 = (f16[1,272,256]{2,1,0:T(8,128)(2,1)S(1)}, f16[1,272,256]{2,1,0:T(8,128)(2,1)S(1)}, u32[]{:S(2)}, u32[]{:S(2)}) collective-permute-start(f16[1,272,256]{2,1,0:T(8,128)(2,1)S(1)} %convert_element_type.87), channel_id=1, source_target_pairs={{0,2},{1,3},{4,0},{5,1},{8,4},{9,5},{12,8},{13,9},{14,12},{15,13},... | collective-permute-start | bytes 417800 | tf_op jit(solution)/shard_map/ppermute | solution.py:291
  58.1 19.5 %copy-start = (bf16[3,2,256,256]{3,2,1,0:T(8,128)(2,1)S(1)}, bf16[3,2,256,256]{3,2,1,0:T(8,128)(2,1)}, u32[]{:S(2)}) copy-start(bf16[3,2,256,256]{3,2,1,0:T(8,128)(2,1)} %lower_ref.1) | copy-start | bytes 2359300
  58.1 19.5 %copy-start.1 = (bf16[2,256,256]{2,1,0:T(8,128)(2,1)S(1)}, bf16[2,256,256]{2,1,0:T(8,128)(2,1)}, u32[]{:S(2)}) copy-start(bf16[2,256,256]{2,1,0:T(8,128)(2,1)} %psi_ref.1) | copy-start | bytes 786436
  58.1 5.8 %collective-permute-start.22 = (f16[1,256,256]{2,1,0:T(8,128)(2,1)S(1)}, f16[1,256,256]{2,1,0:T(8,128)(2,1)S(1)}, u32[]{:S(2)}, u32[]{:S(2)}) collective-permute-start(f16[1,256,256]{2,1,0:T(8,128)(2,1)S(1)} %add_convert_fusion.9), channel_id=1, source_target_pairs={{0,2},{1,3},{4,0},{5,1},{8,4},{9,5},{12,8},{13,9},{14,12},{15,13},... | collective-permute-start | bytes 393224 | tf_op jit(solution)/shard_map/ppermute | solution.py:291
  58.3 6.2 %collective-permute-start.21 = (f16[1,272,256]{2,1,0:T(8,128)(2,1)S(1)}, f16[1,272,256]{2,1,0:T(8,128)(2,1)S(1)}, u32[]{:S(2)}, u32[]{:S(2)}) collective-permute-start(f16[1,272,256]{2,1,0:T(8,128)(2,1)S(1)} %add_convert_fusion.4), channel_id=1, source_target_pairs={{0,4},{1,5},{4,8},{5,9},{8,12},{9,13},{12,14},{13,15},{14,10},{15,... | collective-permute-start | bytes 417800 | tf_op jit(solution)/shard_map/ppermute | solution.py:288
  60.4 6.3 %collective-permute-start.27 = (f16[1,256,256]{2,1,0:T(8,128)(2,1)S(1)}, f16[1,256,256]{2,1,0:T(8,128)(2,1)S(1)}, u32[]{:S(2)}, u32[]{:S(2)}) collective-permute-start(f16[1,256,256]{2,1,0:T(8,128)(2,1)S(1)} %add_convert_fusion.8), channel_id=1, source_target_pairs={{0,4},{1,5},{4,8},{5,9},{8,12},{9,13},{12,14},{13,15},{14,10},{15,... | collective-permute-start | bytes 393224 | tf_op jit(solution)/shard_map/ppermute | solution.py:288
  61.0 6.6 %collective-permute-start.28 = (f16[1,272,256]{2,1,0:T(8,128)(2,1)S(1)}, f16[1,272,256]{2,1,0:T(8,128)(2,1)S(1)}, u32[]{:S(2)}, u32[]{:S(2)}) collective-permute-start(f16[1,272,256]{2,1,0:T(8,128)(2,1)S(1)} %add_convert_fusion.3), channel_id=1, source_target_pairs={{0,2},{1,3},{4,0},{5,1},{8,4},{9,5},{12,8},{13,9},{14,12},{15,13},... | collective-permute-start | bytes 417800 | tf_op jit(solution)/shard_map/ppermute | solution.py:291
  64.5 6.4 %collective-permute-start.26 = (f16[1,256,256]{2,1,0:T(8,128)(2,1)S(1)}, f16[1,256,256]{2,1,0:T(8,128)(2,1)S(1)}, u32[]{:S(2)}, u32[]{:S(2)}) collective-permute-start(f16[1,256,256]{2,1,0:T(8,128)(2,1)S(1)} %add_convert_fusion.7), channel_id=1, source_target_pairs={{0,2},{1,3},{4,0},{5,1},{8,4},{9,5},{12,8},{13,9},{14,12},{15,13},... | collective-permute-start | bytes 393224 | tf_op jit(solution)/shard_map/ppermute | solution.py:291
  65.6 5.6 %collective-permute-start.25 = (f16[1,272,256]{2,1,0:T(8,128)(2,1)S(1)}, f16[1,272,256]{2,1,0:T(8,128)(2,1)S(1)}, u32[]{:S(2)}, u32[]{:S(2)}) collective-permute-start(f16[1,272,256]{2,1,0:T(8,128)(2,1)S(1)} %add_convert_fusion.2), channel_id=1, source_target_pairs={{0,4},{1,5},{4,8},{5,9},{8,12},{9,13},{12,14},{13,15},{14,10},{15,... | collective-permute-start | bytes 417800 | tf_op jit(solution)/shard_map/ppermute | solution.py:288
  67.6 6.0 %collective-permute-start.30 = (f16[1,256,256]{2,1,0:T(8,128)(2,1)S(1)}, f16[1,256,256]{2,1,0:T(8,128)(2,1)S(1)}, u32[]{:S(2)}, u32[]{:S(2)}) collective-permute-start(f16[1,256,256]{2,1,0:T(8,128)(2,1)S(1)} %add_convert_fusion.6), channel_id=1, source_target_pairs={{0,4},{1,5},{4,8},{5,9},{8,12},{9,13},{12,14},{13,15},{14,10},{15,... | collective-permute-start | bytes 393224 | tf_op jit(solution)/shard_map/ppermute | solution.py:288
  68.4 5.4 %collective-permute-start.31 = (f16[1,272,256]{2,1,0:T(8,128)(2,1)S(1)}, f16[1,272,256]{2,1,0:T(8,128)(2,1)S(1)}, u32[]{:S(2)}, u32[]{:S(2)}) collective-permute-start(f16[1,272,256]{2,1,0:T(8,128)(2,1)S(1)} %add_convert_fusion.1), channel_id=1, source_target_pairs={{0,2},{1,3},{4,0},{5,1},{8,4},{9,5},{12,8},{13,9},{14,12},{15,13},... | collective-permute-start | bytes 417800 | tf_op jit(solution)/shard_map/ppermute | solution.py:291
  71.3 6.3 %collective-permute-start.29 = (f16[1,272,256]{2,1,0:T(8,128)(2,1)S(1)}, f16[1,272,256]{2,1,0:T(8,128)(2,1)S(1)}, u32[]{:S(2)}, u32[]{:S(2)}) collective-permute-start(f16[1,272,256]{2,1,0:T(8,128)(2,1)S(1)} %add_convert_fusion), channel_id=1, source_target_pairs={{0,4},{1,5},{4,8},{5,9},{8,12},{9,13},{12,14},{13,15},{14,10},{15,... | collective-permute-start | bytes 417800 | tf_op jit(solution)/shard_map/ppermute | solution.py:288
  72.5 5.0 %collective-permute-start.32 = (f16[1,256,256]{2,1,0:T(8,128)(2,1)S(1)}, f16[1,256,256]{2,1,0:T(8,128)(2,1)S(1)}, u32[]{:S(2)}, u32[]{:S(2)}) collective-permute-start(f16[1,256,256]{2,1,0:T(8,128)(2,1)S(1)} %add_convert_fusion.5), channel_id=1, source_target_pairs={{0,2},{1,3},{4,0},{5,1},{8,4},{9,5},{12,8},{13,9},{14,12},{15,13},... | collective-permute-start | bytes 393224 | tf_op jit(solution)/shard_map/ppermute | solution.py:291
